TPU v7x, 512 devices: a whole 4x4x16 slice. The times are simulated.
512 devices in a mesh: ctx: 64 (over z, y), uly: 8 (over x, core).
Axes of the slice: x: 4, y: 4, z: 16, core: 2. Of those that a mesh axis runs over, the one named last changes fastest.
Arguments:
- queries: bfloat16 [65536, 3584], P(('ctx', 'uly')), may hold values from -10 to 10
- keys: bfloat16 [65536, 3584], P(('ctx', 'uly')), may hold values from -10 to 10
- values: bfloat16 [65536, 3584], P(('ctx', 'uly')), may hold values from -6 to 6
- step_raw: bfloat16 [65536, 56], P(('ctx', 'uly')), may hold values from -4 to 4
- step_bias: float32 [56], P('uly'), may hold values from -1.5 to 1
- decay_rate: float32 [56], P('uly'), may hold values from 0.0003 to 0.05
- skip_gain: float32 [56], P('uly'), may hold values from 0.1 to 1.9
- state_in: bfloat16 [65536, 64], P('ctx'), may hold values from -0.75 to 0.75
- state_out: bfloat16 [65536, 64], P('ctx'), may hold values from -0.75 to 0.75
- segment_ids: int32 [65536], replicated, may hold values from 0 to 127, never falling along the last dimension, each value on 1 to 2048 neighbouring positions
Outputs:
- mixed: bfloat16 [65536, 3584], P(('ctx', 'uly'))
Inputs may be any that keep to these rules, and one draw needn't show every extreme that they name: `segment_ids`: ids never fall along the sequence; every document holds at most 2048 tokens, and one holds exactly that many.
All inputs are finite; a program needn't handle non-finite values.
Results may differ from a plain program's by a relative error of at most 0.008.
Values may be sent and summed in bfloat16 or wider, within the bound.
No kernel may reach another device: no remote copies, remote signals or barrier semaphores. Data moves between devices by JAX's collectives and lax.ppermute only.
A program may use at most 128 MiB of HBM per device.

v0:
```python
import jax
import jax.numpy as jnp
from jax import lax
from jax.sharding import PartitionSpec as P

HEAD_DIM = 224
SSM_DIM = 64
STATE = 64
BLOCK = 256
REACH = 2


def from_behind(block, axis, distance):
    devices = range(lax.axis_size(axis))
    route = [(i - distance, i) for i in devices if i - distance in devices]
    return lax.ppermute(block, axis, route)


def carried_in(shard, axis, combine, identity):
    size, index = (lax.axis_size(axis), lax.axis_index(axis))
    everything = jax.tree.map(
        lambda part, kind: lax.all_gather(part.astype(kind), axis),
        shard,
        (jnp.bfloat16, jnp.bfloat16),
    )
    start = jax.tree.map(
        lambda part, zero: jnp.broadcast_to(jnp.asarray(zero, part.dtype), part.shape),
        shard,
        identity,
    )

    def lap(k, before):
        reached = k < index
        new = combine(
            before, jax.tree.map(lambda part, own: part[k].astype(own.dtype), everything, shard)
        )
        return jax.tree.map(lambda a, b: jnp.where(reached, a, b), new, before)

    return lax.fori_loop(0, size, lap, start)


def ssd_block(ssm_state, seg_before, x_half, dt_blk, decay_rate, b_blk, c_blk, seg_blk):
    log_step = -dt_blk * decay_rate[None, :]
    running_log = jnp.cumsum(log_step, axis=0)
    blk_len = seg_blk.shape[0]
    offsets = jnp.arange(blk_len, dtype=jnp.int32)
    lower_mask = (offsets[:, None] >= offsets[None, :]) & (seg_blk[:, None] == seg_blk[None, :])
    by_head = jnp.transpose(running_log)
    log_gap = by_head[:, :, None] - by_head[:, None, :]
    decay_mat = jnp.where(lower_mask[None], jnp.exp(jnp.where(lower_mask[None], log_gap, 0.0)), 0.0)
    mixing = jnp.dot(c_blk, jnp.transpose(b_blk), preferred_element_type=jnp.float32)
    weighted = (decay_mat * mixing[None] * jnp.transpose(dt_blk)[:, None, :]).astype(jnp.bfloat16)
    y_local = jnp.einsum("hts,shp->thp", weighted, x_half, preferred_element_type=jnp.float32)
    c_wide = c_blk.astype(jnp.float32)
    b_wide = b_blk.astype(jnp.float32)
    x_blk = x_half.astype(jnp.float32)
    enter_gain = jnp.exp(running_log) * (seg_blk == seg_before).astype(jnp.float32)[:, None]
    y_carried = (
        jnp.einsum("tn,hnp->thp", c_wide, ssm_state, precision=lax.Precision.HIGHEST)
        * enter_gain[:, :, None]
    )
    same_last = (seg_blk == seg_blk[-1]).astype(jnp.float32)[:, None]
    tail_gain = jnp.exp(running_log[-1][None, :] - running_log) * same_last * dt_blk
    keep_gain = jnp.exp(running_log[-1]) * (seg_blk[-1] == seg_before).astype(jnp.float32)
    new_state = jnp.einsum(
        "sh,sn,shp->hnp", tail_gain, b_wide, x_blk, precision=lax.Precision.HIGHEST
    )
    new_state = new_state + ssm_state * keep_gain[:, None, None]
    return (new_state, y_local + y_carried)


def tile_pass(carried, query_heads, own_ids, key_part, value_part, key_ids, causal):
    row_top, row_total, running = carried
    tok_rows = own_ids.shape[0]
    local_heads = query_heads.shape[1]
    key_heads = key_part.reshape(tok_rows, local_heads, HEAD_DIM)
    value_heads = value_part.reshape(tok_rows, local_heads, HEAD_DIM)
    scores = jnp.einsum("rhe,whe->hrw", query_heads, key_heads, preferred_element_type=jnp.float32)
    scores = scores / jnp.sqrt(jnp.float32(HEAD_DIM))
    allowed = own_ids[:, None] == key_ids[None, :]
    if causal:
        offsets = jnp.arange(tok_rows, dtype=jnp.int32)
        allowed = allowed & (offsets[None, :] <= offsets[:, None])
    scores = jnp.where(allowed[None], scores, -1e30)
    new_top = jnp.maximum(row_top, jnp.max(scores, axis=2))
    expo = jnp.exp(scores - new_top[:, :, None])
    fade = jnp.exp(row_top - new_top)
    row_total = row_total * fade + jnp.sum(expo, axis=2)
    update = jnp.einsum(
        "hrw,whe->rhe", expo.astype(jnp.bfloat16), value_heads, preferred_element_type=jnp.float32
    )
    running = running * jnp.transpose(fade)[:, :, None] + update
    return (new_top, row_total, running)


def shard_ids(segment_ids, ctx_index, distance, tok_rows):
    start = jnp.maximum((ctx_index - distance) * tok_rows, 0)
    taken = lax.dynamic_slice_in_dim(segment_ids, start, tok_rows, 0)
    return jnp.where(ctx_index >= distance, taken, -1)


def on_device(
    queries,
    keys,
    values,
    step_raw,
    step_bias,
    decay_rate,
    skip_gain,
    state_in,
    state_out,
    segment_ids,
):
    q_all, k_all, v_all, dt_raw = (
        lax.all_to_all(queries, "uly", split_axis=1, concat_axis=0, tiled=True),
        lax.all_to_all(keys, "uly", split_axis=1, concat_axis=0, tiled=True),
        lax.all_to_all(values, "uly", split_axis=1, concat_axis=0, tiled=True),
        lax.all_to_all(step_raw, "uly", split_axis=1, concat_axis=0, tiled=True),
    )
    tok_rows = q_all.shape[0]
    local_heads = q_all.shape[1] // HEAD_DIM
    ssm_local = q_all.shape[1] // SSM_DIM
    ctx_index = lax.axis_index("ctx")
    own_ids = shard_ids(segment_ids, ctx_index, 0, tok_rows)
    prev_ids = shard_ids(segment_ids, ctx_index, 1, tok_rows)
    prev_last = prev_ids[-1]
    query_heads = q_all.reshape(tok_rows, local_heads, HEAD_DIM)
    start_carry = (
        jnp.full((local_heads, tok_rows), -1e30, jnp.float32),
        jnp.zeros((local_heads, tok_rows), jnp.float32),
        jnp.zeros((tok_rows, local_heads, HEAD_DIM), jnp.float32),
    )
    carried = tile_pass(start_carry, query_heads, own_ids, k_all, v_all, own_ids, True)
    moving = (k_all, v_all)
    for distance in range(1, REACH + 1):
        moving = from_behind((moving[0], moving[1]), "ctx", 1)
        key_ids = shard_ids(segment_ids, ctx_index, distance, tok_rows)
        key_part, value_part = moving
        carried = tile_pass(carried, query_heads, own_ids, key_part, value_part, key_ids, False)
    row_top, row_total, running = carried
    attended = (running / jnp.transpose(row_total)[:, :, None]).astype(jnp.bfloat16)
    x_half = attended.reshape(tok_rows, ssm_local, SSM_DIM)
    dt_all = jax.nn.softplus(dt_raw.astype(jnp.float32) + step_bias[None, :])
    blk_len = min(BLOCK, tok_rows)
    count = tok_rows // blk_len
    inputs = (
        x_half.reshape(count, blk_len, ssm_local, SSM_DIM),
        dt_all.reshape(count, blk_len, ssm_local),
        state_in.reshape(count, blk_len, STATE),
        state_out.reshape(count, blk_len, STATE),
        own_ids.reshape(count, blk_len),
    )

    def advance(pair, pieces):
        ssm_state, seg_before = pair
        x_blk, dt_blk, b_blk, c_blk, seg_blk = pieces
        new_state, y_blk = ssd_block(
            ssm_state, seg_before, x_blk, dt_blk, decay_rate, b_blk, c_blk, seg_blk
        )
        return ((new_state, seg_blk[-1]), y_blk)

    zero_state = jnp.zeros((ssm_local, STATE, SSM_DIM), jnp.float32)
    final_pair, outputs = lax.scan(advance, (zero_state, prev_last), inputs)
    end_state = final_pair[0]
    y_local = outputs.reshape(tok_rows, ssm_local, SSM_DIM)
    shard_log = jnp.cumsum(-dt_all * decay_rate[None, :], axis=0)
    linked = (own_ids[-1] == prev_last).astype(jnp.float32)
    shard_decay = jnp.exp(shard_log[-1]) * linked

    def link(earlier, later):
        return (earlier[0] * later[0], earlier[1] * later[0][:, None, None] + later[1])

    identity = (jnp.ones((ssm_local,), jnp.float32), zero_state)
    passed_decay, incoming = carried_in((shard_decay, end_state), "ctx", link, identity)
    enter_gain = jnp.exp(shard_log) * (own_ids == prev_last).astype(jnp.float32)[:, None]
    c_wide = state_out.astype(jnp.float32)
    y_carried = (
        jnp.einsum("tn,hnp->thp", c_wide, incoming, precision=lax.Precision.HIGHEST)
        * enter_gain[:, :, None]
    )
    mixed = y_local + y_carried + skip_gain[None, :, None] * x_half
    mixed = mixed.reshape(tok_rows, ssm_local * SSM_DIM).astype(jnp.bfloat16)
    return lax.all_to_all(mixed, "uly", split_axis=0, concat_axis=1, tiled=True)


def solution(mesh):
    return jax.shard_map(
        on_device,
        mesh=mesh,
        in_specs=(
            P(("ctx", "uly"), None),
            P(("ctx", "uly"), None),
            P(("ctx", "uly"), None),
            P(("ctx", "uly"), None),
            P("uly"),
            P("uly"),
            P("uly"),
            P("ctx", None),
            P("ctx", None),
            P(),
        ),
        out_specs=P(("ctx", "uly"), None),
        check_vma=False,
    )
```

profile of v0, /device:TPU:1, one launch (start us, length us, event | category | flops | bytes accessed | tf_op | source)
XLA Modules:
  0.0 466.7 jit_solution(57355750852946910)
XLA Ops:
  6.5 1.3 all_to_all.62
  7.9 10.1 %all-to-all-start = ((bf16[128,8,7]{0,2,1:T(8,128)(2,1)}), bf16[128,8,7]{0,2,1:T(8,128)(2,1)S(1)}, u32[]{:S(2)}, u32[]{:S(2)}) async-start(bf16[128,8,7]{0,2,1:T(8,128)(2,1)} %all_to_all.62), calls=%async_computation | async-start | bytes 32768 | tf_op jit(solution)/shard_map/all_to_all | solution.py:118
  18.0 2.2 copy.156
  20.2 2.5 all-to-all-done
  22.7 4.2 all-to-all-start.2
  28.3 2.2 copy.154
  30.5 2.2 copy.158
  32.7 1.9 compare_convert_fusion.2
  34.6 5.9 %all-to-all-done.2 = bf16[128,8,448]{0,2,1:T(8,128)(2,1)S(1)} async-done(((bf16[128,8,448]{0,2,1:T(8,128)(2,1)}), bf16[128,8,448]{0,2,1:T(8,128)(2,1)S(1)}, u32[]{:S(2)}, u32[]{:S(2)}) %all-to-all-start.2) | async-done | bytes 917536 | tf_op jit(solution)/shard_map/all_to_all | solution.py:116
  40.5 4.3 all-to-all-start.3
  44.9 3.3 fusion.59
  48.1 1.1 copy_bitcast_fusion.4
  49.2 2.2 collective-permute-start
  51.4 7.2 %all-to-all-done.3 = bf16[128,8,448]{0,2,1:T(8,128)(2,1)S(1)} async-done(((bf16[128,8,448]{0,2,1:T(8,128)(2,1)}), bf16[128,8,448]{0,2,1:T(8,128)(2,1)S(1)}, u32[]{:S(2)}, u32[]{:S(2)}) %all-to-all-start.3) | async-done | bytes 917536 | tf_op jit(solution)/shard_map/all_to_all | solution.py:117
  58.6 5.0 %all-to-all-start.1 = ((bf16[128,8,448]{0,2,1:T(8,128)(2,1)}), bf16[128,8,448]{0,2,1:T(8,128)(2,1)}, u32[]{:S(2)}, u32[]{:S(2)}) async-start(bf16[128,8,448]{0,2,1:T(8,128)(2,1)} %bitcast.309), calls=%async_computation.1 | async-start | bytes 1835008 | tf_op jit(solution)/shard_map/all_to_all | solution.py:115
  64.2 1.1 copy_bitcast_fusion.3
  65.3 2.2 collective-permute-start.1
  69.6 7.8 %all-to-all-done.1 = bf16[128,8,448]{0,2,1:T(8,128)(2,1)} async-done(((bf16[128,8,448]{0,2,1:T(8,128)(2,1)}), bf16[128,8,448]{0,2,1:T(8,128)(2,1)}, u32[]{:S(2)}, u32[]{:S(2)}) %all-to-all-start.1) | async-done | bytes 917536 | tf_op jit(solution)/shard_map/all_to_all | solution.py:115
  77.4 2.7 copy.155
  80.1 2.3 reshape.304
  82.4 1.5 copy.157
  83.9 2.3 reshape.305
  86.8 1.3 reshape.306
  88.1 1.3 collective-permute-start.2
  89.5 3.9 fusion.35
  93.4 2.2 collective-permute-start.3
  95.7 3.2 fusion.36
  98.9 10.6 %collective-permute-done.2 = bf16[1024,448]{0,1:T(8,128)(2,1)S(1)} collective-permute-done((bf16[1024,448]{0,1:T(8,128)(2,1)}, bf16[1024,448]{0,1:T(8,128)(2,1)S(1)}, u32[]{:S(2)}, u32[]{:S(2)}) %collective-permute-start.2) | collective-permute-done | bytes 917536 | tf_op jit(solution)/shard_map/ppermute | solution.py:16
  109.5 2.0 fusion.37
  112.2 4.0 fusion.48
  116.2 5.4 %fusion.38 = (f32[2,1024]{1,0:T(2,128)}, f32[2,1024]{1,0:T(2,128)}) fusion(f32[2,1024,1024]{1,2,0:T(8,128)S(1)} %get-tuple-element.346, f32[2,1024]{1,0:T(2,128)} %copy-done.14, pred[1024,1024]{0,1:T(8,128)(4,1)S(1)} %copy-done.1, f32[2,1024]{1,0:T(2,128)} %get-tuple-element.326, f32[2,1024,1024]{1,2,0:T(8,128)S(1)} %get-tuple-element.344, ...), kind=kLoop, calls=%fused_computation.63 | loop fusion | flops 16773120 | bytes 18907136 | tf_op jit(solution)/shard_map/reduce_sum | solution.py:88
  121.6 2.8 fusion.42
  124.5 4.0 fusion.46
  129.2 4.2 fusion.67
  134.4 77.2 %while.29 = (s32[]{:T(128)}, f32[7,64,64]{2,1,0:T(8,128)S(1)}, s32[]{:T(128)}, f32[4,256,7,64]{1,0,3,2:T(4,128)}, bf16[4,256,64]{1,2,0:T(8,128)(2,1)S(1)}, /*ind...) while((s32[]{:T(128)}, f32[7,64,64]{2,1,0:T(8,128)S(1)}, ...), condition=%wide.region_9.10_spmd.clone, body=%wide.region_6.9_spmd.clone.sunk | while | flops 246906400 | bytes 5800473 | solution.py:163
  135.2 2.1 reduce-window.26
  141.2 10.9 %dynamic_update_slice.6 = f32[4,256,7,64]{1,0,3,2:T(4,128)} dynamic-update-slice(f32[4,256,7,64]{1,0,3,2:T(4,128)} %get-tuple-element.470, f32[1,256,7,64]{1,0,3,2:T(1,128)S(1)} %copy.242, s32[]{:T(128)} %get-tuple-element.467, s32[]{:T(128)} %constant.75.clone.1..sunk, s32[]{:T(128)} %constant.75.clone.1..sunk, s32[]{:T(128)} %constant.75.clone.1..sunk) | dynamic-update-slice | bytes 917508 | tf_op jit(solution)/shard_map/while/body/jit(dynamic_update_index_in_dim)/dynamic_update_slice | solution.py:163
  154.5 2.1 reduce-window.26
  160.5 10.9 %dynamic_update_slice.6 = f32[4,256,7,64]{1,0,3,2:T(4,128)} dynamic-update-slice(f32[4,256,7,64]{1,0,3,2:T(4,128)} %get-tuple-element.470, f32[1,256,7,64]{1,0,3,2:T(1,128)S(1)} %copy.242, s32[]{:T(128)} %get-tuple-element.467, s32[]{:T(128)} %constant.75.clone.1..sunk, s32[]{:T(128)} %constant.75.clone.1..sunk, s32[]{:T(128)} %constant.75.clone.1..sunk) | dynamic-update-slice | bytes 917508 | tf_op jit(solution)/shard_map/while/body/jit(dynamic_update_index_in_dim)/dynamic_update_slice | solution.py:163
  173.8 2.1 reduce-window.26
  179.8 10.9 %dynamic_update_slice.6 = f32[4,256,7,64]{1,0,3,2:T(4,128)} dynamic-update-slice(f32[4,256,7,64]{1,0,3,2:T(4,128)} %get-tuple-element.470, f32[1,256,7,64]{1,0,3,2:T(1,128)S(1)} %copy.242, s32[]{:T(128)} %get-tuple-element.467, s32[]{:T(128)} %constant.75.clone.1..sunk, s32[]{:T(128)} %constant.75.clone.1..sunk, s32[]{:T(128)} %constant.75.clone.1..sunk) | dynamic-update-slice | bytes 917508 | tf_op jit(solution)/shard_map/while/body/jit(dynamic_update_index_in_dim)/dynamic_update_slice | solution.py:163
  193.1 2.1 reduce-window.26
  199.1 10.9 %dynamic_update_slice.6 = f32[4,256,7,64]{1,0,3,2:T(4,128)} dynamic-update-slice(f32[4,256,7,64]{1,0,3,2:T(4,128)} %get-tuple-element.470, f32[1,256,7,64]{1,0,3,2:T(1,128)S(1)} %copy.242, s32[]{:T(128)} %get-tuple-element.467, s32[]{:T(128)} %constant.75.clone.1..sunk, s32[]{:T(128)} %constant.75.clone.1..sunk, s32[]{:T(128)} %constant.75.clone.1..sunk) | dynamic-update-slice | bytes 917508 | tf_op jit(solution)/shard_map/while/body/jit(dynamic_update_index_in_dim)/dynamic_update_slice | solution.py:163
  214.2 2.0 reduce-window.16
  216.8 68.9 %all-gather.1 = bf16[64,1,7]{2,1,0:T(2,128)(2,1)S(1)} all-gather(bf16[1,1,7]{2,1,0:T(2,128)(2,1)S(1)} %bitcast.327), channel_id=1, replica_groups=mesh['ctx'=64,'uly'=8] {'ctx'}, dimensions={0}, use_global_device_ids=true | all-gather | bytes 910 | tf_op jit(solution)/shard_map/all_gather | solution.py:22
  285.7 2.5 reshape.312
  288.2 74.7 %all-gather.4.cloned.1.call-done = bf16[448,64,64]{2,1,0:T(8,128)(2,1)} async-done(((bf16[7,64,64]{2,1,0:T(8,128)(2,1)}), bf16[448,64,64]{2,1,0:T(8,128)(2,1)}) %all-gather.4.cloned.1.call-update) | async-done | bytes 3670032 | tf_op jit(solution)/shard_map/all_gather | solution.py:22
  363.0 66.8 %while.30 = (s32[]{:T(128)}, f32[7,64,64]{2,1,0:T(8,128)S(1)}, s32[]{:T(128)}, bf16[64,7]{1,0:T(8,128)(2,1)S(1)}, bf16[64,7,64,64]{3,2,1,0:T(8,128)(2,1)}, /*index=5*/s32[]{:T(128)}, s32[]{:T(128)}) while((s32[]{:T(128)}, f32[7,64,64]{2,1,0:T(8,128)S(1)}, s32[]{:T(128)}, bf16[64,7]{1,0:T(8,128)(2,1)S(1)}, ...), condition=%wide.region_13.14_spmd.clone, body=%wide.region_12.13_spmd.clone.sunk | while | flops 143371 | bytes 286895 | solution.py:39
  367.1 1.0 fusion.141
  372.4 1.0 fusion.141
  376.5 1.0 fusion.141
  377.6 1.0 fusion.141
  381.8 1.0 fusion.141
  387.0 1.0 fusion.141
  392.2 1.0 fusion.141
  396.4 1.0 fusion.141
  397.4 1.0 fusion.141
  401.6 1.0 fusion.141
  406.8 1.0 fusion.141
  412.0 1.0 fusion.141
  416.2 1.0 fusion.141
  417.2 1.0 fusion.141
  431.7 26.9 %all_to_all.83 = bf16[8,128,448]{1,2,0:T(8,128)(2,1)S(1)} all-to-all(bf16[8,128,448]{1,2,0:T(8,128)(2,1)S(1)} %copy.173), channel_id=1, replica_groups=mesh['ctx'=64,'uly'=8] {'uly'}, dimensions={0} | all-to-all | bytes 1835008 | tf_op jit(solution)/shard_map/all_to_all | solution.py:183
  458.6 1.3 copy.174
  (308 shorter events, 81.3 us)
Async XLA Ops:
  7.9 14.8 %all-to-all-start = ((bf16[128,8,7]{0,2,1:T(8,128)(2,1)}), bf16[128,8,7]{0,2,1:T(8,128)(2,1)S(1)}, u32[]{:S(2)}, u32[]{:S(2)}) async-start(bf16[128,8,7]{0,2,1:T(8,128)(2,1)} %all_to_all.62), calls=%async_computation | async-start | bytes 32768 | tf_op jit(solution)/shard_map/all_to_all | solution.py:118
  20.2 43.4 %copy-start.6 = (bf16[1024,64]{0,1:T(8,128)(2,1)S(1)}, bf16[1024,64]{0,1:T(8,128)(2,1)}, u32[]{:S(2)}) copy-start(bf16[1024,64]{0,1:T(8,128)(2,1)} %param.22) | copy-start | bytes 393220
  20.2 43.4 %copy-start.9 = (bf16[1024,64]{0,1:T(8,128)(2,1)S(1)}, bf16[1024,64]{0,1:T(8,128)(2,1)}, u32[]{:S(2)}) copy-start(bf16[1024,64]{0,1:T(8,128)(2,1)} %param.21) | copy-start | bytes 393220
  22.7 44.8 %copy-start.7 = (bf16[128,8,7]{0,2,1:T(8,128)(2,1)}, bf16[128,8,7]{0,2,1:T(8,128)(2,1)S(1)}, u32[]{:S(2)}) copy-start(bf16[128,8,7]{0,2,1:T(8,128)(2,1)S(1)} %all-to-all-done) | copy-start | bytes 43012
  22.7 17.9 %all-to-all-start.2 = ((bf16[128,8,448]{0,2,1:T(8,128)(2,1)}), bf16[128,8,448]{0,2,1:T(8,128)(2,1)S(1)}, u32[]{:S(2)}, u32[]{:S(2)}) async-start(bf16[128,8,448]{0,2,1:T(8,128)(2,1)} %bitcast.4), calls=%async_computation.2 | async-start | bytes 1835008 | tf_op jit(solution)/shard_map/all_to_all | solution.py:116
  28.3 40.6 %copy-start.23 = (f32[7]{0:T(128)S(1)}, f32[7]{0:T(128)}, u32[]{:S(2)}) copy-start(f32[7]{0:T(128)} %param.18) | copy-start | bytes 88
  40.5 18.0 %all-to-all-start.3 = ((bf16[128,8,448]{0,2,1:T(8,128)(2,1)}), bf16[128,8,448]{0,2,1:T(8,128)(2,1)S(1)}, u32[]{:S(2)}, u32[]{:S(2)}) async-start(bf16[128,8,448]{0,2,1:T(8,128)(2,1)} %bitcast.7), calls=%async_computation.3 | async-start | bytes 1835008 | tf_op jit(solution)/shard_map/all_to_all | solution.py:117
  49.2 38.9 %collective-permute-start = (bf16[1024,448]{0,1:T(8,128)(2,1)}, bf16[1024,448]{0,1:T(8,128)(2,1)}, u32[]{:S(2)}, u32[]{:S(2)}) collective-permute-start(bf16[1024,448]{0,1:T(8,128)(2,1)} %copy_bitcast_fusion.4), channel_id=1, source_target_pairs={{0,8},{8,16},{16,24},{24,32},{32,40},{40,48},{48,56},{56,64},{64,7... | collective-permute-start | bytes 2752520 | tf_op jit(solution)/shard_map/ppermute | solution.py:16
  58.6 18.8 %all-to-all-start.1 = ((bf16[128,8,448]{0,2,1:T(8,128)(2,1)}), bf16[128,8,448]{0,2,1:T(8,128)(2,1)}, u32[]{:S(2)}, u32[]{:S(2)}) async-start(bf16[128,8,448]{0,2,1:T(8,128)(2,1)} %bitcast.309), calls=%async_computation.1 | async-start | bytes 1835008 | tf_op jit(solution)/shard_map/all_to_all | solution.py:115
  63.6 299.4 %all-gather.4.cloned.1.call-start = ((), (), s32[]{:S(2)}) async-start(), calls=%async_computation.5 | async-start | bytes 7454720 | tf_op jit(solution)/shard_map/all_gather | solution.py:22
  65.3 28.2 %collective-permute-start.1 = (bf16[1024,448]{0,1:T(8,128)(2,1)}, bf16[1024,448]{0,1:T(8,128)(2,1)}, u32[]{:S(2)}, u32[]{:S(2)}) collective-permute-start(bf16[1024,448]{0,1:T(8,128)(2,1)} %copy_bitcast_fusion.3), channel_id=1, source_target_pairs={{0,8},{8,16},{16,24},{24,32},{32,40},{40,48},{48,56},{56,64},{64,7... | collective-permute-start | bytes 2752520 | tf_op jit(solution)/shard_map/ppermute | solution.py:16
  88.1 21.4 %collective-permute-start.2 = (bf16[1024,448]{0,1:T(8,128)(2,1)}, bf16[1024,448]{0,1:T(8,128)(2,1)S(1)}, u32[]{:S(2)}, u32[]{:S(2)}) collective-permute-start(bf16[1024,448]{0,1:T(8,128)(2,1)} %collective-permute-done), channel_id=1, source_target_pairs={{0,8},{8,16},{16,24},{24,32},{32,40},{40,48},{48,56},{56,64},{64,7... | collective-permute-start | bytes 2752520 | tf_op jit(solution)/shard_map/ppermute | solution.py:16
  89.5 6.2 %copy-start = (pred[1024,1024]{0,1:T(8,128)(4,1)S(1)}, pred[1024,1024]{0,1:T(8,128)(4,1)}, u32[]{:S(2)}) copy-start(pred[1024,1024]{0,1:T(8,128)(4,1)} %get-tuple-element.340) | copy-start | bytes 3145732
  89.5 6.2 %copy-start.4 = (bf16[1024,2,224]{0,2,1:T(8,128)(2,1)S(1)}, bf16[1024,2,224]{0,2,1:T(8,128)(2,1)}, u32[]{:S(2)}) copy-start(bf16[1024,2,224]{0,2,1:T(8,128)(2,1)} %reshape.304) | copy-start | bytes 2752516
  93.4 18.1 %copy-start.15 = (f32[2,1024]{1,0:T(2,128)}, f32[2,1024]{1,0:T(2,128)S(1)}, u32[]{:S(2)}) copy-start(f32[2,1024]{1,0:T(2,128)S(1)} %get-tuple-element.345) | copy-start | bytes 24580
  93.4 35.8 %collective-permute-start.3 = (bf16[1024,448]{0,1:T(8,128)(2,1)}, bf16[1024,448]{0,1:T(8,128)(2,1)}, u32[]{:S(2)}, u32[]{:S(2)}) collective-permute-start(bf16[1024,448]{0,1:T(8,128)(2,1)} %collective-permute-done.1), channel_id=1, source_target_pairs={{0,8},{8,16},{16,24},{24,32},{32,40},{40,48},{48,56},{56,64},{64,7... | collective-permute-start | bytes 2752520 | tf_op jit(solution)/shard_map/ppermute | solution.py:16
  98.9 12.7 %copy-start.17 = (f32[2,1024]{1,0:T(2,128)}, f32[2,1024]{1,0:T(2,128)S(1)}, u32[]{:S(2)}) copy-start(f32[2,1024]{1,0:T(2,128)S(1)} %get-tuple-element.343) | copy-start | bytes 24580
  109.5 2.7 copy-start.1
  109.5 2.7 copy-start.5
  111.5 0.6 copy-start.19
  112.2 4.0 copy-start.14
  121.6 2.8 copy-start.10
  121.6 2.8 copy-start.11
  121.6 2.8 copy-start.16
  121.6 2.8 copy-start.18
  121.6 2.8 copy-start.20
  121.6 2.9 copy-start.13
  124.5 4.7 %copy-start.12 = (f32[2,1024]{1,0:T(2,128)S(1)}, f32[2,1024]{1,0:T(2,128)}, u32[]{:S(2)}) copy-start(f32[2,1024]{1,0:T(2,128)} %get-tuple-element.325) | copy-start | bytes 24580
  124.5 4.7 %copy-start.26 = (f32[2,1024,224]{1,2,0:T(8,128)S(1)}, f32[2,1024,224]{1,2,0:T(8,128)}, u32[]{:S(2)}) copy-start(f32[2,1024,224]{1,2,0:T(8,128)} %fusion.48) | copy-start | bytes 5505028
  129.2 5.1 %copy-start.21 = (f32[7]{0:T(128)S(1)}, f32[7]{0:T(128)}, u32[]{:S(2)}) copy-start(f32[7]{0:T(128)} %param.19) | copy-start | bytes 88
  133.4 0.9 copy-start.2
  134.3 79.8 %copy-start.8 = (bf16[128,8,7]{0,2,1:T(8,128)(2,1)S(1)}, bf16[128,8,7]{0,2,1:T(8,128)(2,1)}, u32[]{:S(2)}) copy-start(bf16[128,8,7]{0,2,1:T(8,128)(2,1)} %copy-done.7) | copy-start | bytes 43012
  134.3 79.8 %copy-start.24 = (f32[7]{0:T(128)S(1)}, f32[7]{0:T(128)}, u32[]{:S(2)}) copy-start(f32[7]{0:T(128)} %param.18) | copy-start | bytes 88
  134.3 151.4 %copy-start.22 = (f32[1024]{0:T(1024)S(1)}, f32[1024]{0:T(1024)}, u32[]{:S(2)}) copy-start(f32[1024]{0:T(1024)} %get-tuple-element.321) | copy-start | bytes 12292
  211.6 219.1 %copy-start.3 = (bf16[1024,2,224]{0,2,1:T(8,128)(2,1)S(1)}, bf16[1024,2,224]{0,2,1:T(8,128)(2,1)}, u32[]{:S(2)}) copy-start(bf16[1024,2,224]{0,2,1:T(8,128)(2,1)} %copy-done.2) | copy-start | bytes 2752516
  211.6 219.1 %copy-start.25 = (f32[7]{0:T(128)S(1)}, f32[7]{0:T(128)}, u32[]{:S(2)}) copy-start(f32[7]{0:T(128)} %param.20) | copy-start | bytes 88
Sparse Core Ops, SparseCore 0:
  212.4 150.5 all-gather.3
where the time goes:
time: 471 us; the launch traced here: 467 us
  waiting for transfers between devices  109 us (23%)
  other arithmetic  96.5 us (20%)
  blocking collectives  95.8 us (20%)
  local copies, waits for them, and re-layouts  82.1 us (17%)
  starting transfers between devices  31.6 us (7%)
  matrix products  28.9 us (6%)
  between operations  15.6 us (3%)
  loops' own time  6.88 us (1%)
    all_gather x1, waiting for transfers between devices, carried_in(): lax.all_gather(part.astype(kind), axis)  74.7 us
    all_gather x1, blocking collectives, carried_in(): lax.all_gather(part.astype(kind), axis)  68.9 us
    select_n x64, other arithmetic, lap(): return jax.tree.map(lambda a, b: jnp.where(reached, a, b), new, before)  64.1 us
    dynamic_update_slice x8, local copies, waits for them, and re-layouts, on_device(): final_pair, outputs = lax.scan(advance, (zero_state, prev_last), inputs)  45.5 us
    all_to_all x1, blocking collectives, on_device(): return lax.all_to_all(mixed, 'uly', split_axis=0, concat_axis=1, tiled=True)  26.9 us
    dot_general x3, matrix products, tile_pass(): jnp.einsum('hrw,whe->rhe', expo.astype(jnp.bfloat16), value_heads, prefer...  12.3 us
    ppermute x4, waiting for transfers between devices, from_behind(): return lax.ppermute(block, axis, route)  11.3 us
    another operation x14, other arithmetic  10.8 us
  transfers between devices with their start and end apart: 9, of which 7 were waited for; matrix products, arithmetic and copies ran while one was open for 13% of the time, Pallas kernels for 0%

commit v1 on v0

v1 whole, which is shorter than its diff:
```python
import functools
import math

import jax
import jax.numpy as jnp
from jax import lax
from jax.experimental import pallas as pl
from jax.experimental.pallas import tpu as pltpu
from jax.sharding import Mesh
from jax.sharding import PartitionSpec as P

HEADS = 16
HEAD_DIM = 224
SSM_DIM = 64
STATE = 64
ROWS = 128
PLANE = 4096
REACH = 2048
CHUNKS = 16
SSM = 4
WIDE = SSM * SSM_DIM
PACK = 464
LOG2E = math.log2(math.e)
NT = (((1,), (1,)), ((), ()))
VMEM_LIMIT = 56 * 1024 * 1024

f32, bf16, i32 = jnp.float32, jnp.bfloat16, jnp.int32


def iota(shape, dim):
    return lax.broadcasted_iota(i32, shape, dim)


def spread(rows, count=WIDE):
    width = rows.shape[-1]
    return jnp.concatenate(
        [jnp.broadcast_to(rows[r : r + 1, :], (SSM_DIM, width)) for r in range(SSM)], axis=0
    )


def pack_kernel(k_ref, v_ref, raw_ref, par_ref, out_ref):
    step = pl.program_id(0)
    kt = jnp.transpose(k_ref[...])
    vt = jnp.transpose(v_ref[...])
    rr, jj = iota((64, 56), 0), iota((64, 56), 1)
    head, r = 4 * step + (rr >> 4), rr & 15
    chosen = ((r < SSM) & (jj == ((7 * head) >> 1) + r)).astype(bf16)
    rows = lax.dot_general(chosen, raw_ref[...], NT, preferred_element_type=f32)
    whole = par_ref[...]
    high = whole.astype(bf16).astype(f32)
    mid = (whole - high).astype(bf16).astype(f32)
    low = whole - high - mid
    r = iota((64, ROWS), 0) & 15
    rows = jnp.where(r == 4, high, jnp.where(r == 5, mid, jnp.where(r == 6, low, rows))).astype(bf16)
    for h in range(4):
        out_ref[h, 0:224, :] = kt[224 * h : 224 * h + 224, :]
        out_ref[h, 224:448, :] = vt[224 * h : 224 * h + 224, :]
        out_ref[h, 448:464, :] = rows[16 * h : 16 * h + 16, :]


def pack(keys, values, step_raw, params):
    return pl.pallas_call(
        pack_kernel,
        grid=(4,),
        in_specs=[
            pl.BlockSpec((ROWS, 896), lambda i: (0, i)),
            pl.BlockSpec((ROWS, 896), lambda i: (0, i)),
            pl.BlockSpec((ROWS, 56), lambda i: (0, 0)),
            pl.BlockSpec((1, ROWS), lambda i: (0, 0)),
        ],
        out_specs=pl.BlockSpec((4, PACK, ROWS), lambda i: (i, 0, 0)),
        out_shape=jax.ShapeDtypeStruct((HEADS, PACK, ROWS), bf16),
        compiler_params=pltpu.CompilerParams(vmem_limit_bytes=VMEM_LIMIT),
        name="pack_keys_values",
    )(keys, values, step_raw, params)


def turn_kernel(own_ref, other_ref, out_ref):
    out_ref[0, 0:128, :] = jnp.transpose(own_ref[0])
    out_ref[0, 128:256, :] = jnp.transpose(other_ref[0])


def turn(own, other):
    count = own.shape[0]
    block = pl.BlockSpec((1, HEAD_DIM, ROWS), lambda i: (i, 0, 0))
    return pl.pallas_call(
        turn_kernel,
        grid=(count,),
        in_specs=[block, block],
        out_specs=pl.BlockSpec((1, 256, HEAD_DIM), lambda i: (i, 0, 0)),
        out_shape=jax.ShapeDtypeStruct((count, 256, HEAD_DIM), bf16),
        compiler_params=pltpu.CompilerParams(vmem_limit_bytes=VMEM_LIMIT),
        cost_estimate=pl.CostEstimate(flops=0, bytes_accessed=count * 256 * 256 * 4, transcendentals=0),
        name="turn_keys",
    )(own, other)


def prep_kernel(core_ref, par_ref, own_ref, other_ref, ds_ref, dso_ref, bc_ref, inner_ref, rows_ref, keep_ref):
    core = core_ref[0]
    shape = (CHUNKS * 16, ROWS)
    line, lane = iota(shape, 0), iota(shape, 1)
    r = line & 15
    bias, decay = jnp.zeros(shape, f32), jnp.zeros(shape, f32)
    for n in range(SSM):
        bias = jnp.where(r == n, par_ref[0, n], bias)
        decay = jnp.where(r == n, par_ref[1, n], decay)
    upper = (iota((ROWS, ROWS), 0) <= iota((ROWS, ROWS), 1)).astype(f32)

    def steps(ref, ids, which):
        raw = ref[...].reshape(shape).astype(f32)
        z = raw + bias
        dt = jnp.maximum(z, 0.0) + jnp.log1p(jnp.exp(-jnp.abs(z)))
        running = jnp.dot(-dt * decay, upper, precision=lax.Precision.HIGHEST, preferred_element_type=f32)
        start = 256 * (line >> 4) + 128 * which
        whole = jnp.broadcast_to(running[:, 127:128], shape)
        last = jnp.broadcast_to(ids[:, 127:128], shape)
        keep = jnp.where(last < start, jnp.exp(whole), 0.0)
        return dt, running, start, whole, last, keep

    ids = ds_ref[...].reshape(shape)
    dt, running, start, whole, last, keep = steps(own_ref, ids, core)
    tail = jnp.where(start + lane >= last, jnp.exp(whole - running) * dt, 0.0)
    enter = jnp.where(ids < start, jnp.exp(running), 0.0)
    keep_other = steps(other_ref, dso_ref[...].reshape(shape), 1 - core)[5]
    for b in range(CHUNKS):
        at = 16 * b
        rows_ref[b, 0:4, :] = tail[at : at + 4, :]
        rows_ref[b, 4:8, :] = enter[at : at + 4, :]
        keep_ref[b, 0:4, :] = jnp.where(core == 0, keep[at : at + 4, :], keep_other[at : at + 4, :])
        keep_ref[b, 4:8, :] = jnp.where(core == 0, keep_other[at : at + 4, :], keep[at : at + 4, :])
    running_t, dt_t = jnp.transpose(running), jnp.transpose(dt)
    s_at, t_at = iota((ROWS, ROWS), 0), iota((ROWS, ROWS), 1)
    for b in range(CHUNKS):
        at = 16 * b
        mix = lax.dot_general(
            bc_ref[b, :, 0:64], bc_ref[b, :, 64:128], NT, preferred_element_type=f32
        )
        base = 256 * b + 128 * core
        allowed = (s_at <= t_at) & (s_at >= ids[at : at + 1, :] - base)
        for n in range(SSM):
            gap = running[at + n : at + n + 1, :] - running_t[:, at + n : at + n + 1]
            value = jnp.exp(jnp.where(allowed, gap, 0.0)) * mix * dt_t[:, at + n : at + n + 1]
            inner_ref[b, n, :, :] = jnp.where(allowed, value, 0.0).astype(bf16)


def prep(core, params, own_steps, other_steps, ids, ids_other, bc):
    return pl.pallas_call(
        prep_kernel,
        in_specs=[pl.BlockSpec(memory_space=pltpu.SMEM)] * 2
        + [pl.BlockSpec(memory_space=pltpu.VMEM)] * 5,
        out_shape=(
            jax.ShapeDtypeStruct((CHUNKS, SSM, ROWS, ROWS), bf16),
            jax.ShapeDtypeStruct((CHUNKS, 8, ROWS), f32),
            jax.ShapeDtypeStruct((CHUNKS, 8, ROWS), f32),
        ),
        compiler_params=pltpu.CompilerParams(vmem_limit_bytes=VMEM_LIMIT),
        cost_estimate=pl.CostEstimate(flops=200_000_000, bytes_accessed=8_000_000, transcendentals=2_000_000),
        name="scan_weights",
    )(core, params, own_steps, other_steps, ids, ids_other, bc)


def attend_kernel(
    core_ref, low_ref, q_ref, kn_ref, knh_ref, own_ref, other_ref, hown_ref, hother_ref, ds_ref, rows_ref, bc_ref,
    keep_ref, x_ref, s_ref, send_ref, f_ref,
):
    core, off = core_ref[0], pl.multiple_of(core_ref[1], 32)
    scale = LOG2E / math.sqrt(HEAD_DIM)
    x_ref[...] = jnp.zeros_like(x_ref)
    line = iota((ROWS, 256), 0)
    lane = iota((1, 256), 1)

    def tile(i, carry):
        q = jnp.concatenate([q_ref[2 * i], q_ref[2 * i + 1]], axis=1)
        ids = jnp.concatenate([ds_ref[2 * i], ds_ref[2 * i + 1]], axis=1)
        q_at = 512 * i + 128 * core + (lane & 127) + 256 * (lane >> 7)

        def part(state, k_pair, v_parts, start, causal):
            top, total, acc = state
            pieces = []
            for j in range(4):
                at = start + 256 * (j // 2) + 128 * (core if j % 2 == 0 else 1 - core)
                k = k_pair[j // 2][128 * (j % 2) : 128 * (j % 2) + 128, :]
                score = jnp.dot(k, q, preferred_element_type=f32) * scale
                allowed = line >= ids - at
                if causal:
                    allowed = allowed & (line <= q_at - at)
                pieces.append(jnp.where(allowed, score, -1e30))
            score = jnp.concatenate(pieces, axis=0)
            new_top = jnp.maximum(top, jnp.max(score, axis=0, keepdims=True))
            expo = jnp.exp2(score - new_top)
            fade = jnp.exp2(top - new_top)
            total = total * fade + jnp.sum(expo, axis=0, keepdims=True)
            v = jnp.concatenate(v_parts, axis=1)
            acc = acc * fade + jnp.dot(v, expo.astype(bf16), preferred_element_type=f32)
            return new_top, total, acc

        def own(p, state, causal=False):
            k = (kn_ref[2 * p], kn_ref[2 * p + 1])
            v = [ref[2 * p + j, 224:448, :] for j in range(2) for ref in (own_ref, other_ref)]
            return part(state, k, v, 512 * p, causal)

        def halo(p, state):
            k = (knh_ref[2 * p], knh_ref[2 * p + 1])
            v = [ref[2 * p + j, 224:448, :] for j in range(2) for ref in (hown_ref, hother_ref)]
            return part(state, k, v, 512 * p - REACH, False)

        state = (
            jnp.full((1, 256), -1e30, f32),
            jnp.zeros((1, 256), f32),
            jnp.zeros((HEAD_DIM, 256), f32),
        )
        state = own(i, state, True)
        low = low_ref[i]
        state = lax.fori_loop(jnp.maximum(low, 0), i, own, state)
        state = lax.fori_loop(jnp.minimum(low + 4, 4), 4, halo, state)
        top, total, acc = state
        x = (acc / total).astype(bf16)
        x_ref[2 * i, pl.ds(off, HEAD_DIM), :] = x[:, 0:128]
        x_ref[2 * i + 1, pl.ds(off, HEAD_DIM), :] = x[:, 128:256]
        return carry

    lax.fori_loop(0, CHUNKS // 2, tile, 0)
    total = jnp.zeros((WIDE, STATE), f32)
    for b in range(CHUNKS):
        weighted = (x_ref[b].astype(f32) * spread(rows_ref[b, 0:4, :])).astype(bf16)
        state = jnp.dot(weighted, bc_ref[b, :, 0:64], preferred_element_type=f32)
        s_ref[b] = state
        send_ref[b % 8, :, 64 * (b // 8) : 64 * (b // 8) + 64] = state.astype(bf16)
        first = spread(keep_ref[b, 0:4, 0:64])
        second = spread(keep_ref[b, 4:8, 0:64])
        total = (first * second) * total + jnp.where(core == 0, second, 1.0) * state
    f_ref[...] = jnp.concatenate([total[0:128, :], total[128:256, :]], axis=1).astype(bf16)


def attend(core, low, q, kn, knh, own, other, hown, hother, ids, rows, bc, keep):
    return pl.pallas_call(
        attend_kernel,
        in_specs=[pl.BlockSpec(memory_space=pltpu.SMEM)] * 2
        + [pl.BlockSpec(memory_space=pltpu.VMEM)] * 11,
        out_shape=(
            jax.ShapeDtypeStruct((CHUNKS, WIDE, ROWS), bf16),
            jax.ShapeDtypeStruct((CHUNKS, WIDE, STATE), f32),
            jax.ShapeDtypeStruct((8, WIDE, 128), bf16),
            jax.ShapeDtypeStruct((128, 128), bf16),
        ),
        compiler_params=pltpu.CompilerParams(vmem_limit_bytes=VMEM_LIMIT),
        cost_estimate=pl.CostEstimate(flops=6_000_000_000, bytes_accessed=12_000_000, transcendentals=4_000_000),
        name="attend",
    )(core, low, q, kn, knh, own, other, hown, hother, ids, rows, bc, keep)


def local_kernel(par_ref, x_ref, inner_ref, y_ref):
    for b in range(CHUNKS):
        for n in range(SSM):
            x = x_ref[b, 64 * n : 64 * n + 64, :]
            y = jnp.dot(x, inner_ref[b, n], preferred_element_type=f32)
            y_ref[b, 64 * n : 64 * n + 64, :] = y + par_ref[2, n] * x.astype(f32)


def local(params, x, inner):
    return pl.pallas_call(
        local_kernel,
        in_specs=[pl.BlockSpec(memory_space=pltpu.SMEM)] + [pl.BlockSpec(memory_space=pltpu.VMEM)] * 2,
        out_shape=jax.ShapeDtypeStruct((CHUNKS, WIDE, ROWS), f32),
        compiler_params=pltpu.CompilerParams(vmem_limit_bytes=VMEM_LIMIT),
        cost_estimate=pl.CostEstimate(flops=150_000_000, bytes_accessed=6_000_000, transcendentals=0),
        name="scan_local",
    )(params, x, inner)


def carry_kernel(core_ref, y_ref, s_ref, other_ref, f_ref, g_ref, rows_ref, keep_ref, bc_ref, out_ref, hold):
    core, off = core_ref[0], pl.multiple_of(core_ref[1], 32)
    packed = f_ref[...].astype(f32) + g_ref[...].astype(f32)
    state = jnp.concatenate([packed[:, 0:64], packed[:, 64:128]], axis=0)
    for b in range(CHUNKS):
        mine = s_ref[b]
        theirs = other_ref[b % 8, :, 64 * (b // 8) : 64 * (b // 8) + 64].astype(f32)
        first, second = spread(keep_ref[b, 0:4, 0:64]), spread(keep_ref[b, 4:8, 0:64])
        middle = first * state + jnp.where(core == 0, mine, theirs)
        entering = jnp.where(core == 0, state, middle).astype(bf16)
        carried = lax.dot_general(entering, bc_ref[b, :, 64:128], NT, preferred_element_type=f32)
        hold[...] = y_ref[b] + carried * spread(rows_ref[b, 4:8, :])
        out_ref[b] = hold[pl.ds(off, HEAD_DIM), :].astype(bf16)
        state = second * middle + jnp.where(core == 0, theirs, mine)


def carry(core, y, s, other, f, g, rows, keep, bc):
    return pl.pallas_call(
        carry_kernel,
        in_specs=[pl.BlockSpec(memory_space=pltpu.SMEM)] + [pl.BlockSpec(memory_space=pltpu.VMEM)] * 8,
        out_shape=jax.ShapeDtypeStruct((CHUNKS, HEAD_DIM, ROWS), bf16),
        scratch_shapes=[pltpu.VMEM((WIDE, ROWS), f32)],
        compiler_params=pltpu.CompilerParams(vmem_limit_bytes=VMEM_LIMIT),
        name="scan_carry",
    )(core, y, s, other, f, g, rows, keep, bc)


def other_core(x):
    return lax.ppermute(x, "core", [(0, 1), (1, 0)])


def exchange(x):
    return lax.all_to_all(x, ("y", "x"), split_axis=0, concat_axis=0, tiled=True)


def document_starts(segment_ids, plane):
    padded = jnp.concatenate([jnp.full((REACH + 1,), -1, i32), segment_ids])
    window = lax.dynamic_slice_in_dim(padded, plane * PLANE, PLANE + REACH + 1, 0)
    place = jnp.arange(PLANE + REACH, dtype=i32) - REACH
    starts = jnp.where(window[1:] != window[:-1], place, -REACH).reshape(48, 128)
    within = lax.cummax(starts, axis=1)
    before = lax.cummax(within[:, 127], axis=0)
    before = jnp.concatenate([jnp.full((1,), -REACH, i32), before[:-1]])
    return jnp.maximum(within, before[:, None])[16:]


def on_device(
    queries, keys, values, step_raw, step_bias, decay_rate, skip_gain, state_in, state_out, segment_ids
):
    core, planes = lax.axis_index("core"), lax.axis_size("z")
    plane, head = lax.axis_index("z"), 4 * lax.axis_index("y") + lax.axis_index("x")

    both = jnp.concatenate([state_in, state_out], axis=1).reshape(4, 2, ROWS, 128)
    both = lax.dynamic_index_in_dim(both, core, 1, keepdims=False)
    bc = lax.all_gather(both, "y").reshape(CHUNKS, ROWS, 128)
    params = jnp.concatenate([step_bias, decay_rate, skip_gain, jnp.zeros((ROWS - 21,), f32)])[None]
    own = exchange(pack(keys, values, step_raw, params))
    other = other_core(own)
    following = [(i, i + 1) for i in range(planes - 1)]
    halo_own = lax.ppermute(own[8:, :448], "z", following)
    q = exchange(jnp.transpose(queries).reshape(HEADS, HEAD_DIM, ROWS))
    halo_other = other_core(halo_own)

    def whole(rows):
        return jnp.sum(rows[0:4, 452:455, 0:21].astype(f32), axis=1).reshape(4, 3, 7)

    mine, theirs = whole(own), whole(other)
    zero = jnp.where(core == 0, mine, theirs)
    one = jnp.where(core == 0, theirs, mine)
    table = jnp.stack([zero, one], axis=1).transpose(2, 0, 1, 3).reshape(3, 56)
    mamba = lax.dynamic_slice_in_dim(table, (7 * head) >> 1, SSM, 1)

    starts = document_starts(segment_ids, plane).reshape(CHUNKS, 2, ROWS)
    ids = lax.dynamic_index_in_dim(starts, core, 1, keepdims=False)
    ids_other = lax.dynamic_index_in_dim(starts, 1 - core, 1, keepdims=False)
    low = ids[0::2, 0] >> 9
    where = jnp.stack([core, 32 * (head & 1)]).astype(i32)

    def wide(x):
        return jnp.broadcast_to(x[:, None, :], (CHUNKS, 16, ROWS))

    inner, rows, keep = prep(
        where, mamba, own[:, 448:464], other[:, 448:464], wide(ids), wide(ids_other), bc
    )
    kn = turn(own, other)
    knh = turn(halo_own, halo_other)
    x, s, send, final = attend(
        where, low, q, kn, knh, own, other, halo_own, halo_other, ids[:, None, :], rows, bc, keep
    )
    s_other = other_core(send)
    same = lax.ppermute(final, "z", following)
    cross = lax.ppermute(
        final, ("z", "core"), [(2 * i + c, 2 * i + 3 - c) for i in range(planes - 1) for c in range(2)]
    )
    y = local(mamba, x, inner)
    mixed = exchange(carry(where, y, s, s_other, same, cross, rows, keep, bc))
    return jnp.transpose(mixed.reshape(HEADS * HEAD_DIM, ROWS))


def solution(mesh):
    devices = mesh.devices.reshape(-1, 4, 4, 2)
    return jax.shard_map(
        on_device,
        mesh=Mesh(devices, ("z", "y", "x", "core")),
        in_specs=(
            P(("z", "y", "x", "core"), None),
            P(("z", "y", "x", "core"), None),
            P(("z", "y", "x", "core"), None),
            P(("z", "y", "x", "core"), None),
            P(("x", "core")),
            P(("x", "core")),
            P(("x", "core")),
            P(("z", "y"), None),
            P(("z", "y"), None),
            P(),
        ),
        out_specs=P(("z", "y", "x", "core"), None),
        check_vma=False,
    )
```

time: 471 us -> 173 us (0.37)
  the two profiles are of different devices: /device:TPU:1 before, /device:TPU:192 now
where the time goes in v1:
time: 173 us; the launch traced here: 171 us
  blocking collectives  66.9 us (39%)
  Pallas kernels  52.9 us (31%)
  starting transfers between devices  23.5 us (14%)
  local copies, waits for them, and re-layouts  11.7 us (7%)
  waiting for transfers between devices  11.6 us (7%)
  other arithmetic  4.14 us (2%)
    all_to_all x2, blocking collectives, exchange(): lax.all_to_all(x, ('y', 'x'), split_axis=0, concat_axis=0, tiled=True)  53 us
    pallas_call x1, Pallas kernels, attend(): pl.pallas_call(attend_kernel, in_specs=[pl.BlockSpec(memory_space=pltpu.S...  19.3 us
    pallas_call x2, Pallas kernels, turn(): pl.pallas_call(turn_kernel, grid=(count,), in_specs=[block, block], out_s...  14.8 us
    all_gather x1, blocking collectives, on_device(): bc = lax.all_gather(both, 'y').reshape(CHUNKS, ROWS, 128)  14 us
    ppermute x1, waiting for transfers between devices, on_device(): halo_own = lax.ppermute(own[8:, :448], 'z', following)  11.6 us
    ppermute x1, starting transfers between devices, on_device(): same = lax.ppermute(final, 'z', following)  8.21 us
    pallas_call x1, Pallas kernels, prep(): pl.pallas_call(prep_kernel, in_specs=[pl.BlockSpec(memory_space=pltpu.SME...  5.8 us
    ppermute x3, starting transfers between devices, other_core(): return lax.ppermute(x, 'core', [(0, 1), (1, 0)])  5.74 us
  transfers between devices with their start and end apart: 7, of which 1 were waited for; matrix products, arithmetic and copies ran while one was open for 5% of the time, Pallas kernels for 14%

profile of v1, /device:TPU:192, one launch (start us, length us, event | category | flops | bytes accessed | tf_op | source)
XLA Modules:
  0.0 171.0 jit_solution(13289111182448684176)
XLA Ops:
  0.0 1.4 copy.30.raw_ref
  1.4 1.3 maximum_bitcast_fusion.1.par_ref
  2.8 4.0 %pack_keys_values.1 = bf16[16,464,128]{2,1,0:T(8,128)(2,1)} custom-call(bf16[128,3584]{1,0:T(8,128)(2,1)} %k_ref.1, bf16[128,3584]{1,0:T(8,128)(2,1)} %v_ref.1, bf16[128,56]{1,0:T(8,128)(2,1)} %copy.30.raw_ref, f32[1,128]{1,0:T(1,128)} %maximum_bitcast_fusion.1.par_ref), custom_call_target="tpu_custom_call" | custom-call | tf_op jit(solution)/shard_map/pack_keys_values/pallas_call | solution.py:62
  6.8 33.4 %all_to_all.15.own_ref = bf16[16,464,128]{2,1,0:T(8,128)(2,1)S(1)} all-to-all(bf16[16,464,128]{2,1,0:T(8,128)(2,1)} %pack_keys_values.1), channel_id=1, replica_groups=mesh['z'=16,'y'=4,'x'=4,'core'=2] {'y','x'}, dimensions={0} | all-to-all | bytes 3801088 | tf_op jit(solution)/shard_map/all_to_all | solution.py:303
  40.3 1.1 slice.54
  41.4 3.9 %collective-permute-start.1 = (bf16[8,448,128]{2,1,0:T(8,128)(2,1)}, bf16[8,448,128]{2,1,0:T(8,128)(2,1)}, u32[]{:S(2)}, u32[]{:S(2)}) collective-permute-start(bf16[8,448,128]{2,1,0:T(8,128)(2,1)} %slice.54), channel_id=1, source_target_pairs={{0,32},{32,64},{64,96},{96,128},{128,160},{160,192},{192,224},{224... | collective-permute-start | bytes 2752520 | tf_op jit(solution)/shard_map/ppermute | solution.py:330
  45.3 1.9 %collective-permute-start = (bf16[16,464,128]{2,1,0:T(8,128)(2,1)S(1)}, bf16[16,464,128]{2,1,0:T(8,128)(2,1)}, u32[]{:S(2)}, u32[]{:S(2)}) collective-permute-start(bf16[16,464,128]{2,1,0:T(8,128)(2,1)S(1)} %all_to_all.15.own_ref), channel_id=1, source_target_pairs={{0,1},{1,0},{2,3},{3,2},{4,5},{5,4},{6,7},{7,6},{8,9},{9,8},{10,11... | collective-permute-start | bytes 5701640 | tf_op jit(solution)/shard_map/ppermute | solution.py:299
  47.2 0.0 copy-done.1
  47.3 0.0 copy-start.5
  47.3 0.0 copy-start.6
  47.3 1.3 copy.32
  48.6 3.6 %all-to-all-start.1 = ((bf16[16,224,128]{2,1,0:T(8,128)(2,1)}), bf16[16,224,128]{2,1,0:T(8,128)(2,1)S(1)}, u32[]{:S(2)}, u32[]{:S(2)}) async-start(bf16[16,224,128]{2,1,0:T(8,128)(2,1)} %bitcast.8), calls=%async_computation.1 | async-start | bytes 1835008 | tf_op jit(solution)/shard_map/all_to_all | solution.py:303
  52.2 0.0 copy-done.4
  52.2 0.1 add_select_fusion
  52.3 0.3 reduce_window_max.16
  52.6 0.1 slice.50
  52.7 0.1 reduce-window.4
  52.8 0.1 slice_reduce_fusion
  52.9 0.1 pad_add_fusion.1
  52.9 0.1 slice.53
  53.0 11.6 %collective-permute-done.1.own_ref.hown_ref = bf16[8,448,128]{2,1,0:T(8,128)(2,1)} collective-permute-done((bf16[8,448,128]{2,1,0:T(8,128)(2,1)}, bf16[8,448,128]{2,1,0:T(8,128)(2,1)}, u32[]{:S(2)}, u32[]{:S(2)}) %collective-permute-start.1) | collective-permute-done | bytes 917536 | tf_op jit(solution)/shard_map/ppermute | solution.py:330
  64.6 1.9 %collective-permute-start.2 = (bf16[8,448,128]{2,1,0:T(8,128)(2,1)}, bf16[8,448,128]{2,1,0:T(8,128)(2,1)}, u32[]{:S(2)}, u32[]{:S(2)}) collective-permute-start(bf16[8,448,128]{2,1,0:T(8,128)(2,1)} %collective-permute-done.1.own_ref.hown_ref), channel_id=1, source_target_pairs={{0,1},{1,0},{2,3},{3,2},{4,5},{5,4},{6,7},{7,6},{8,9},{9,8},{10,11... | collective-permute-start | bytes 2752520 | tf_op jit(solution)/shard_map/ppermute | solution.py:299
  66.5 0.1 slice_maximum_fusion
  66.6 0.0 copy-start.7
  66.7 0.0 copy-done.5
  66.7 0.2 copy.33
  66.8 0.0 copy-done.6
  66.9 0.2 copy.34
  67.0 0.6 pad_add_fusion.core_ref
  67.6 0.7 shift-right-arithmetic_reduce_fusion.low_ref
  68.3 0.1 pad_maximum_fusion
  68.5 14.0 %all-gather = bf16[16,1,128,128]{3,2,1,0:T(8,128)(2,1)} all-gather(bf16[4,1,128,128]{3,2,1,0:T(8,128)(2,1)S(1)} %constant_dynamic-slice_fusion), channel_id=2, replica_groups=mesh['z'=16,'y'=4,'x'=4,'core'=2] {'y'}, dimensions={0}, use_global_device_ids=true | all-gather | bytes 655360 | tf_op jit(solution)/shard_map/all_gather | solution.py:325
  82.5 0.6 slice.55.own_ref
  83.1 0.0 copy-done
  83.1 0.0 collective-permute-done.2.other_ref.hother_ref
  83.1 5.2 %turn_keys.3.knh_ref = bf16[8,256,224]{2,1,0:T(8,128)(2,1)} custom-call(bf16[8,448,128]{2,1,0:T(8,128)(2,1)} %collective-permute-done.1.own_ref.hown_ref, bf16[8,448,128]{2,1,0:T(8,128)(2,1)} %collective-permute-done.2.other_ref.hother_ref), custom_call_target="tpu_custom_call" | custom-call | bytes 2097152 | tf_op jit(solution)/shard_map/turn_keys/pallas_call | solution.py:86
  88.3 0.0 collective-permute-done.other_ref
  88.4 0.7 convert_reduce_fusion
  89.1 0.1 select_n.54
  89.2 0.1 select_n.56
  89.3 0.1 reshape.71
  89.4 1.5 slice.56.other_ref
  90.8 9.6 %turn_keys.2.kn_ref = bf16[16,256,224]{2,1,0:T(8,128)(2,1)} custom-call(bf16[16,464,128]{2,1,0:T(8,128)(2,1)} %copy-done, bf16[16,464,128]{2,1,0:T(8,128)(2,1)} %collective-permute-done.other_ref), custom_call_target="tpu_custom_call" | custom-call | bytes 4194304 | tf_op jit(solution)/shard_map/turn_keys/pallas_call | solution.py:86
  100.4 0.6 constant_dynamic-slice_fusion.3.par_ref
  101.0 0.7 broadcast_in_dim.29.dso_ref
  101.7 0.0 copy-done.7
  101.7 0.7 broadcast_in_dim.14.ds_ref
  102.3 5.8 %scan_weights.1 = (bf16[16,4,128,128]{3,2,1,0:T(8,128)(2,1)}, f32[16,8,128]{2,1,0:T(8,128)}, f32[16,8,128]{2,1,0:T(8,128)}) custom-call(s32[2]{0:T(128)} %pad_add_fusion.core_ref, f32[3,4]{1,0:T(4,128)} %constant_dynamic-slice_fusion.3.par_ref, bf16[16,16,128]{2,1,0:T(8,128)(2,1)} %slice.55.own_ref, bf16[16,16,128]{2,1,0:T(8,128)(2,1)} %slice.56.other_ref, ...), custom_call_target="tpu_custom_call" | custom-call | flops 200000000 | bytes 8000000 | tf_op jit(solution)/shard_map/scan_weights/pallas_call | solution.py:147
  108.1 0.0 all-to-all-done.1.q_ref
  108.2 0.9 copy-done.2
  109.1 19.3 %attend.1 = (bf16[16,256,128]{2,1,0:T(8,128)(2,1)}, f32[16,256,64]{2,1,0:T(8,128)}, bf16[8,256,128]{2,1,0:T(8,128)(2,1)}, bf16[128,128]{1,0:T(8,128)(2,1)}) custom-call(s32[2]{0:T(128)} %pad_add_fusion.core_ref, s32[8]{0:T(128)} %shift-right-arithmetic_reduce_fusion.low_ref, bf16[16,224,128]{2,1,0:T(8,128)(2,1)} %copy-done.2, ...), custom_call_target="tpu_custom_call" | custom-call | flops 6000000000 | bytes 12000000 | tf_op jit(solution)/shard_map/attend/pallas_call | solution.py:236
  128.4 1.9 %collective-permute-start.3 = (bf16[8,256,128]{2,1,0:T(8,128)(2,1)}, bf16[8,256,128]{2,1,0:T(8,128)(2,1)S(1)}, u32[]{:S(2)}, u32[]{:S(2)}) collective-permute-start(bf16[8,256,128]{2,1,0:T(8,128)(2,1)} %get-tuple-element.17), channel_id=1, source_target_pairs={{0,1},{1,0},{2,3},{3,2},{4,5},{5,4},{6,7},{7,6},{8,9},{9,8},{10,11... | collective-permute-start | bytes 1572872 | tf_op jit(solution)/shard_map/ppermute | solution.py:299
  130.3 1.9 %collective-permute-start.5 = (bf16[128,128]{1,0:T(8,128)(2,1)}, bf16[128,128]{1,0:T(8,128)(2,1)S(1)}, u32[]{:S(2)}, u32[]{:S(2)}) collective-permute-start(bf16[128,128]{1,0:T(8,128)(2,1)} %get-tuple-element.18), channel_id=1, source_target_pairs={{0,33},{1,32},{32,65},{33,64},{64,97},{65,96},{96,129},{97,128},{1... | collective-permute-start | bytes 98312 | tf_op jit(solution)/shard_map/ppermute | solution.py:362
  132.3 8.2 %collective-permute-start.4 = (bf16[128,128]{1,0:T(8,128)(2,1)}, bf16[128,128]{1,0:T(8,128)(2,1)S(1)}, u32[]{:S(2)}, u32[]{:S(2)}) collective-permute-start(bf16[128,128]{1,0:T(8,128)(2,1)} %get-tuple-element.18), channel_id=1, source_target_pairs={{0,32},{32,64},{64,96},{96,128},{128,160},{160,192},{192,224},{224... | collective-permute-start | bytes 98312 | tf_op jit(solution)/shard_map/ppermute | solution.py:361
  140.5 3.9 %scan_local.1.y_ref = f32[16,256,128]{2,1,0:T(8,128)} custom-call(f32[3,4]{1,0:T(4,128)} %constant_dynamic-slice_fusion.3.par_ref, bf16[16,256,128]{2,1,0:T(8,128)(2,1)} %get-tuple-element.14.x_ref, bf16[16,4,128,128]{3,2,1,0:T(8,128)(2,1)} %get-tuple-element.15.inner_ref), custom_call_target="tpu_custom_call" | custom-call | flops 150000000 | bytes 6000000 | tf_op jit(solution)/shard_map/scan_local/pallas_call | solution.py:261
  144.4 0.0 collective-permute-done.5.g_ref
  144.4 0.0 collective-permute-done.4.f_ref
  144.4 0.0 collective-permute-done.3.other_ref
  144.5 0.6 copy-done.8
  145.0 0.0 copy-done.9
  145.1 0.2 copy-done.3
  145.3 5.0 %scan_carry.1 = bf16[16,224,128]{2,1,0:T(8,128)(2,1)} custom-call(s32[2]{0:T(128)} %pad_add_fusion.core_ref, f32[16,256,128]{2,1,0:T(8,128)} %scan_local.1.y_ref, f32[16,256,64]{2,1,0:T(8,128)} %get-tuple-element.16.s_ref, bf16[8,256,128]{2,1,0:T(8,128)(2,1)} %copy-done.3, bf16[128,128]{1,0:T(8,128)(2,1)} %copy-done.9, bf16[128,128]{1,0:T(8,128)(2,1)} %copy-done.8, ...), custom_call_target="tpu_custom_call" | custom-call | tf_op jit(solution)/shard_map/scan_carry/pallas_call | solution.py:288
  150.2 19.5 %all_to_all.16 = bf16[16,224,128]{2,1,0:T(8,128)(2,1)S(1)} all-to-all(bf16[16,224,128]{2,1,0:T(8,128)(2,1)} %scan_carry.1), channel_id=1, replica_groups=mesh['z'=16,'y'=4,'x'=4,'core'=2] {'y','x'}, dimensions={0} | all-to-all | bytes 1835008 | tf_op jit(solution)/shard_map/all_to_all | solution.py:303
  169.7 1.3 copy.35
  (15 shorter events, 0.1 us)
Async XLA Ops:
  6.8 40.4 %copy-start.1 = (bf16[128,3584]{1,0:T(8,128)(2,1)S(1)}, bf16[128,3584]{1,0:T(8,128)(2,1)}, u32[]{:S(2)}) copy-start(bf16[128,3584]{1,0:T(8,128)(2,1)} %param.10) | copy-start | bytes 2752516
  40.3 42.8 %copy-start = (bf16[16,464,128]{2,1,0:T(8,128)(2,1)}, bf16[16,464,128]{2,1,0:T(8,128)(2,1)S(1)}, u32[]{:S(2)}) copy-start(bf16[16,464,128]{2,1,0:T(8,128)(2,1)S(1)} %all_to_all.15.own_ref) | copy-start | bytes 5701636
  41.4 10.8 %copy-start.4 = (s32[65536]{0:T(1024)S(1)}, s32[65536]{0:T(1024)}, u32[]{:S(2)}) copy-start(s32[65536]{0:T(1024)} %param.19) | copy-start | bytes 786436
  41.4 23.3 %collective-permute-start.1 = (bf16[8,448,128]{2,1,0:T(8,128)(2,1)}, bf16[8,448,128]{2,1,0:T(8,128)(2,1)}, u32[]{:S(2)}, u32[]{:S(2)}) collective-permute-start(bf16[8,448,128]{2,1,0:T(8,128)(2,1)} %slice.54), channel_id=1, source_target_pairs={{0,32},{32,64},{64,96},{96,128},{128,160},{160,192},{192,224},{224... | collective-permute-start | bytes 2752520 | tf_op jit(solution)/shard_map/ppermute | solution.py:330
  45.3 43.0 %collective-permute-start = (bf16[16,464,128]{2,1,0:T(8,128)(2,1)S(1)}, bf16[16,464,128]{2,1,0:T(8,128)(2,1)}, u32[]{:S(2)}, u32[]{:S(2)}) collective-permute-start(bf16[16,464,128]{2,1,0:T(8,128)(2,1)S(1)} %all_to_all.15.own_ref), channel_id=1, source_target_pairs={{0,1},{1,0},{2,3},{3,2},{4,5},{5,4},{6,7},{7,6},{8,9},{9,8},{10,11... | collective-permute-start | bytes 5701640 | tf_op jit(solution)/shard_map/ppermute | solution.py:299
  47.3 19.4 %copy-start.5 = (bf16[1024,64]{0,1:T(8,128)(2,1)S(1)}, bf16[1024,64]{0,1:T(8,128)(2,1)}, u32[]{:S(2)}) copy-start(bf16[1024,64]{0,1:T(8,128)(2,1)} %param.17) | copy-start | bytes 393220
  47.3 19.6 %copy-start.6 = (bf16[1024,64]{0,1:T(8,128)(2,1)S(1)}, bf16[1024,64]{0,1:T(8,128)(2,1)}, u32[]{:S(2)}) copy-start(bf16[1024,64]{0,1:T(8,128)(2,1)} %param.18) | copy-start | bytes 393220
  48.6 59.6 %all-to-all-start.1 = ((bf16[16,224,128]{2,1,0:T(8,128)(2,1)}), bf16[16,224,128]{2,1,0:T(8,128)(2,1)S(1)}, u32[]{:S(2)}, u32[]{:S(2)}) async-start(bf16[16,224,128]{2,1,0:T(8,128)(2,1)} %bitcast.8), calls=%async_computation.1 | async-start | bytes 1835008 | tf_op jit(solution)/shard_map/all_to_all | solution.py:303
  64.6 18.5 %collective-permute-start.2 = (bf16[8,448,128]{2,1,0:T(8,128)(2,1)}, bf16[8,448,128]{2,1,0:T(8,128)(2,1)}, u32[]{:S(2)}, u32[]{:S(2)}) collective-permute-start(bf16[8,448,128]{2,1,0:T(8,128)(2,1)} %collective-permute-done.1.own_ref.hown_ref), channel_id=1, source_target_pairs={{0,1},{1,0},{2,3},{3,2},{4,5},{5,4},{6,7},{7,6},{8,9},{9,8},{10,11... | collective-permute-start | bytes 2752520 | tf_op jit(solution)/shard_map/ppermute | solution.py:299
  66.6 35.0 %copy-start.7 = (s32[16,1,128]{2,1,0:T(1,128)}, s32[16,1,128]{2,1,0:T(1,128)S(1)}, u32[]{:S(2)}) copy-start(s32[16,1,128]{2,1,0:T(1,128)S(1)} %get-tuple-element.20.ds_ref) | copy-start | bytes 24580
  108.1 0.9 copy-start.2
  128.4 16.0 %collective-permute-start.3 = (bf16[8,256,128]{2,1,0:T(8,128)(2,1)}, bf16[8,256,128]{2,1,0:T(8,128)(2,1)S(1)}, u32[]{:S(2)}, u32[]{:S(2)}) collective-permute-start(bf16[8,256,128]{2,1,0:T(8,128)(2,1)} %get-tuple-element.17), channel_id=1, source_target_pairs={{0,1},{1,0},{2,3},{3,2},{4,5},{5,4},{6,7},{7,6},{8,9},{9,8},{10,11... | collective-permute-start | bytes 1572872 | tf_op jit(solution)/shard_map/ppermute | solution.py:299
  130.3 14.1 %collective-permute-start.5 = (bf16[128,128]{1,0:T(8,128)(2,1)}, bf16[128,128]{1,0:T(8,128)(2,1)S(1)}, u32[]{:S(2)}, u32[]{:S(2)}) collective-permute-start(bf16[128,128]{1,0:T(8,128)(2,1)} %get-tuple-element.18), channel_id=1, source_target_pairs={{0,33},{1,32},{32,65},{33,64},{64,97},{65,96},{96,129},{97,128},{1... | collective-permute-start | bytes 98312 | tf_op jit(solution)/shard_map/ppermute | solution.py:362
  132.3 12.2 %collective-permute-start.4 = (bf16[128,128]{1,0:T(8,128)(2,1)}, bf16[128,128]{1,0:T(8,128)(2,1)S(1)}, u32[]{:S(2)}, u32[]{:S(2)}) collective-permute-start(bf16[128,128]{1,0:T(8,128)(2,1)} %get-tuple-element.18), channel_id=1, source_target_pairs={{0,32},{32,64},{64,96},{96,128},{128,160},{160,192},{192,224},{224... | collective-permute-start | bytes 98312 | tf_op jit(solution)/shard_map/ppermute | solution.py:361
  144.4 0.6 copy-start.8
  144.4 0.6 copy-start.9
  144.5 0.8 copy-start.3

commit v2 on v1

v2 whole, which is shorter than its diff:
```python
import functools
import math

import jax
import jax.numpy as jnp
from jax import lax
from jax.experimental import pallas as pl
from jax.experimental.pallas import tpu as pltpu
from jax.sharding import Mesh
from jax.sharding import PartitionSpec as P

HEADS = 16
HEAD_DIM = 224
SSM_DIM = 64
STATE = 64
ROWS = 128
PLANE = 4096
REACH = 2048
CHUNKS = 16
SSM = 4
WIDE = SSM * SSM_DIM
KV = 480
FIRST = 496
LOG2E = math.log2(math.e)
NT = (((1,), (1,)), ((), ()))
VMEM_LIMIT = 20 * 1024 * 1024

f32, bf16, i32 = jnp.float32, jnp.bfloat16, jnp.int32


def in_hbm(x):
    return pltpu.with_memory_space_constraint(x, pltpu.HBM)


def iota(shape, dim):
    return lax.broadcasted_iota(i32, shape, dim)


def spread(rows):
    width = rows.shape[-1]
    return jnp.concatenate(
        [jnp.broadcast_to(rows[r : r + 1, :], (SSM_DIM, width)) for r in range(SSM)], axis=0
    )


def parts(x):
    high = x.astype(bf16).astype(f32)
    mid = (x - high).astype(bf16).astype(f32)
    return high, mid, x - high - mid


def pack_first_kernel(bias_ref, decay_ref, skip_ref, k_ref, v_ref, raw_ref, out_ref):
    step = pl.program_id(0)
    vt = jnp.transpose(v_ref[...])
    rr, jj = iota((64, 56), 0), iota((64, 56), 1)
    head, r = 4 * step + (rr >> 4), rr & 15
    chosen = ((r < SSM) & (jj == ((7 * head) >> 1) + r)).astype(bf16)
    rows = jnp.dot(chosen, raw_ref[...], preferred_element_type=f32)
    lane = iota((1, ROWS), 1)
    whole = jnp.zeros((1, ROWS), f32)
    for n, ref in enumerate((bias_ref, decay_ref, skip_ref)):
        for j in range(7):
            whole = jnp.where(lane == 7 * n + j, ref[j], whole)
    high, mid, low = parts(whole)
    r = iota((64, ROWS), 0) & 15
    rows = jnp.where(r == 4, high, jnp.where(r == 5, mid, jnp.where(r == 6, low, rows))).astype(bf16)
    for h in range(4):
        k = k_ref[:, 224 * h : 224 * h + 224]
        out_ref[h, 0:128, :] = k[:, 0:128]
        out_ref[h, 128:256, :] = jnp.concatenate([k[:, 128:224], jnp.zeros((ROWS, 32), bf16)], axis=1)
        out_ref[h, 256:480, :] = vt[224 * h : 224 * h + 224, :]
        out_ref[h, 480:496, :] = rows[16 * h : 16 * h + 16, :]


def pack_first(keys, values, raw, step_bias, decay_rate, skip_gain):
    return pl.pallas_call(
        pack_first_kernel,
        grid=(4,),
        in_specs=[pl.BlockSpec(memory_space=pltpu.SMEM)] * 3
        + [pl.BlockSpec((ROWS, 896), lambda i: (0, i))] * 2
        + [pl.BlockSpec((56, ROWS), lambda i: (0, 0))],
        out_specs=pl.BlockSpec((4, FIRST, ROWS), lambda i: (i, 0, 0)),
        out_shape=jax.ShapeDtypeStruct((HEADS, FIRST, ROWS), bf16),
        name="pack_keys_values",
    )(step_bias, decay_rate, skip_gain, keys, values, raw)


VMEM = pl.BlockSpec(memory_space=pltpu.VMEM)
ANYWHERE = pl.BlockSpec(memory_space=pl.ANY)
SMEM = pl.BlockSpec(memory_space=pltpu.SMEM)
HBM = pl.BlockSpec(memory_space=pltpu.HBM)
CORE, OFFSET, Y_AT, FIRST_MAMBA, LOW = range(5)
NUMBERS = LOW + 4


def cut_kernel(first_ref, before_ref, out_ref):
    out_ref[...] = first_ref[8:16, 0:KV, :]


def cut(first, before):
    return pl.pallas_call(
        cut_kernel,
        in_specs=[VMEM, ANYWHERE],
        out_specs=VMEM,
        out_shape=jax.ShapeDtypeStruct((8, KV, ROWS), bf16),
        compiler_params=pltpu.CompilerParams(vmem_limit_bytes=VMEM_LIMIT),
        name="cut_halo",
    )(first, before)


def gate_kernel(*refs):
    pass


def gate(x, *before):
    return pl.pallas_call(
        gate_kernel,
        in_specs=[HBM] + [ANYWHERE] * len(before),
        out_specs=HBM,
        out_shape=pltpu.HBM(x.shape, x.dtype),
        input_output_aliases={0: 0},
        name="gate",
    )(in_hbm(x), *before)


def tie_kernel(first_ref, *refs):
    refs[-2][...] = first_ref[...]


def tie(first, q, *before):
    return pl.pallas_call(
        tie_kernel,
        in_specs=[VMEM] + [ANYWHERE] * (1 + len(before)),
        out_specs=(VMEM, ANYWHERE),
        out_shape=(jax.ShapeDtypeStruct(first.shape, first.dtype), jax.ShapeDtypeStruct(q.shape, q.dtype)),
        input_output_aliases={0: 0, 1: 1},
        compiler_params=pltpu.CompilerParams(vmem_limit_bytes=VMEM_LIMIT),
        name="tie",
    )(first, q, *before)


def step_sizes(raw, bias, decay):
    z = raw + bias
    dt = jnp.maximum(z, 0.0) + jnp.log1p(jnp.exp(-jnp.abs(z)))
    return dt, -dt * decay


def prep_kernel(
    num_ref, own_ref, other_ref, ds_ref, b0_ref, b1_ref, b2_ref, b3_ref, inner_ref, rows_ref, par_ref, bc_ref, sems
):
    core = num_ref[CORE]
    copies = [
        pltpu.make_async_copy(ref, bc_ref.at[pl.ds(4 * ((num_ref[Y_AT] - d) & 3), 4)], sems.at[d])
        for d, ref in enumerate((b0_ref, b1_ref, b2_ref, b3_ref))
    ]
    for copy in copies:
        copy.start()
    shape = (CHUNKS * 16, ROWS)
    line, lane = iota(shape, 0), iota(shape, 1)
    r = line & 15
    bias, decay = jnp.zeros(shape, f32), jnp.zeros(shape, f32)
    par_ref[...] = jnp.zeros_like(par_ref)
    for n in range(SSM):
        mamba = num_ref[FIRST_MAMBA] + n
        holder = (mamba * 37) >> 8
        at = mamba - 7 * holder
        held = jnp.where((holder & 1) == core, own_ref[holder >> 1], other_ref[holder >> 1]).astype(f32)
        held = held[4:5, :] + held[5:6, :] + held[6:7, :]

        def value(which):
            chosen = jnp.where(iota((1, ROWS), 1) == 7 * which + at, held, 0.0)
            return jnp.sum(chosen, axis=1, keepdims=True)

        for which in range(3):
            par_ref[4 * which + n : 4 * which + n + 1, :] = jnp.broadcast_to(value(which), (1, ROWS))
        bias = jnp.where(r == n, value(0), bias)
        decay = jnp.where(r == n, value(1), decay)
    upper = (iota((ROWS, ROWS), 0) <= iota((ROWS, ROWS), 1)).astype(f32)
    ids = spread_ids(ds_ref, 0)
    dt, log_step = step_sizes(own_ref[...].reshape(shape).astype(f32), bias, decay)
    running = jnp.dot(log_step, upper, precision=lax.Precision.HIGHEST, preferred_element_type=f32)
    start = 256 * (line >> 4) + 128 * core
    whole = jnp.broadcast_to(running[:, 127:128], shape)
    last = jnp.broadcast_to(ids[:, 127:128], shape)
    tail = jnp.where(start + lane >= last, jnp.exp(whole - running) * dt, 0.0)
    enter = jnp.where(ids < start, jnp.exp(running), 0.0)
    for b in range(CHUNKS):
        at = 16 * b
        rows_ref[b, 0:4, :] = tail[at : at + 4, :]
        rows_ref[b, 4:8, :] = enter[at : at + 4, :]
    running_t, dt_t = jnp.transpose(running), jnp.transpose(dt)
    s_at, t_at = iota((ROWS, ROWS), 0), iota((ROWS, ROWS), 1)
    for copy in copies:
        copy.wait()
    for b in range(CHUNKS):
        at = 16 * b
        state_in = jnp.transpose(bc_ref[b, 0:64, :].astype(f32)).astype(bf16)
        mix = jnp.dot(state_in, bc_ref[b, 64:128, :], preferred_element_type=f32)
        base = 256 * b + 128 * core
        allowed = (s_at <= t_at) & (s_at >= ids[at : at + 1, :] - base)
        for n in range(SSM):
            gap = running[at + n : at + n + 1, :] - running_t[:, at + n : at + n + 1]
            value = jnp.exp(jnp.where(allowed, gap, 0.0)) * mix * dt_t[:, at + n : at + n + 1]
            inner_ref[b, n, :, :] = jnp.where(allowed, value, 0.0).astype(bf16)


def spread_ids(ds_ref, which):
    return jnp.concatenate(
        [jnp.broadcast_to(ds_ref[b, which : which + 1, :], (16, ROWS)) for b in range(CHUNKS)], axis=0
    )


STEPS = pl.BlockSpec((CHUNKS, 16, ROWS), lambda i: (0, 30, 0))


def prep(numbers, own, other, ids, maps):
    return pl.pallas_call(
        prep_kernel,
        grid=(1,),
        in_specs=[SMEM, STEPS, STEPS, VMEM] + [ANYWHERE] * 4,
        out_shape=(
            jax.ShapeDtypeStruct((CHUNKS, SSM, ROWS, ROWS), bf16),
            jax.ShapeDtypeStruct((CHUNKS, 8, ROWS), f32),
            jax.ShapeDtypeStruct((16, ROWS), f32),
            jax.ShapeDtypeStruct((CHUNKS, 128, ROWS), bf16),
        ),
        out_specs=(VMEM,) * 4,
        scratch_shapes=[pltpu.SemaphoreType.DMA((4,))],
        compiler_params=pltpu.CompilerParams(vmem_limit_bytes=VMEM_LIMIT),
        cost_estimate=pl.CostEstimate(flops=200_000_000, bytes_accessed=8_000_000, transcendentals=2_000_000),
        name="scan_weights",
    )(numbers, own, other, ids, *maps)


def keep_kernel(num_ref, par_ref, own_ref, other_ref, ds_ref, keep_ref):
    core = num_ref[CORE]
    shape = (CHUNKS * 16, ROWS)
    line = iota(shape, 0)
    bias = jnp.concatenate([par_ref[0:4, :], jnp.zeros((12, ROWS), f32)] * CHUNKS, axis=0)
    decay = jnp.concatenate([par_ref[4:8, :], jnp.zeros((12, ROWS), f32)] * CHUNKS, axis=0)

    def keep(which):
        at = jnp.where(which == core, 0, 1)
        ids = jnp.where(at == 0, spread_ids(ds_ref, 0), spread_ids(ds_ref, 1))
        raw = jnp.where(at == 0, own_ref[...], other_ref[...]).reshape(shape).astype(f32)
        whole = jnp.sum(step_sizes(raw, bias, decay)[1], axis=1, keepdims=True)
        value = jnp.where(ids[:, 127:128] < 256 * (line[:, 0:1] >> 4) + 128 * which, jnp.exp(whole), 0.0)
        return jnp.broadcast_to(value, shape)

    for which in range(2):
        kept = keep(which)
        for b in range(CHUNKS):
            keep_ref[b, 4 * which : 4 * which + 4, :] = kept[16 * b : 16 * b + 4, :]


def keeps(numbers, params, own, other, ids):
    return pl.pallas_call(
        keep_kernel,
        grid=(1,),
        in_specs=[SMEM, VMEM, STEPS, STEPS, VMEM],
        out_specs=VMEM,
        out_shape=jax.ShapeDtypeStruct((CHUNKS, 8, ROWS), f32),
        compiler_params=pltpu.CompilerParams(vmem_limit_bytes=VMEM_LIMIT),
        name="scan_keeps",
    )(numbers, params, own, other, ids)


class Tiles:
    def __init__(self, core, shift, own, other, q, ds, scratch):
        self.core, self.shift, self.refs, self.q, self.ds = core, shift, (own, other), q, ds
        self.even, self.odd, self.turned = scratch

    def start(self, tile):
        for n in range(4):
            self.turned[0:HEAD_DIM, 128 * n : 128 * n + 128] = self.q[4 * tile + n]
        self.turned[HEAD_DIM:256, :] = jnp.zeros((32, 512), bf16)
        self.ids = jnp.concatenate([self.ds[4 * tile + n, 0:1, :] for n in range(4)], axis=1)
        lane = iota((1, 512), 1)
        self.q_at = 1024 * tile + 128 * self.core + (lane & 127) + 256 * (lane >> 7)

    def score(self, p, s, lanes=slice(0, 512)):
        k = jnp.concatenate(
            [
                jnp.concatenate([ref[2 * p + j, 0:128, :], ref[2 * p + j, 128:256, :]], axis=1)
                for j in range(2)
                for ref in self.refs
            ],
            axis=0,
        )
        s[:, lanes] = jnp.dot(k, self.turned[:, lanes], preferred_element_type=f32)

    def absorb(self, p, s, acc_ref, stat_ref, lanes=slice(0, 512), causal=False, valid=True):
        width = lanes.stop - lanes.start
        scale = LOG2E / math.sqrt(HEAD_DIM)
        line = iota((ROWS, width), 0)
        ids = jnp.where(valid, self.ids[:, lanes], 1 << 20)
        pieces = []
        for j in range(4):
            at = 512 * p + self.shift + 256 * (j // 2) + 128 * (self.core if j % 2 == 0 else 1 - self.core)
            allowed = line >= ids - at
            if causal:
                allowed = allowed & (line <= self.q_at[:, lanes] - at)
            pieces.append(jnp.where(allowed, s[128 * j : 128 * j + 128, lanes], -1e30))
        masked = jnp.concatenate(pieces, axis=0)
        top = stat_ref[0:1, lanes]
        new_top = jnp.maximum(top, jnp.max(masked, axis=0, keepdims=True))
        expo = jnp.exp2((masked - new_top) * scale)
        fade = jnp.exp2((top - new_top) * scale)
        stat_ref[1:2, lanes] = stat_ref[1:2, lanes] * fade + jnp.sum(expo, axis=0, keepdims=True)
        stat_ref[0:1, lanes] = new_top
        v = jnp.concatenate([ref[2 * p + j, 256:480, :] for j in range(2) for ref in self.refs], axis=1)
        acc_ref[:, lanes] = acc_ref[:, lanes] * fade + jnp.dot(v, expo.astype(bf16), preferred_element_type=f32)

    def back(self, p, low, acc_ref, stat_ref):
        def two(n, carry):
            at = p - 2 * n
            self.score(jnp.maximum(at - 1, 0), self.odd)
            self.absorb(at, self.even, acc_ref, stat_ref)
            self.score(jnp.maximum(at - 2, 0), self.even)
            self.absorb(jnp.maximum(at - 1, 0), self.odd, acc_ref, stat_ref, valid=at - 1 >= low)
            return carry

        lax.fori_loop(0, jnp.maximum(p - low + 2, 0) >> 1, two, 0)


def buffers(tiles):
    return [
        pltpu.VMEM((512, 512), f32),
        pltpu.VMEM((512, 512), f32),
        pltpu.VMEM((256, 512), bf16),
        pltpu.VMEM((tiles, HEAD_DIM, 512), f32),
        pltpu.VMEM((tiles, 8, 512), f32),
    ]


def own_states(x_ref, rows_ref, keep_ref, maps_ref, send_ref, core):
    total = jnp.zeros((WIDE, STATE), f32)
    for pair in range(4):
        states = []
        for b in (2 * pair, 2 * pair + 1):
            weighted = (x_ref[b].astype(f32) * spread(rows_ref[b, 0:4, :])).astype(bf16)
            state = lax.dot_general(weighted, maps_ref[b, 0:64, :], NT, preferred_element_type=f32)
            states.append(state)
            first, second = spread(keep_ref[b, 0:4, 0:64]), spread(keep_ref[b, 4:8, 0:64])
            total = (first * second) * total + jnp.where(core == 0, second, 1.0) * state
        send_ref[pair] = jnp.concatenate(states, axis=1).astype(bf16)
    return total


def start_all(copies):
    for copy in copies:
        copy.start()


def wait_all(copies):
    for copy in copies:
        copy.wait()


def put_x(x_ref, at, off, acc, total):
    x = (acc / total).astype(bf16)
    for n in range(4):
        x_ref[at + n, pl.ds(off, HEAD_DIM), :] = x[:, 128 * n : 128 * n + 128]


def near_kernel(
    num_any, q_ref, own_ref, other_ref, ds_ref, rows_any, keep_any, maps_any,
    x_out, send_out, left_ref, acc_out, stat_out,
    even, odd, turned, acc_ref, stat_ref, rows_ref, keep_ref, maps_ref, x_ref, send_ref, num_ref, sems,
):
    numbers = pltpu.make_async_copy(num_any, num_ref, sems.at[7])
    numbers.start()
    reads = [
        pltpu.make_async_copy(ref.at[pl.ds(8, 8)], to, sems.at[n])
        for n, (ref, to) in enumerate(((rows_any, rows_ref), (keep_any, keep_ref), (maps_any, maps_ref)))
    ]
    start_all(reads)
    x_ref[...] = jnp.zeros_like(x_ref)
    acc_ref[...] = jnp.zeros_like(acc_ref)
    stat_ref[...] = jnp.where(iota(stat_ref.shape, 1) == 0, -1e30, 0.0)
    numbers.wait()
    core, off = num_ref[CORE], pl.multiple_of(num_ref[OFFSET], 32)
    tiles = Tiles(core, 0, own_ref, other_ref, q_ref, ds_ref, (even, odd, turned))
    late = slice(256, 512)
    for i in range(4):
        acc, stat = acc_ref.at[i], stat_ref.at[i]
        tiles.start(i)
        tiles.score(2 * i + 1, odd, late)
        tiles.score(2 * i, even)
        tiles.absorb(2 * i + 1, odd, acc, stat, late, causal=True)
        tiles.score(max(2 * i - 1, 0), odd)
        tiles.absorb(2 * i, even, acc, stat, causal=True)
        tiles.even, tiles.odd = odd, even
        tiles.back(2 * i - 1, jnp.maximum(num_ref[LOW + i], 0), acc, stat)
        tiles.even, tiles.odd = even, odd
    writes = [
        pltpu.make_async_copy(acc_ref.at[pl.ds(0, 2)], acc_out, sems.at[3]),
        pltpu.make_async_copy(stat_ref.at[pl.ds(0, 2)], stat_out, sems.at[4]),
        pltpu.make_async_copy(x_ref, x_out, sems.at[5]),
        pltpu.make_async_copy(send_ref, send_out, sems.at[6]),
    ]
    start_all(writes[0:2])
    for i in range(2, 4):
        put_x(x_ref, 4 * i - 8, off, acc_ref[i], stat_ref[i, 1:2, :])
    start_all(writes[2:3])
    wait_all(reads)
    total = own_states(x_ref, rows_ref, keep_ref, maps_ref, send_ref, core)
    start_all(writes[3:4])
    left_ref[...] = jnp.concatenate([total[0:128, :], total[128:256, :]], axis=1).astype(bf16)
    wait_all(writes)


STATE_BUFFERS = [
    pltpu.VMEM((8, 8, ROWS), f32),
    pltpu.VMEM((8, 8, ROWS), f32),
    pltpu.VMEM((8, 128, ROWS), bf16),
]


def attend_near(numbers, q, own, other, ids, rows, keep, maps):
    return pl.pallas_call(
        near_kernel,
        in_specs=[HBM] + [VMEM] * 4 + [HBM] * 3,
        out_specs=(HBM, HBM, VMEM, HBM, HBM),
        out_shape=(
            pltpu.HBM((8, WIDE, ROWS), bf16),
            pltpu.HBM((4, WIDE, 128), bf16),
            jax.ShapeDtypeStruct((128, 128), bf16),
            pltpu.HBM((2, HEAD_DIM, 512), f32),
            pltpu.HBM((2, 8, 512), f32),
        ),
        scratch_shapes=buffers(4)
        + STATE_BUFFERS
        + [
            pltpu.VMEM((8, WIDE, ROWS), bf16),
            pltpu.VMEM((4, WIDE, 128), bf16),
            pltpu.SMEM((NUMBERS,), i32),
            pltpu.SemaphoreType.DMA((8,)),
        ],
        compiler_params=pltpu.CompilerParams(vmem_limit_bytes=VMEM_LIMIT),
        cost_estimate=pl.CostEstimate(flops=5_000_000_000, bytes_accessed=9_000_000, transcendentals=4_000_000),
        name="attend_near",
    )(in_hbm(numbers), q, own, other, ids, in_hbm(rows), in_hbm(keep), in_hbm(maps))


def far_kernel(
    num_any, q_ref, own_any, other_ref, ds_ref, came_ref, acc_any, stat_any, rows_any, keep_any, maps_any, late_any,
    x_ref, send_ref, even, odd, turned, acc_ref, stat_ref, rows_ref, keep_ref, maps_ref, own_ref, num_ref, sems,
):
    reads = [
        pltpu.make_async_copy(num_any, num_ref, sems.at[0]),
        pltpu.make_async_copy(own_any, own_ref, sems.at[1]),
        pltpu.make_async_copy(acc_any, acc_ref, sems.at[2]),
        pltpu.make_async_copy(stat_any, stat_ref, sems.at[3]),
        pltpu.make_async_copy(late_any, send_ref.at[pl.ds(4, 4)], sems.at[4]),
        pltpu.make_async_copy(rows_any.at[pl.ds(0, 8)], rows_ref, sems.at[5]),
        pltpu.make_async_copy(keep_any.at[pl.ds(0, 8)], keep_ref, sems.at[6]),
        pltpu.make_async_copy(maps_any.at[pl.ds(0, 8)], maps_ref, sems.at[7]),
    ]
    start_all(reads)
    x_ref[...] = jnp.zeros_like(x_ref)
    send_ref[8, 0:128, :] = came_ref[...]
    send_ref[8, 128:256, :] = jnp.zeros((128, 128), bf16)
    wait_all(reads[0:4])
    core, off = num_ref[CORE], pl.multiple_of(num_ref[OFFSET], 32)
    tiles = Tiles(core, -REACH, own_ref, other_ref, q_ref, ds_ref, (even, odd, turned))
    for i in range(2):
        low = jnp.clip(num_ref[LOW + i] + 4, 0, 4)

        @pl.when(low < 4)
        def _():
            tiles.start(i)
            tiles.score(3, even)
            tiles.back(3, low, acc_ref.at[i], stat_ref.at[i])

        put_x(x_ref, 4 * i, off, acc_ref[i], stat_ref[i, 1:2, :])
    wait_all(reads[4:])
    own_states(x_ref, rows_ref, keep_ref, maps_ref, send_ref, core)


def attend_far(numbers, q, own, other, ids, came, acc, stat, rows, keep, maps, late_states):
    return pl.pallas_call(
        far_kernel,
        in_specs=[HBM, VMEM, HBM] + [VMEM] * 3 + [HBM] * 6,
        out_specs=(VMEM,) * 2,
        out_shape=(
            jax.ShapeDtypeStruct((8, WIDE, ROWS), bf16),
            jax.ShapeDtypeStruct((9, WIDE, 128), bf16),
        ),
        scratch_shapes=buffers(2)
        + STATE_BUFFERS
        + [
            pltpu.VMEM((8, KV, ROWS), bf16),
            pltpu.SMEM((NUMBERS,), i32),
            pltpu.SemaphoreType.DMA((8,)),
        ],
        compiler_params=pltpu.CompilerParams(vmem_limit_bytes=VMEM_LIMIT),
        cost_estimate=pl.CostEstimate(flops=2_000_000_000, bytes_accessed=5_000_000, transcendentals=1_000_000),
        name="attend_far",
    )(
        in_hbm(numbers), q, in_hbm(own), other, ids, came, in_hbm(acc), in_hbm(stat), in_hbm(rows), in_hbm(keep),
        in_hbm(maps), in_hbm(late_states),
    )


def scan_kernel(
    num_ref, par_ref, xe_ref, xl_ref, inner_ref, own_ref, other_ref, f_ref, g_ref, rows_ref, keep_ref, bc_ref,
    out_ref, state_ref, hold,
):
    step = pl.program_id(0)
    core, off = num_ref[CORE], pl.multiple_of(num_ref[OFFSET], 32)
    early = step < 2

    @pl.when(step == 0)
    def _():
        packed = f_ref[0, 0:128, :].astype(f32) + g_ref[0, 0:128, :].astype(f32)
        state_ref[0:128, :] = packed[:, 0:64]
        state_ref[128:256, :] = packed[:, 64:128]

    state = state_ref[...]
    for b in range(4):
        at = slice(64 * (b % 2), 64 * (b % 2) + 64)
        mine, theirs = own_ref[b // 2, :, at].astype(f32), other_ref[b // 2, :, at].astype(f32)
        first, second = spread(keep_ref[b, 0:4, 0:64]), spread(keep_ref[b, 4:8, 0:64])
        middle = first * state + jnp.where(core == 0, mine, theirs)
        entering = jnp.where(core == 0, state, middle).astype(bf16)
        state = second * middle + jnp.where(core == 0, theirs, mine)
        carried = jnp.dot(entering, bc_ref[b, 64:128, :], preferred_element_type=f32)
        enter = rows_ref[b, 4:8, :]
        for n in range(SSM):
            rows = slice(64 * n, 64 * n + 64)
            x = jnp.where(early, xe_ref[b, rows, :], xl_ref[b, rows, :])
            y = jnp.dot(x, inner_ref[b, n], preferred_element_type=f32)
            hold[b, rows, :] = y + par_ref[8 + n : 9 + n, :] * x.astype(f32) + carried[rows] * enter[n : n + 1, :]
        out_ref[b] = hold[b, pl.ds(off, HEAD_DIM), :].astype(bf16)
    state_ref[...] = state


def scan(numbers, params, x, inner, own, other, rows, keep, maps):
    def chunks(*shape):
        return pl.BlockSpec(shape, lambda i: (i,) + (0,) * (len(shape) - 1))

    def halves(*shape):
        zeros = (0,) * (len(shape) - 1)
        return [
            pl.BlockSpec(shape, lambda i: (jnp.minimum(i, 1),) + zeros),
            pl.BlockSpec(shape, lambda i: (jnp.maximum(i - 2, 0),) + zeros),
        ]

    return pl.pallas_call(
        scan_kernel,
        grid=(4,),
        in_specs=[SMEM, pl.BlockSpec((16, ROWS), lambda i: (0, 0))]
        + halves(4, WIDE, ROWS)
        + [chunks(4, SSM, ROWS, ROWS)]
        + [chunks(2, WIDE, 128)] * 2
        + [pl.BlockSpec((1, WIDE, 128), lambda i: (8, 0, 0))] * 2
        + [chunks(4, 8, ROWS), chunks(4, 8, ROWS), chunks(4, 128, ROWS)],
        out_specs=chunks(4, HEAD_DIM, ROWS),
        out_shape=jax.ShapeDtypeStruct((CHUNKS, HEAD_DIM, ROWS), bf16),
        scratch_shapes=[pltpu.VMEM((WIDE, STATE), f32), pltpu.VMEM((4, WIDE, ROWS), f32)],
        compiler_params=pltpu.CompilerParams(vmem_limit_bytes=VMEM_LIMIT),
        name="scan",
    )(numbers, params, *x, inner, own, other, own, other, rows, keep, maps)


def other_core(x):
    return lax.ppermute(x, "core", [(0, 1), (1, 0)])


def exchange(x):
    return lax.all_to_all(x, ("y", "x"), split_axis=0, concat_axis=0, tiled=True)


def document_starts(segment_ids, plane):
    padded = jnp.concatenate([jnp.full((REACH + 1,), -1, i32), segment_ids])
    window = lax.dynamic_slice_in_dim(padded, plane * PLANE, PLANE + REACH + 1, 0)
    place = jnp.arange(PLANE + REACH, dtype=i32) - REACH
    starts = jnp.where(window[1:] != window[:-1], place, -REACH).reshape(48, 128)
    within = lax.cummax(starts, axis=1)
    before = lax.cummax(within[:, 127], axis=0)
    before = jnp.concatenate([jnp.full((1,), -REACH, i32), before[:-1]])
    return jnp.maximum(within, before[:, None])[16:]


def on_device(
    queries, keys, values, step_raw, step_bias, decay_rate, skip_gain, state_in, state_out, segment_ids
):
    core, planes = lax.axis_index("core"), lax.axis_size("z")
    plane, head = lax.axis_index("z"), 4 * lax.axis_index("y") + lax.axis_index("x")
    following = [(i, i + 1) for i in range(planes - 1)]

    first = exchange(pack_first(keys, values, jnp.transpose(step_raw), step_bias, decay_rate, skip_gain))
    both = jnp.concatenate([jnp.transpose(state_in), jnp.transpose(state_out)], axis=0).reshape(128, 4, 2, ROWS)
    both = jnp.transpose(lax.dynamic_index_in_dim(both, core, 2, keepdims=False), (1, 0, 2))
    maps = [both] + [lax.ppermute(both, "y", [(i, (i + d) % 4) for i in range(4)]) for d in range(1, 4)]

    starts = document_starts(segment_ids, plane).reshape(CHUNKS, 2, ROWS)
    ids = jnp.where(core == 0, starts, starts[:, ::-1])
    low = ids[0::4, 0, 0] >> 9
    numbers = [core, 32 * (head & 1), lax.axis_index("y"), (7 * head) >> 1]
    numbers = jnp.concatenate([jnp.stack(numbers).astype(i32), low])
    q = jnp.transpose(queries).reshape(HEADS, HEAD_DIM, ROWS)
    first, q = tie(first, q, ids, numbers, *maps)

    q = exchange(q)
    other = other_core(first)
    halo = lax.ppermute(cut(first, other), "z", following)
    inner, rows, params, bc = prep(numbers, first, other, ids, maps)
    keep = keeps(numbers, params, first, other, ids)

    late, late_states, left, acc, stat = attend_near(numbers, q, first, other, ids, rows, keep, bc)
    came = lax.ppermute(left, "z", following)
    halo = gate(halo, late_states)
    early, states = attend_far(
        numbers, q, halo, other_core(halo), ids, came, acc, stat, rows, keep, bc, late_states
    )
    mixed = scan(numbers, params, (early, late), inner, states, other_core(states), rows, keep, bc)
    return jnp.transpose(exchange(mixed).reshape(HEADS * HEAD_DIM, ROWS))


def solution(mesh):
    devices = mesh.devices.reshape(-1, 4, 4, 2)
    return jax.shard_map(
        on_device,
        mesh=Mesh(devices, ("z", "y", "x", "core")),
        in_specs=(
            P(("z", "y", "x", "core"), None),
            P(("z", "y", "x", "core"), None),
            P(("z", "y", "x", "core"), None),
            P(("z", "y", "x", "core"), None),
            P(("x", "core")),
            P(("x", "core")),
            P(("x", "core")),
            P(("z", "y"), None),
            P(("z", "y"), None),
            P(),
        ),
        out_specs=P(("z", "y", "x", "core"), None),
        check_vma=False,
    )
```

time: 173 us -> 124 us (0.72)
  the two profiles are of different devices: /device:TPU:192 before, /device:TPU:128 now
where the time goes in v2:
time: 124 us; the launch traced here: 123 us
  starting transfers between devices  36.2 us (29%)
  Pallas kernels  30.8 us (25%)
  waiting for transfers between devices  23.4 us (19%)
  blocking collectives  21.7 us (18%)
  local copies, waits for them, and re-layouts  8.03 us (6%)
  other arithmetic  2.36 us (2%)
    all_to_all x1, blocking collectives, exchange(): lax.all_to_all(x, ('y', 'x'), split_axis=0, concat_axis=0, tiled=True)  21.7 us
    ppermute x3, waiting for transfers between devices, on_device(): lax.ppermute(both, 'y', [(i, (i + d) % 4) for i in range(4)])  15.3 us
    all_to_all x2, starting transfers between devices, exchange(): lax.all_to_all(x, ('y', 'x'), split_axis=0, concat_axis=0, tiled=True)  12.1 us
    pallas_call x1, Pallas kernels, attend_near(): pl.pallas_call(near_kernel, in_specs=[HBM] + [VMEM] * 4 + [HBM] * 3, out_...  11.4 us
    ppermute x3, starting transfers between devices, on_device(): lax.ppermute(both, 'y', [(i, (i + d) % 4) for i in range(4)])  10.6 us
    pallas_call x1, Pallas kernels, attend_far(): pl.pallas_call(far_kernel, in_specs=[HBM, VMEM, HBM] + [VMEM] * 3 + [HBM]...  6.05 us
    ppermute x3, starting transfers between devices, other_core(): return lax.ppermute(x, 'core', [(0, 1), (1, 0)])  5.87 us
    pallas_call x1, Pallas kernels, prep(): pl.pallas_call(prep_kernel, grid=(1,), in_specs=[SMEM, STEPS, STEPS, VMEM...  4.79 us
  transfers between devices with their start and end apart: 10, of which 5 were waited for; matrix products, arithmetic and copies ran while one was open for 4% of the time, Pallas kernels for 14%

profile of v2, /device:TPU:128, one launch (start us, length us, event | category | flops | bytes accessed | tf_op | source)
XLA Modules:
  0.0 122.8 jit_solution(15321466224799097992)
XLA Ops:
  0.0 4.2 %pack_keys_values.1 = bf16[16,496,128]{2,1,0:T(8,128)(2,1)} custom-call(f32[7]{0:T(128)} %bias_ref.1, f32[7]{0:T(128)} %decay_ref.1, f32[7]{0:T(128)} %skip_ref.1, bf16[128,3584]{1,0:T(8,128)(2,1)} %k_ref.1, bf16[128,3584]{1,0:T(8,128)(2,1)} %v_ref.1, bf16[56,128]{1,0:T(8,128)(2,1)} %bitcast.40), custom_call_target="tpu_custom_call" | custom-call | tf_op jit(solution)/shard_map/pack_keys_values/pallas_call | solution.py:76
  4.2 7.2 %all-to-all-start = ((bf16[16,496,128]{2,1,0:T(8,128)(2,1)}), bf16[16,496,128]{2,1,0:T(8,128)(2,1)S(1)}, u32[]{:S(2)}, u32[]{:S(2)}) async-start(bf16[16,496,128]{2,1,0:T(8,128)(2,1)} %pack_keys_values.1), calls=%async_computation | async-start | bytes 4063232 | tf_op jit(solution)/shard_map/all_to_all | solution.py:572
  11.4 0.0 copy-start.14
  11.4 0.0 copy-done.15
  11.4 0.0 copy-done.16
  11.5 0.2 reshape.26
  11.6 0.3 constant_dynamic-slice_fusion
  12.0 5.0 %collective-permute-start.2 = (bf16[4,128,128]{2,1,0:T(8,128)(2,1)S(1)}, bf16[4,128,128]{2,1,0:T(8,128)(2,1)S(1)}, u32[]{:S(2)}, u32[]{:S(2)}) collective-permute-start(bf16[4,128,128]{2,1,0:T(8,128)(2,1)S(1)} %bitcast.22), channel_id=1, source_target_pairs={{0,24},{8,0},{16,8},{24,16},{1,25},{9,1},{17,9},{25,17},{2,26},{10... | collective-permute-start | bytes 393224 | tf_op jit(solution)/shard_map/ppermute | solution.py:596
  17.0 2.8 %collective-permute-start.1 = (bf16[4,128,128]{2,1,0:T(8,128)(2,1)S(1)}, bf16[4,128,128]{2,1,0:T(8,128)(2,1)S(1)}, u32[]{:S(2)}, u32[]{:S(2)}) collective-permute-start(bf16[4,128,128]{2,1,0:T(8,128)(2,1)S(1)} %bitcast.23), channel_id=1, source_target_pairs={{0,16},{8,24},{16,0},{24,8},{1,17},{9,25},{17,1},{25,9},{2,18},{10... | collective-permute-start | bytes 393224 | tf_op jit(solution)/shard_map/ppermute | solution.py:596
  19.8 2.8 %collective-permute-start = (bf16[4,128,128]{2,1,0:T(8,128)(2,1)S(1)}, bf16[4,128,128]{2,1,0:T(8,128)(2,1)S(1)}, u32[]{:S(2)}, u32[]{:S(2)}) collective-permute-start(bf16[4,128,128]{2,1,0:T(8,128)(2,1)S(1)} %bitcast.24), channel_id=1, source_target_pairs={{0,8},{8,16},{16,24},{24,0},{1,9},{9,17},{17,25},{25,1},{2,10},{10... | collective-permute-start | bytes 393224 | tf_op jit(solution)/shard_map/ppermute | solution.py:596
  22.6 0.9 add_select_fusion
  23.5 0.3 reduce_window_max.16
  23.8 0.7 slice.28
  24.5 0.8 reduce-window.4
  25.3 0.1 slice_reduce_fusion
  25.4 0.1 pad_add_fusion
  25.5 0.1 slice.31
  25.6 0.1 slice_maximum_fusion
  25.6 0.1 rev.3
  25.7 0.0 copy-done.14
  25.7 1.3 %copy.17 = bf16[3584,128]{1,0:T(8,128)(2,1)} copy(bf16[3584,128]{0,1:T(8,128)(2,1)S(1)} %bitcast.34) | data formatting | bytes 1835008 | tf_op jit(solution)/shard_map/transpose | solution.py:603
  27.0 0.2 shift-right-arithmetic_reduce_fusion
  27.2 0.1 concatenate.14.refs_2_.num_ref.num_any
  27.3 12.4 %collective-permute-done.2.refs_6_.b3_ref = bf16[4,128,128]{2,1,0:T(8,128)(2,1)S(1)} collective-permute-done((bf16[4,128,128]{2,1,0:T(8,128)(2,1)S(1)}, bf16[4,128,128]{2,1,0:T(8,128)(2,1)S(1)}, u32[]{:S(2)}, u32[]{:S(2)}) %collective-permute-start.2) | collective-permute-done | bytes 131104 | tf_op jit(solution)/shard_map/ppermute | solution.py:596
  39.7 0.0 collective-permute-done.1.refs_5_.b2_ref
  39.7 2.9 %collective-permute-done.refs_4_.b1_ref = bf16[4,128,128]{2,1,0:T(8,128)(2,1)S(1)} collective-permute-done((bf16[4,128,128]{2,1,0:T(8,128)(2,1)S(1)}, bf16[4,128,128]{2,1,0:T(8,128)(2,1)S(1)}, u32[]{:S(2)}, u32[]{:S(2)}) %collective-permute-start) | collective-permute-done | bytes 131104 | tf_op jit(solution)/shard_map/ppermute | solution.py:596
  42.5 0.0 all-to-all-done.first_ref
  42.6 0.5 tie.1
  43.1 2.0 %collective-permute-start.3 = (bf16[16,496,128]{2,1,0:T(8,128)(2,1)S(1)}, bf16[16,496,128]{2,1,0:T(8,128)(2,1)}, u32[]{:S(2)}, u32[]{:S(2)}) collective-permute-start(bf16[16,496,128]{2,1,0:T(8,128)(2,1)S(1)} %get-tuple-element.18.own_ref.first_ref), channel_id=1, source_target_pairs={{0,1},{1,0},{2,3},{3,2},{4,5},{5,4},{6,7},{7,6},{8,9},{9,8},{10,11... | collective-permute-start | bytes 6094856 | tf_op jit(solution)/shard_map/ppermute | solution.py:568
  45.1 0.0 copy-done.11
  45.1 5.0 %all-to-all-start.1 = ((bf16[16,224,128]{2,1,0:T(8,128)(2,1)}), bf16[16,224,128]{2,1,0:T(8,128)(2,1)}, u32[]{:S(2)}, u32[]{:S(2)}) async-start(bf16[16,224,128]{2,1,0:T(8,128)(2,1)} %get-tuple-element.20), calls=%async_computation.1 | async-start | bytes 1835008 | tf_op jit(solution)/shard_map/all_to_all | solution.py:572
  50.1 0.0 copy-start.12
  50.1 0.0 collective-permute-done.3.other_ref.before_ref
  50.1 0.1 cut_halo.1
  50.2 3.8 %collective-permute-start.4 = (bf16[8,480,128]{2,1,0:T(8,128)(2,1)S(1)}, bf16[8,480,128]{2,1,0:T(8,128)(2,1)}, u32[]{:S(2)}, u32[]{:S(2)}) collective-permute-start(bf16[8,480,128]{2,1,0:T(8,128)(2,1)S(1)} %cut_halo.1), channel_id=1, source_target_pairs={{0,32},{32,64},{64,96},{96,128},{128,160},{160,192},{192,224},{224... | collective-permute-start | bytes 2949128 | tf_op jit(solution)/shard_map/ppermute | solution.py:608
  54.0 0.0 copy-done.12
  54.0 4.8 %scan_weights.1 = (bf16[16,4,128,128]{3,2,1,0:T(8,128)(2,1)S(1)}, f32[16,8,128]{2,1,0:T(8,128)S(1)}, f32[16,128]{1,0:T(8,128)S(1)}, bf16[16,128,128]{2,1,0:T(8,128)(2,1)S(1)}) custom-call(s32[8]{0:T(128)S(1)} %copy-done.12, bf16[16,496,128]{2,1,0:T(8,128)(2,1)S(1)} %get-tuple-element.18.own_ref.first_ref, ...), custom_call_target="tpu_custom_call" | custom-call | flops 200000000 | bytes 8000000 | tf_op jit(solution)/shard_map/scan_weights/pallas_call | solution.py:217
  58.8 0.0 copy-start
  58.8 1.3 %copy-done = bf16[16,4,128,128]{3,2,1,0:T(8,128)(2,1)} copy-done((bf16[16,4,128,128]{3,2,1,0:T(8,128)(2,1)}, bf16[16,4,128,128]{3,2,1,0:T(8,128)(2,1)S(1)}, u32[]{:S(2)}) %copy-start) | copy-done | bytes 2097176
  60.2 0.8 copy-done.2
  61.0 0.6 copy-done.7
  61.6 1.1 scan_keeps.1.keep_any.keep_ref
  62.7 0.6 copy-done.5
  63.3 0.6 copy-done.9
  63.9 2.9 %all-to-all-done.1.q_ref = bf16[16,224,128]{2,1,0:T(8,128)(2,1)} async-done(((bf16[16,224,128]{2,1,0:T(8,128)(2,1)}), bf16[16,224,128]{2,1,0:T(8,128)(2,1)}, u32[]{:S(2)}, u32[]{:S(2)}) %all-to-all-start.1) | async-done | bytes 917536 | tf_op jit(solution)/shard_map/all_to_all | solution.py:572
  66.8 11.4 %attend_near.1 = (bf16[8,256,128]{2,1,0:T(8,128)(2,1)}, bf16[4,256,128]{2,1,0:T(8,128)(2,1)}, bf16[128,128]{1,0:T(8,128)(2,1)S(1)}, f32[2,224,512]{2,1,0:T(8,128)}, f32[2,8,512]{2,1,0:T(8,128)}) custom-call(s32[8]{0:T(128)} %copy-done.11, bf16[16,224,128]{2,1,0:T(8,128)(2,1)} %all-to-all-done.1.q_ref, ...), custom_call_target="tpu_custom_call" | custom-call | flops 5000000000 | bytes 9000000 | tf_op jit(solution)/shard_map/attend_near/pallas_call | solution.py:421
  78.3 0.0 collective-permute-done.4.refs_0_
  78.3 1.9 %collective-permute-start.5 = (bf16[8,480,128]{2,1,0:T(8,128)(2,1)}, bf16[8,480,128]{2,1,0:T(8,128)(2,1)S(1)}, u32[]{:S(2)}, u32[]{:S(2)}) collective-permute-start(bf16[8,480,128]{2,1,0:T(8,128)(2,1)} %gate.1.own_any), channel_id=1, source_target_pairs={{0,1},{1,0},{2,3},{3,2},{4,5},{5,4},{6,7},{7,6},{8,9},{9,8},{10,11... | collective-permute-start | bytes 2949128 | tf_op jit(solution)/shard_map/ppermute | solution.py:568
  80.2 3.8 %collective-permute-start.6 = (bf16[128,128]{1,0:T(8,128)(2,1)S(1)}, bf16[128,128]{1,0:T(8,128)(2,1)S(1)}, u32[]{:S(2)}, u32[]{:S(2)}) collective-permute-start(bf16[128,128]{1,0:T(8,128)(2,1)S(1)} %get-tuple-element.24), channel_id=1, source_target_pairs={{0,32},{32,64},{64,96},{96,128},{128,160},{160,192},{192,224},{224... | collective-permute-start | bytes 98312 | tf_op jit(solution)/shard_map/ppermute | solution.py:613
  84.1 3.2 %collective-permute-done.6.came_ref = bf16[128,128]{1,0:T(8,128)(2,1)S(1)} collective-permute-done((bf16[128,128]{1,0:T(8,128)(2,1)S(1)}, bf16[128,128]{1,0:T(8,128)(2,1)S(1)}, u32[]{:S(2)}, u32[]{:S(2)}) %collective-permute-start.6) | collective-permute-done | bytes 32800 | tf_op jit(solution)/shard_map/ppermute | solution.py:613
  87.3 0.0 collective-permute-done.5.other_ref
  87.3 0.0 copy-start.6
  87.3 0.0 copy-start.8
  87.3 0.0 copy-start.10
  87.3 0.0 copy-start.13
  87.3 6.1 %attend_far.1 = (bf16[8,256,128]{2,1,0:T(8,128)(2,1)S(1)}, bf16[9,256,128]{2,1,0:T(8,128)(2,1)S(1)}) custom-call(s32[8]{0:T(128)} %copy-done.11, bf16[16,224,128]{2,1,0:T(8,128)(2,1)} %all-to-all-done.1.q_ref, bf16[8,480,128]{2,1,0:T(8,128)(2,1)} %gate.1.own_any, bf16[8,480,128]{2,1,0:T(8,128)(2,1)S(1)} %collective-permute-done.5.other_ref, ...), custom_call_target="tpu_custom_call" | custom-call | flops 2000000000 | bytes 5000000 | tf_op jit(solution)/shard_map/attend_far/pallas_call | solution.py:482
  93.4 1.9 %collective-permute-start.7 = (bf16[9,256,128]{2,1,0:T(8,128)(2,1)S(1)}, bf16[9,256,128]{2,1,0:T(8,128)(2,1)S(1)}, u32[]{:S(2)}, u32[]{:S(2)}) collective-permute-start(bf16[9,256,128]{2,1,0:T(8,128)(2,1)S(1)} %get-tuple-element.30.own_ref.f_ref), channel_id=1, source_target_pairs={{0,1},{1,0},{2,3},{3,2},{4,5},{5,4},{6,7},{7,6},{8,9},{9,8},{10,11... | collective-permute-start | bytes 1769480 | tf_op jit(solution)/shard_map/ppermute | solution.py:568
  95.3 2.0 %collective-permute-done.7.other_ref.g_ref = bf16[9,256,128]{2,1,0:T(8,128)(2,1)S(1)} collective-permute-done((bf16[9,256,128]{2,1,0:T(8,128)(2,1)S(1)}, bf16[9,256,128]{2,1,0:T(8,128)(2,1)S(1)}, u32[]{:S(2)}, u32[]{:S(2)}) %collective-permute-start.7) | collective-permute-done | bytes 589856 | tf_op jit(solution)/shard_map/ppermute | solution.py:568
  97.3 0.0 copy-done.1
  97.3 0.0 copy-done.3
  97.3 0.0 copy-done.4
  97.3 2.6 %scan.1 = bf16[16,224,128]{2,1,0:T(8,128)(2,1)S(1)} custom-call(s32[8]{0:T(128)S(1)} %copy-done.13, f32[16,128]{1,0:T(8,128)S(1)} %copy-done.10, bf16[8,256,128]{2,1,0:T(8,128)(2,1)S(1)} %get-tuple-element.27.xe_ref, bf16[8,256,128]{2,1,0:T(8,128)(2,1)S(1)} %copy-done.4, bf16[16,4,128,128]{3,2,1,0:T(8,128)(2,1)S(1)} %copy-done.1, ...), custom_call_target="tpu_custom_call" | custom-call | tf_op jit(solution)/shard_map/scan/pallas_call | solution.py:550
  99.9 21.7 %all_to_all.15 = bf16[16,224,128]{2,1,0:T(8,128)(2,1)S(1)} all-to-all(bf16[16,224,128]{2,1,0:T(8,128)(2,1)S(1)} %scan.1), channel_id=1, replica_groups=mesh['z'=16,'y'=4,'x'=4,'core'=2] {'y','x'}, dimensions={0} | all-to-all | bytes 1835008 | tf_op jit(solution)/shard_map/all_to_all | solution.py:572
  121.6 1.3 %copy.19 = bf16[3584,128]{0,1:T(8,128)(2,1)} copy(bf16[3584,128]{1,0:T(8,128)(2,1)S(1)} %bitcast.33) | data formatting | bytes 1835008 | tf_op jit(solution)/shard_map/reshape | solution.py:619
  (18 shorter events, 0.1 us)
Async XLA Ops:
  4.2 7.2 %copy-start.15 = (bf16[1024,64]{0,1:T(8,128)(2,1)S(1)}, bf16[1024,64]{0,1:T(8,128)(2,1)}, u32[]{:S(2)}) copy-start(bf16[1024,64]{0,1:T(8,128)(2,1)} %param.18) | copy-start | bytes 393220
  4.2 7.2 %copy-start.16 = (bf16[1024,64]{0,1:T(8,128)(2,1)S(1)}, bf16[1024,64]{0,1:T(8,128)(2,1)}, u32[]{:S(2)}) copy-start(bf16[1024,64]{0,1:T(8,128)(2,1)} %param.17) | copy-start | bytes 393220
  4.2 38.3 %all-to-all-start = ((bf16[16,496,128]{2,1,0:T(8,128)(2,1)}), bf16[16,496,128]{2,1,0:T(8,128)(2,1)S(1)}, u32[]{:S(2)}, u32[]{:S(2)}) async-start(bf16[16,496,128]{2,1,0:T(8,128)(2,1)} %pack_keys_values.1), calls=%async_computation | async-start | bytes 4063232 | tf_op jit(solution)/shard_map/all_to_all | solution.py:572
  11.4 14.3 %copy-start.14 = (bf16[128,3584]{1,0:T(8,128)(2,1)S(1)}, bf16[128,3584]{1,0:T(8,128)(2,1)}, u32[]{:S(2)}) copy-start(bf16[128,3584]{1,0:T(8,128)(2,1)} %param.10) | copy-start | bytes 2752516
  12.0 27.7 %collective-permute-start.2 = (bf16[4,128,128]{2,1,0:T(8,128)(2,1)S(1)}, bf16[4,128,128]{2,1,0:T(8,128)(2,1)S(1)}, u32[]{:S(2)}, u32[]{:S(2)}) collective-permute-start(bf16[4,128,128]{2,1,0:T(8,128)(2,1)S(1)} %bitcast.22), channel_id=1, source_target_pairs={{0,24},{8,0},{16,8},{24,16},{1,25},{9,1},{17,9},{25,17},{2,26},{10... | collective-permute-start | bytes 393224 | tf_op jit(solution)/shard_map/ppermute | solution.py:596
  17.0 22.7 %collective-permute-start.1 = (bf16[4,128,128]{2,1,0:T(8,128)(2,1)S(1)}, bf16[4,128,128]{2,1,0:T(8,128)(2,1)S(1)}, u32[]{:S(2)}, u32[]{:S(2)}) collective-permute-start(bf16[4,128,128]{2,1,0:T(8,128)(2,1)S(1)} %bitcast.23), channel_id=1, source_target_pairs={{0,16},{8,24},{16,0},{24,8},{1,17},{9,25},{17,1},{25,9},{2,18},{10... | collective-permute-start | bytes 393224 | tf_op jit(solution)/shard_map/ppermute | solution.py:596
  19.8 22.8 %collective-permute-start = (bf16[4,128,128]{2,1,0:T(8,128)(2,1)S(1)}, bf16[4,128,128]{2,1,0:T(8,128)(2,1)S(1)}, u32[]{:S(2)}, u32[]{:S(2)}) collective-permute-start(bf16[4,128,128]{2,1,0:T(8,128)(2,1)S(1)} %bitcast.24), channel_id=1, source_target_pairs={{0,8},{8,16},{16,24},{24,0},{1,9},{9,17},{17,25},{25,1},{2,10},{10... | collective-permute-start | bytes 393224 | tf_op jit(solution)/shard_map/ppermute | solution.py:596
  27.2 17.9 %copy-start.11 = (s32[8]{0:T(128)}, s32[8]{0:T(128)S(1)}, u32[]{:S(2)}) copy-start(s32[8]{0:T(128)S(1)} %concatenate.14.refs_2_.num_ref.num_any) | copy-start | bytes 100
  43.1 7.0 %collective-permute-start.3 = (bf16[16,496,128]{2,1,0:T(8,128)(2,1)S(1)}, bf16[16,496,128]{2,1,0:T(8,128)(2,1)}, u32[]{:S(2)}, u32[]{:S(2)}) collective-permute-start(bf16[16,496,128]{2,1,0:T(8,128)(2,1)S(1)} %get-tuple-element.18.own_ref.first_ref), channel_id=1, source_target_pairs={{0,1},{1,0},{2,3},{3,2},{4,5},{5,4},{6,7},{7,6},{8,9},{9,8},{10,11... | collective-permute-start | bytes 6094856 | tf_op jit(solution)/shard_map/ppermute | solution.py:568
  45.1 21.7 %all-to-all-start.1 = ((bf16[16,224,128]{2,1,0:T(8,128)(2,1)}), bf16[16,224,128]{2,1,0:T(8,128)(2,1)}, u32[]{:S(2)}, u32[]{:S(2)}) async-start(bf16[16,224,128]{2,1,0:T(8,128)(2,1)} %get-tuple-element.20), calls=%async_computation.1 | async-start | bytes 1835008 | tf_op jit(solution)/shard_map/all_to_all | solution.py:572
  50.1 3.9 %copy-start.12 = (s32[8]{0:T(128)S(1)}, s32[8]{0:T(128)}, u32[]{:S(2)}) copy-start(s32[8]{0:T(128)} %copy-done.11) | copy-start | bytes 100
  50.2 28.1 %collective-permute-start.4 = (bf16[8,480,128]{2,1,0:T(8,128)(2,1)S(1)}, bf16[8,480,128]{2,1,0:T(8,128)(2,1)}, u32[]{:S(2)}, u32[]{:S(2)}) collective-permute-start(bf16[8,480,128]{2,1,0:T(8,128)(2,1)S(1)} %cut_halo.1), channel_id=1, source_target_pairs={{0,32},{32,64},{64,96},{96,128},{128,160},{160,192},{192,224},{224... | collective-permute-start | bytes 2949128 | tf_op jit(solution)/shard_map/ppermute | solution.py:608
  58.8 1.3 %copy-start = (bf16[16,4,128,128]{3,2,1,0:T(8,128)(2,1)}, bf16[16,4,128,128]{3,2,1,0:T(8,128)(2,1)S(1)}, u32[]{:S(2)}) copy-start(bf16[16,4,128,128]{3,2,1,0:T(8,128)(2,1)S(1)} %get-tuple-element.29.inner_ref) | copy-start | bytes 6291460
  60.2 0.8 copy-start.2
  61.0 0.6 copy-start.7
  62.7 0.6 copy-start.5
  63.3 0.6 copy-start.9
  78.3 8.9 %collective-permute-start.5 = (bf16[8,480,128]{2,1,0:T(8,128)(2,1)}, bf16[8,480,128]{2,1,0:T(8,128)(2,1)S(1)}, u32[]{:S(2)}, u32[]{:S(2)}) collective-permute-start(bf16[8,480,128]{2,1,0:T(8,128)(2,1)} %gate.1.own_any), channel_id=1, source_target_pairs={{0,1},{1,0},{2,3},{3,2},{4,5},{5,4},{6,7},{7,6},{8,9},{9,8},{10,11... | collective-permute-start | bytes 2949128 | tf_op jit(solution)/shard_map/ppermute | solution.py:568
  80.2 7.0 %collective-permute-start.6 = (bf16[128,128]{1,0:T(8,128)(2,1)S(1)}, bf16[128,128]{1,0:T(8,128)(2,1)S(1)}, u32[]{:S(2)}, u32[]{:S(2)}) collective-permute-start(bf16[128,128]{1,0:T(8,128)(2,1)S(1)} %get-tuple-element.24), channel_id=1, source_target_pairs={{0,32},{32,64},{64,96},{96,128},{128,160},{160,192},{192,224},{224... | collective-permute-start | bytes 98312 | tf_op jit(solution)/shard_map/ppermute | solution.py:613
  87.3 10.0 %copy-start.1 = (bf16[16,4,128,128]{3,2,1,0:T(8,128)(2,1)S(1)}, bf16[16,4,128,128]{3,2,1,0:T(8,128)(2,1)}, u32[]{:S(2)}) copy-start(bf16[16,4,128,128]{3,2,1,0:T(8,128)(2,1)} %copy-done) | copy-start | bytes 6291460
  87.3 10.0 %copy-start.3 = (bf16[16,128,128]{2,1,0:T(8,128)(2,1)S(1)}, bf16[16,128,128]{2,1,0:T(8,128)(2,1)}, u32[]{:S(2)}) copy-start(bf16[16,128,128]{2,1,0:T(8,128)(2,1)} %copy-done.2) | copy-start | bytes 1572868
  87.3 10.0 %copy-start.4 = (bf16[8,256,128]{2,1,0:T(8,128)(2,1)S(1)}, bf16[8,256,128]{2,1,0:T(8,128)(2,1)}, u32[]{:S(2)}) copy-start(bf16[8,256,128]{2,1,0:T(8,128)(2,1)} %get-tuple-element.28.xl_ref) | copy-start | bytes 1572868
  87.3 10.0 %copy-start.6 = (f32[16,8,128]{2,1,0:T(8,128)S(1)}, f32[16,8,128]{2,1,0:T(8,128)}, u32[]{:S(2)}) copy-start(f32[16,8,128]{2,1,0:T(8,128)} %copy-done.5) | copy-start | bytes 196612
  87.3 10.0 %copy-start.8 = (f32[16,8,128]{2,1,0:T(8,128)S(1)}, f32[16,8,128]{2,1,0:T(8,128)}, u32[]{:S(2)}) copy-start(f32[16,8,128]{2,1,0:T(8,128)} %copy-done.7) | copy-start | bytes 196612
  87.3 10.0 %copy-start.10 = (f32[16,128]{1,0:T(8,128)S(1)}, f32[16,128]{1,0:T(8,128)}, u32[]{:S(2)}) copy-start(f32[16,128]{1,0:T(8,128)} %copy-done.9) | copy-start | bytes 24580
  87.3 10.0 %copy-start.13 = (s32[8]{0:T(128)S(1)}, s32[8]{0:T(128)}, u32[]{:S(2)}) copy-start(s32[8]{0:T(128)} %copy-done.11) | copy-start | bytes 100
  93.4 3.9 %collective-permute-start.7 = (bf16[9,256,128]{2,1,0:T(8,128)(2,1)S(1)}, bf16[9,256,128]{2,1,0:T(8,128)(2,1)S(1)}, u32[]{:S(2)}, u32[]{:S(2)}) collective-permute-start(bf16[9,256,128]{2,1,0:T(8,128)(2,1)S(1)} %get-tuple-element.30.own_ref.f_ref), channel_id=1, source_target_pairs={{0,1},{1,0},{2,3},{3,2},{4,5},{5,4},{6,7},{7,6},{8,9},{9,8},{10,11... | collective-permute-start | bytes 1769480 | tf_op jit(solution)/shard_map/ppermute | solution.py:568

commit v3 on v2

--- a/solution.py
+++ b/solution.py
@@ -25,11 +25,22 @@
 NT = (((1,), (1,)), ((), ()))
 VMEM_LIMIT = 20 * 1024 * 1024
 
+VMEM = pl.BlockSpec(memory_space=pltpu.VMEM)
+ANYWHERE = pl.BlockSpec(memory_space=pl.ANY)
+SMEM = pl.BlockSpec(memory_space=pltpu.SMEM)
+HBM = pl.BlockSpec(memory_space=pltpu.HBM)
+CORE, OFFSET, Y_AT, FIRST_MAMBA, LOW = range(5)
+NUMBERS = LOW + 4
+
 f32, bf16, i32 = jnp.float32, jnp.bfloat16, jnp.int32
 
 
 def in_hbm(x):
     return pltpu.with_memory_space_constraint(x, pltpu.HBM)
+
+
+def in_vmem(x):
+    return pltpu.with_memory_space_constraint(x, pltpu.VMEM)
 
 
 def iota(shape, dim):
@@ -49,48 +60,71 @@
     return high, mid, x - high - mid
 
 
-def pack_first_kernel(bias_ref, decay_ref, skip_ref, k_ref, v_ref, raw_ref, out_ref):
-    step = pl.program_id(0)
-    vt = jnp.transpose(v_ref[...])
-    rr, jj = iota((64, 56), 0), iota((64, 56), 1)
-    head, r = 4 * step + (rr >> 4), rr & 15
-    chosen = ((r < SSM) & (jj == ((7 * head) >> 1) + r)).astype(bf16)
-    rows = jnp.dot(chosen, raw_ref[...], preferred_element_type=f32)
+def pack_first_kernel(
+    bias_any, decay_any, skip_any, k_any, v_any, raw_any, out_any,
+    k_ref, v_ref, raw_ref, out_ref, bias_ref, decay_ref, skip_ref, sems
+):
+    copies = []
+    for step in range(4):
+        at = pl.ds(896 * step, 896)
+        copies.append(pltpu.make_async_copy(v_any.at[:, at], v_ref.at[step], sems.at[2 * step]))
+        copies.append(pltpu.make_async_copy(k_any.at[:, at], k_ref.at[step], sems.at[2 * step + 1]))
+    small = [
+        pltpu.make_async_copy(have, need, sems.at[12 + n])
+        for n, (have, need) in enumerate(
+            ((raw_any, raw_ref), (bias_any, bias_ref), (decay_any, decay_ref), (skip_any, skip_ref))
+        )
+    ]
+    start_all(small + copies)
+    wait_all(small)
     lane = iota((1, ROWS), 1)
     whole = jnp.zeros((1, ROWS), f32)
     for n, ref in enumerate((bias_ref, decay_ref, skip_ref)):
         for j in range(7):
             whole = jnp.where(lane == 7 * n + j, ref[j], whole)
     high, mid, low = parts(whole)
-    r = iota((64, ROWS), 0) & 15
+    rr, jj = iota((256, 56), 0), iota((256, 56), 1)
+    chosen = (((rr & 15) < SSM) & (jj == ((7 * (rr >> 4)) >> 1) + (rr & 15))).astype(bf16)
+    rows = jnp.dot(chosen, raw_ref[...], preferred_element_type=f32)
+    r = iota((256, ROWS), 0) & 15
     rows = jnp.where(r == 4, high, jnp.where(r == 5, mid, jnp.where(r == 6, low, rows))).astype(bf16)
-    for h in range(4):
-        k = k_ref[:, 224 * h : 224 * h + 224]
-        out_ref[h, 0:128, :] = k[:, 0:128]
-        out_ref[h, 128:256, :] = jnp.concatenate([k[:, 128:224], jnp.zeros((ROWS, 32), bf16)], axis=1)
-        out_ref[h, 256:480, :] = vt[224 * h : 224 * h + 224, :]
+    for h in range(HEADS):
         out_ref[h, 480:496, :] = rows[16 * h : 16 * h + 16, :]
+    writes = []
+    for step in range(4):
+        wait_all(copies[2 * step : 2 * step + 2])
+        vt = jnp.transpose(v_ref[step])
+        for n in range(4):
+            h = 4 * step + n
+            k = k_ref[step, :, 224 * n : 224 * n + 224]
+            out_ref[h, 0:128, :] = k[:, 0:128]
+            out_ref[h, 128:256, :] = jnp.concatenate([k[:, 128:224], jnp.zeros((ROWS, 32), bf16)], axis=1)
+            out_ref[h, 256:480, :] = vt[224 * n : 224 * n + 224, :]
+        at = pl.ds(4 * step, 4)
+        writes.append(pltpu.make_async_copy(out_ref.at[at], out_any.at[at], sems.at[8 + step]))
+        writes[-1].start()
+    wait_all(writes)
 
 
 def pack_first(keys, values, raw, step_bias, decay_rate, skip_gain):
     return pl.pallas_call(
         pack_first_kernel,
-        grid=(4,),
-        in_specs=[pl.BlockSpec(memory_space=pltpu.SMEM)] * 3
-        + [pl.BlockSpec((ROWS, 896), lambda i: (0, i))] * 2
-        + [pl.BlockSpec((56, ROWS), lambda i: (0, 0))],
-        out_specs=pl.BlockSpec((4, FIRST, ROWS), lambda i: (i, 0, 0)),
-        out_shape=jax.ShapeDtypeStruct((HEADS, FIRST, ROWS), bf16),
+        in_specs=[HBM] * 6,
+        out_specs=HBM,
+        out_shape=pltpu.HBM((HEADS, FIRST, ROWS), bf16),
+        scratch_shapes=[
+            pltpu.VMEM((4, ROWS, 896), bf16),
+            pltpu.VMEM((4, ROWS, 896), bf16),
+            pltpu.VMEM((56, ROWS), bf16),
+            pltpu.VMEM((HEADS, FIRST, ROWS), bf16),
+            pltpu.SMEM((7,), f32),
+            pltpu.SMEM((7,), f32),
+            pltpu.SMEM((7,), f32),
+            pltpu.SemaphoreType.DMA((16,)),
+        ],
+        compiler_params=pltpu.CompilerParams(vmem_limit_bytes=VMEM_LIMIT),
         name="pack_keys_values",
-    )(step_bias, decay_rate, skip_gain, keys, values, raw)
-
-
-VMEM = pl.BlockSpec(memory_space=pltpu.VMEM)
-ANYWHERE = pl.BlockSpec(memory_space=pl.ANY)
-SMEM = pl.BlockSpec(memory_space=pltpu.SMEM)
-HBM = pl.BlockSpec(memory_space=pltpu.HBM)
-CORE, OFFSET, Y_AT, FIRST_MAMBA, LOW = range(5)
-NUMBERS = LOW + 4
+    )(*(in_hbm(x) for x in (step_bias, decay_rate, skip_gain, keys, values, raw)))
 
 
 def cut_kernel(first_ref, before_ref, out_ref):
@@ -115,28 +149,23 @@
 def gate(x, *before):
     return pl.pallas_call(
         gate_kernel,
-        in_specs=[HBM] + [ANYWHERE] * len(before),
-        out_specs=HBM,
-        out_shape=pltpu.HBM(x.shape, x.dtype),
+        in_specs=[ANYWHERE] * (1 + len(before)),
+        out_specs=ANYWHERE,
+        out_shape=pltpu.VMEM(x.shape, x.dtype),
         input_output_aliases={0: 0},
         name="gate",
-    )(in_hbm(x), *before)
-
-
-def tie_kernel(first_ref, *refs):
-    refs[-2][...] = first_ref[...]
+    )(in_vmem(x), *before)
 
 
 def tie(first, q, *before):
     return pl.pallas_call(
-        tie_kernel,
-        in_specs=[VMEM] + [ANYWHERE] * (1 + len(before)),
-        out_specs=(VMEM, ANYWHERE),
-        out_shape=(jax.ShapeDtypeStruct(first.shape, first.dtype), jax.ShapeDtypeStruct(q.shape, q.dtype)),
+        gate_kernel,
+        in_specs=[ANYWHERE] * (2 + len(before)),
+        out_specs=(ANYWHERE,) * 2,
+        out_shape=(pltpu.VMEM(first.shape, first.dtype), jax.ShapeDtypeStruct(q.shape, q.dtype)),
         input_output_aliases={0: 0, 1: 1},
-        compiler_params=pltpu.CompilerParams(vmem_limit_bytes=VMEM_LIMIT),
         name="tie",
-    )(first, q, *before)
+    )(in_vmem(first), q, *before)
 
 
 def step_sizes(raw, bias, decay):
@@ -323,16 +352,6 @@
         lax.fori_loop(0, jnp.maximum(p - low + 2, 0) >> 1, two, 0)
 
 
-def buffers(tiles):
-    return [
-        pltpu.VMEM((512, 512), f32),
-        pltpu.VMEM((512, 512), f32),
-        pltpu.VMEM((256, 512), bf16),
-        pltpu.VMEM((tiles, HEAD_DIM, 512), f32),
-        pltpu.VMEM((tiles, 8, 512), f32),
-    ]
-
-
 def own_states(x_ref, rows_ref, keep_ref, maps_ref, send_ref, core):
     total = jnp.zeros((WIDE, STATE), f32)
     for pair in range(4):
@@ -366,42 +385,58 @@
 def near_kernel(
     num_any, q_ref, own_ref, other_ref, ds_ref, rows_any, keep_any, maps_any,
     x_out, send_out, left_ref, acc_out, stat_out,
-    even, odd, turned, acc_ref, stat_ref, rows_ref, keep_ref, maps_ref, x_ref, send_ref, num_ref, sems,
+    even, odd, even_2, odd_2, turned, turned_2, acc_ref, stat_ref, x_ref, send_ref, rows_ref, keep_ref, maps_ref, num_ref, sems,
 ):
-    numbers = pltpu.make_async_copy(num_any, num_ref, sems.at[7])
+    numbers = pltpu.make_async_copy(num_any, num_ref, sems.at[3])
     numbers.start()
     reads = [
         pltpu.make_async_copy(ref.at[pl.ds(8, 8)], to, sems.at[n])
         for n, (ref, to) in enumerate(((rows_any, rows_ref), (keep_any, keep_ref), (maps_any, maps_ref)))
     ]
     start_all(reads)
-    x_ref[...] = jnp.zeros_like(x_ref)
     acc_ref[...] = jnp.zeros_like(acc_ref)
     stat_ref[...] = jnp.where(iota(stat_ref.shape, 1) == 0, -1e30, 0.0)
+    writes = [
+        pltpu.make_async_copy(acc_ref.at[pl.ds(0, 2)], acc_out, sems.at[4]),
+        pltpu.make_async_copy(stat_ref.at[pl.ds(0, 2)], stat_out, sems.at[5]),
+        pltpu.make_async_copy(x_ref, x_out, sems.at[6]),
+        pltpu.make_async_copy(send_ref, send_out, sems.at[7]),
+    ]
+    core = lax.axis_index("core")
+    sets = [
+        Tiles(core, 0, own_ref, other_ref, q_ref, ds_ref, scratch)
+        for scratch in ((even, odd, turned), (even_2, odd_2, turned_2))
+    ]
+    late = slice(256, 512)
+
+    def state_of(i):
+        return acc_ref.at[i], stat_ref.at[i]
+
+    def begin(i):
+        tiles = sets[i % 2]
+        tiles.start(i)
+        tiles.score(2 * i + 1, tiles.odd, late)
+        tiles.score(2 * i, tiles.even)
+
+    begin(0)
+    for i in range(4):
+        if i < 3:
+            begin(i + 1)
+        tiles = sets[i % 2]
+        tiles.absorb(2 * i + 1, tiles.odd, *state_of(i), late, causal=True)
+        tiles.absorb(2 * i, tiles.even, *state_of(i), causal=True)
     numbers.wait()
-    core, off = num_ref[CORE], pl.multiple_of(num_ref[OFFSET], 32)
-    tiles = Tiles(core, 0, own_ref, other_ref, q_ref, ds_ref, (even, odd, turned))
-    late = slice(256, 512)
-    for i in range(4):
-        acc, stat = acc_ref.at[i], stat_ref.at[i]
+    off = pl.multiple_of(num_ref[OFFSET], 32)
+    x_ref[...] = jnp.zeros_like(x_ref)
+    for i in range(1, 4):
+        tiles = sets[i % 2]
         tiles.start(i)
-        tiles.score(2 * i + 1, odd, late)
-        tiles.score(2 * i, even)
-        tiles.absorb(2 * i + 1, odd, acc, stat, late, causal=True)
-        tiles.score(max(2 * i - 1, 0), odd)
-        tiles.absorb(2 * i, even, acc, stat, causal=True)
-        tiles.even, tiles.odd = odd, even
-        tiles.back(2 * i - 1, jnp.maximum(num_ref[LOW + i], 0), acc, stat)
-        tiles.even, tiles.odd = even, odd
-    writes = [
-        pltpu.make_async_copy(acc_ref.at[pl.ds(0, 2)], acc_out, sems.at[3]),
-        pltpu.make_async_copy(stat_ref.at[pl.ds(0, 2)], stat_out, sems.at[4]),
-        pltpu.make_async_copy(x_ref, x_out, sems.at[5]),
-        pltpu.make_async_copy(send_ref, send_out, sems.at[6]),
-    ]
-    start_all(writes[0:2])
-    for i in range(2, 4):
-        put_x(x_ref, 4 * i - 8, off, acc_ref[i], stat_ref[i, 1:2, :])
+        tiles.score(2 * i - 1, tiles.even)
+        tiles.back(2 * i - 1, jnp.maximum(num_ref[LOW + i], 0), *state_of(i))
+        if i == 1:
+            start_all(writes[0:2])
+        else:
+            put_x(x_ref, 4 * i - 8, off, acc_ref[i], stat_ref[i, 1:2, :])
     start_all(writes[2:3])
     wait_all(reads)
     total = own_states(x_ref, rows_ref, keep_ref, maps_ref, send_ref, core)
@@ -429,14 +464,12 @@
             pltpu.HBM((2, HEAD_DIM, 512), f32),
             pltpu.HBM((2, 8, 512), f32),
         ),
-        scratch_shapes=buffers(4)
+        scratch_shapes=[pltpu.VMEM((512, 512), f32)] * 4
+        + [pltpu.VMEM((256, 512), bf16)] * 2
+        + [pltpu.VMEM((4, HEAD_DIM, 512), f32), pltpu.VMEM((4, 8, 512), f32)]
+        + [pltpu.VMEM((8, WIDE, ROWS), bf16), pltpu.VMEM((4, WIDE, 128), bf16)]
         + STATE_BUFFERS
-        + [
-            pltpu.VMEM((8, WIDE, ROWS), bf16),
-            pltpu.VMEM((4, WIDE, 128), bf16),
-            pltpu.SMEM((NUMBERS,), i32),
-            pltpu.SemaphoreType.DMA((8,)),
-        ],
+        + [pltpu.SMEM((NUMBERS,), i32), pltpu.SemaphoreType.DMA((8,))],
         compiler_params=pltpu.CompilerParams(vmem_limit_bytes=VMEM_LIMIT),
         cost_estimate=pl.CostEstimate(flops=5_000_000_000, bytes_accessed=9_000_000, transcendentals=4_000_000),
         name="attend_near",
@@ -444,62 +477,74 @@
 
 
 def far_kernel(
-    num_any, q_ref, own_any, other_ref, ds_ref, came_ref, acc_any, stat_any, rows_any, keep_any, maps_any, late_any,
-    x_ref, send_ref, even, odd, turned, acc_ref, stat_ref, rows_ref, keep_ref, maps_ref, own_ref, num_ref, sems,
+    num_any, q_ref, own_ref, other_ref, ds_ref, came_ref, acc_any, stat_any, late_any, rows_any, keep_any, maps_any,
+    x_ref, send_ref, even, odd, turned, acc_ref, stat_ref, near_acc, near_stat, rows_ref, keep_ref, maps_ref, num_ref, sems,
 ):
     reads = [
         pltpu.make_async_copy(num_any, num_ref, sems.at[0]),
-        pltpu.make_async_copy(own_any, own_ref, sems.at[1]),
-        pltpu.make_async_copy(acc_any, acc_ref, sems.at[2]),
-        pltpu.make_async_copy(stat_any, stat_ref, sems.at[3]),
-        pltpu.make_async_copy(late_any, send_ref.at[pl.ds(4, 4)], sems.at[4]),
-        pltpu.make_async_copy(rows_any.at[pl.ds(0, 8)], rows_ref, sems.at[5]),
-        pltpu.make_async_copy(keep_any.at[pl.ds(0, 8)], keep_ref, sems.at[6]),
-        pltpu.make_async_copy(maps_any.at[pl.ds(0, 8)], maps_ref, sems.at[7]),
+        pltpu.make_async_copy(rows_any.at[pl.ds(0, 8)], rows_ref, sems.at[1]),
+        pltpu.make_async_copy(keep_any.at[pl.ds(0, 8)], keep_ref, sems.at[2]),
+        pltpu.make_async_copy(maps_any.at[pl.ds(0, 8)], maps_ref, sems.at[3]),
     ]
+    reads[1:1] = [
+        pltpu.make_async_copy(acc_any, near_acc, sems.at[4]),
+        pltpu.make_async_copy(stat_any, near_stat, sems.at[5]),
+    ]
+    reads.append(pltpu.make_async_copy(late_any, send_ref.at[pl.ds(4, 4)], sems.at[6]))
     start_all(reads)
     x_ref[...] = jnp.zeros_like(x_ref)
     send_ref[8, 0:128, :] = came_ref[...]
     send_ref[8, 128:256, :] = jnp.zeros((128, 128), bf16)
-    wait_all(reads[0:4])
-    core, off = num_ref[CORE], pl.multiple_of(num_ref[OFFSET], 32)
+    acc_ref[...] = jnp.zeros_like(acc_ref)
+    stat_ref[...] = jnp.where(iota(stat_ref.shape, 1) == 0, -1e30, 0.0)
+    core = lax.axis_index("core")
     tiles = Tiles(core, -REACH, own_ref, other_ref, q_ref, ds_ref, (even, odd, turned))
+    tiles.start(0)
+    tiles.score(3, even)
+    wait_all(reads[0:1])
+    off = pl.multiple_of(num_ref[OFFSET], 32)
     for i in range(2):
         low = jnp.clip(num_ref[LOW + i] + 4, 0, 4)
 
         @pl.when(low < 4)
         def _():
-            tiles.start(i)
-            tiles.score(3, even)
+            if i > 0:
+                tiles.start(i)
+                tiles.score(3, even)
             tiles.back(3, low, acc_ref.at[i], stat_ref.at[i])
 
-        put_x(x_ref, 4 * i, off, acc_ref[i], stat_ref[i, 1:2, :])
-    wait_all(reads[4:])
+    wait_all(reads[1:3])
+    scale = LOG2E / math.sqrt(HEAD_DIM)
+    for i in range(2):
+        top = jnp.maximum(near_stat[i, 0:1, :], stat_ref[i, 0:1, :])
+        near = jnp.exp2((near_stat[i, 0:1, :] - top) * scale)
+        far = jnp.exp2((stat_ref[i, 0:1, :] - top) * scale)
+        total = near_stat[i, 1:2, :] * near + stat_ref[i, 1:2, :] * far
+        put_x(x_ref, 4 * i, off, near_acc[i] * near + acc_ref[i] * far, total)
+    wait_all(reads[3:])
     own_states(x_ref, rows_ref, keep_ref, maps_ref, send_ref, core)
 
 
 def attend_far(numbers, q, own, other, ids, came, acc, stat, rows, keep, maps, late_states):
     return pl.pallas_call(
         far_kernel,
-        in_specs=[HBM, VMEM, HBM] + [VMEM] * 3 + [HBM] * 6,
+        in_specs=[HBM] + [VMEM] * 5 + [HBM] * 6,
         out_specs=(VMEM,) * 2,
         out_shape=(
             jax.ShapeDtypeStruct((8, WIDE, ROWS), bf16),
             jax.ShapeDtypeStruct((9, WIDE, 128), bf16),
         ),
-        scratch_shapes=buffers(2)
+        scratch_shapes=[pltpu.VMEM((512, 512), f32)] * 2
+        + [pltpu.VMEM((256, 512), bf16)]
+        + [pltpu.VMEM((2, HEAD_DIM, 512), f32), pltpu.VMEM((2, 8, 512), f32)] * 2
         + STATE_BUFFERS
-        + [
-            pltpu.VMEM((8, KV, ROWS), bf16),
-            pltpu.SMEM((NUMBERS,), i32),
-            pltpu.SemaphoreType.DMA((8,)),
-        ],
+        + [pltpu.SMEM((NUMBERS,), i32), pltpu.SemaphoreType.DMA((7,))],
         compiler_params=pltpu.CompilerParams(vmem_limit_bytes=VMEM_LIMIT),
         cost_estimate=pl.CostEstimate(flops=2_000_000_000, bytes_accessed=5_000_000, transcendentals=1_000_000),
         name="attend_far",
     )(
-        in_hbm(numbers), q, in_hbm(own), other, ids, came, in_hbm(acc), in_hbm(stat), in_hbm(rows), in_hbm(keep),
-        in_hbm(maps), in_hbm(late_states),
+        in_hbm(numbers), q, in_vmem(own), other, ids, came, in_hbm(acc), in_hbm(stat), in_hbm(late_states),
+        in_hbm(rows), in_hbm(keep), in_hbm(maps),
     )
 
 

time: 124 us -> 122 us (0.984)
  the two profiles are of different devices: /device:TPU:128 before, /device:TPU:256 now
where the time goes in v3:
time: 122 us; the launch traced here: 121 us
  starting transfers between devices  35.6 us (29%)
  Pallas kernels  27.1 us (22%)
  waiting for transfers between devices  25.2 us (21%)
  blocking collectives  22.7 us (19%)
  local copies, waits for them, and re-layouts  8.08 us (7%)
  other arithmetic  1.63 us (1%)
    all_to_all x1, blocking collectives, exchange(): lax.all_to_all(x, ('y', 'x'), split_axis=0, concat_axis=0, tiled=True)  22.7 us
    ppermute x3, waiting for transfers between devices, on_device(): lax.ppermute(both, 'y', [(i, (i + d) % 4) for i in range(4)])  16 us
    all_to_all x2, starting transfers between devices, exchange(): lax.all_to_all(x, ('y', 'x'), split_axis=0, concat_axis=0, tiled=True)  12.2 us
    pallas_call x1, Pallas kernels, attend_near(): pl.pallas_call(near_kernel, in_specs=[HBM] + [VMEM] * 4 + [HBM] * 3, out_...  10.6 us
    ppermute x3, starting transfers between devices, on_device(): lax.ppermute(both, 'y', [(i, (i + d) % 4) for i in range(4)])  10.6 us
    ppermute x3, starting transfers between devices, other_core(): return lax.ppermute(x, 'core', [(0, 1), (1, 0)])  5.85 us
    pallas_call x1, Pallas kernels, attend_far(): pl.pallas_call(far_kernel, in_specs=[HBM] + [VMEM] * 5 + [HBM] * 6, out_s...  4.99 us
    pallas_call x1, Pallas kernels, prep(): pl.pallas_call(prep_kernel, grid=(1,), in_specs=[SMEM, STEPS, STEPS, VMEM...  4.79 us
  transfers between devices with their start and end apart: 10, of which 5 were waited for; matrix products, arithmetic and copies ran while one was open for 4% of the time, Pallas kernels for 14%

profile of v3, /device:TPU:256, one launch (start us, length us, event | category | flops | bytes accessed | tf_op | source)
XLA Modules:
  0.0 120.8 jit_solution(2239811398952854825)
XLA Ops:
  0.0 2.9 %pack_keys_values.1 = bf16[16,496,128]{2,1,0:T(8,128)(2,1)} custom-call(f32[7]{0:T(128)} %bias_any.1, f32[7]{0:T(128)} %decay_any.1, f32[7]{0:T(128)} %skip_any.1, bf16[128,3584]{1,0:T(8,128)(2,1)} %k_any.1, bf16[128,3584]{1,0:T(8,128)(2,1)} %v_any.1, bf16[56,128]{1,0:T(8,128)(2,1)} %bitcast.41), custom_call_target="tpu_custom_call" | custom-call | tf_op jit(solution)/shard_map/pack_keys_values/pallas_call | solution.py:110
  2.9 0.0 copy-start.22
  2.9 0.0 copy-start.23
  2.9 7.2 %all-to-all-start = ((bf16[16,496,128]{2,1,0:T(8,128)(2,1)}), bf16[16,496,128]{2,1,0:T(8,128)(2,1)S(1)}, u32[]{:S(2)}, u32[]{:S(2)}) async-start(bf16[16,496,128]{2,1,0:T(8,128)(2,1)} %pack_keys_values.1), calls=%async_computation | async-start | bytes 4063232 | tf_op jit(solution)/shard_map/all_to_all | solution.py:617
  10.1 0.0 copy-start.21
  10.1 0.0 copy-done.22
  10.1 0.0 copy-done.23
  10.2 0.2 reshape.26
  10.4 0.3 constant_dynamic-slice_fusion
  10.7 0.0 copy-start.2
  10.7 5.0 %collective-permute-start.2 = (bf16[4,128,128]{2,1,0:T(8,128)(2,1)S(1)}, bf16[4,128,128]{2,1,0:T(8,128)(2,1)S(1)}, u32[]{:S(2)}, u32[]{:S(2)}) collective-permute-start(bf16[4,128,128]{2,1,0:T(8,128)(2,1)S(1)} %bitcast.22), channel_id=1, source_target_pairs={{0,24},{8,0},{16,8},{24,16},{1,25},{9,1},{17,9},{25,17},{2,26},{10... | collective-permute-start | bytes 393224 | tf_op jit(solution)/shard_map/ppermute | solution.py:641
  15.7 2.8 %collective-permute-start.1 = (bf16[4,128,128]{2,1,0:T(8,128)(2,1)S(1)}, bf16[4,128,128]{2,1,0:T(8,128)(2,1)S(1)}, u32[]{:S(2)}, u32[]{:S(2)}) collective-permute-start(bf16[4,128,128]{2,1,0:T(8,128)(2,1)S(1)} %bitcast.23), channel_id=1, source_target_pairs={{0,16},{8,24},{16,0},{24,8},{1,17},{9,25},{17,1},{25,9},{2,18},{10... | collective-permute-start | bytes 393224 | tf_op jit(solution)/shard_map/ppermute | solution.py:641
  18.5 2.8 %collective-permute-start = (bf16[4,128,128]{2,1,0:T(8,128)(2,1)S(1)}, bf16[4,128,128]{2,1,0:T(8,128)(2,1)S(1)}, u32[]{:S(2)}, u32[]{:S(2)}) collective-permute-start(bf16[4,128,128]{2,1,0:T(8,128)(2,1)S(1)} %bitcast.24), channel_id=1, source_target_pairs={{0,8},{8,16},{16,24},{24,0},{1,9},{9,17},{17,25},{25,1},{2,10},{10... | collective-permute-start | bytes 393224 | tf_op jit(solution)/shard_map/ppermute | solution.py:641
  21.3 0.9 add_select_fusion
  22.2 0.3 reduce_window_max.16
  22.5 0.1 slice.28
  22.6 0.1 reduce-window.4
  22.7 0.1 slice_reduce_fusion
  22.8 0.1 pad_add_fusion
  22.9 0.1 slice.31
  22.9 0.1 slice_maximum_fusion
  23.0 0.1 rev.3
  23.1 0.0 copy-start.13
  23.1 0.0 copy-done.21
  23.1 1.3 %copy.17 = bf16[3584,128]{1,0:T(8,128)(2,1)} copy(bf16[3584,128]{0,1:T(8,128)(2,1)S(1)} %bitcast.35) | data formatting | bytes 1835008 | tf_op jit(solution)/shard_map/transpose | solution.py:648
  24.4 0.2 shift-right-arithmetic_reduce_fusion
  24.6 0.7 concatenate.14.refs_3_.num_ref.num_any
  25.2 13.2 %collective-permute-done.2.refs_7_.b3_ref = bf16[4,128,128]{2,1,0:T(8,128)(2,1)S(1)} collective-permute-done((bf16[4,128,128]{2,1,0:T(8,128)(2,1)S(1)}, bf16[4,128,128]{2,1,0:T(8,128)(2,1)S(1)}, u32[]{:S(2)}, u32[]{:S(2)}) %collective-permute-start.2) | collective-permute-done | bytes 131104 | tf_op jit(solution)/shard_map/ppermute | solution.py:641
  38.4 0.0 collective-permute-done.1.refs_6_.b2_ref
  38.4 2.8 %collective-permute-done.refs_5_.b1_ref = bf16[4,128,128]{2,1,0:T(8,128)(2,1)S(1)} collective-permute-done((bf16[4,128,128]{2,1,0:T(8,128)(2,1)S(1)}, bf16[4,128,128]{2,1,0:T(8,128)(2,1)S(1)}, u32[]{:S(2)}, u32[]{:S(2)}) %collective-permute-start) | collective-permute-done | bytes 131104 | tf_op jit(solution)/shard_map/ppermute | solution.py:641
  41.3 0.0 all-to-all-done.refs_0_
  41.3 0.0 copy-done.2
  41.3 0.0 copy-done.13
  41.3 0.0 copy-done.7
  41.3 0.0 copy-done.9
  41.3 0.6 copy-done.11
  41.9 2.0 %collective-permute-start.3 = (bf16[16,496,128]{2,1,0:T(8,128)(2,1)S(1)}, bf16[16,496,128]{2,1,0:T(8,128)(2,1)}, u32[]{:S(2)}, u32[]{:S(2)}) collective-permute-start(bf16[16,496,128]{2,1,0:T(8,128)(2,1)S(1)} %get-tuple-element.18.own_ref.first_ref), channel_id=1, source_target_pairs={{0,1},{1,0},{2,3},{3,2},{4,5},{5,4},{6,7},{7,6},{8,9},{9,8},{10,11... | collective-permute-start | bytes 6094856 | tf_op jit(solution)/shard_map/ppermute | solution.py:613
  43.9 5.0 %all-to-all-start.1 = ((bf16[16,224,128]{2,1,0:T(8,128)(2,1)}), bf16[16,224,128]{2,1,0:T(8,128)(2,1)}, u32[]{:S(2)}, u32[]{:S(2)}) async-start(bf16[16,224,128]{2,1,0:T(8,128)(2,1)} %get-tuple-element.20), calls=%async_computation.1 | async-start | bytes 1835008 | tf_op jit(solution)/shard_map/all_to_all | solution.py:617
  49.0 0.0 copy-start.3
  49.0 0.0 copy-start.8
  49.0 0.0 copy-start.10
  49.0 0.0 collective-permute-done.3.other_ref.before_ref
  49.1 0.1 cut_halo.1
  49.1 3.1 %collective-permute-start.4 = (bf16[8,480,128]{2,1,0:T(8,128)(2,1)S(1)}, bf16[8,480,128]{2,1,0:T(8,128)(2,1)}, u32[]{:S(2)}, u32[]{:S(2)}) collective-permute-start(bf16[8,480,128]{2,1,0:T(8,128)(2,1)S(1)} %cut_halo.1), channel_id=1, source_target_pairs={{0,32},{32,64},{64,96},{96,128},{128,160},{160,192},{192,224},{224... | collective-permute-start | bytes 2949128 | tf_op jit(solution)/shard_map/ppermute | solution.py:653
  52.3 4.8 %scan_weights.1 = (bf16[16,4,128,128]{3,2,1,0:T(8,128)(2,1)S(1)}, f32[16,8,128]{2,1,0:T(8,128)S(1)}, f32[16,128]{1,0:T(8,128)S(1)}, bf16[16,128,128]{2,1,0:T(8,128)(2,1)S(1)}) custom-call(s32[8]{0:T(128)S(1)} %copy-done.19, bf16[16,496,128]{2,1,0:T(8,128)(2,1)S(1)} %get-tuple-element.18.own_ref.first_ref, ...), custom_call_target="tpu_custom_call" | custom-call | flops 200000000 | bytes 8000000 | tf_op jit(solution)/shard_map/scan_weights/pallas_call | solution.py:246
  57.1 1.3 %copy-done = bf16[16,4,128,128]{3,2,1,0:T(8,128)(2,1)} copy-done((bf16[16,4,128,128]{3,2,1,0:T(8,128)(2,1)}, bf16[16,4,128,128]{3,2,1,0:T(8,128)(2,1)S(1)}, u32[]{:S(2)}) %copy-start) | copy-done | bytes 2097176
  58.4 0.8 copy-done.4
  59.2 0.6 copy-done.17
  59.8 1.1 scan_keeps.1.keep_any.keep_ref
  61.0 0.6 copy-done.15
  61.6 4.2 %all-to-all-done.1.q_ref = bf16[16,224,128]{2,1,0:T(8,128)(2,1)} async-done(((bf16[16,224,128]{2,1,0:T(8,128)(2,1)}), bf16[16,224,128]{2,1,0:T(8,128)(2,1)}, u32[]{:S(2)}, u32[]{:S(2)}) %all-to-all-start.1) | async-done | bytes 917536 | tf_op jit(solution)/shard_map/all_to_all | solution.py:617
  65.7 10.6 %attend_near.1 = (bf16[8,256,128]{2,1,0:T(8,128)(2,1)}, bf16[4,256,128]{2,1,0:T(8,128)(2,1)}, bf16[128,128]{1,0:T(8,128)(2,1)S(1)}, f32[2,224,512]{2,1,0:T(8,128)}, f32[2,8,512]{2,1,0:T(8,128)}) custom-call(s32[8]{0:T(128)} %concatenate.14.refs_3_.num_ref.num_any, bf16[16,224,128]{2,1,0:T(8,128)(2,1)} %all-to-all-done.1.q_ref, ...), custom_call_target="tpu_custom_call" | custom-call | flops 5000000000 | bytes 9000000 | tf_op jit(solution)/shard_map/attend_near/pallas_call | solution.py:456
  76.4 0.0 collective-permute-done.4.refs_0_
  76.4 1.9 %collective-permute-start.5 = (bf16[8,480,128]{2,1,0:T(8,128)(2,1)}, bf16[8,480,128]{2,1,0:T(8,128)(2,1)S(1)}, u32[]{:S(2)}, u32[]{:S(2)}) collective-permute-start(bf16[8,480,128]{2,1,0:T(8,128)(2,1)} %gate.1.own_ref), channel_id=1, source_target_pairs={{0,1},{1,0},{2,3},{3,2},{4,5},{5,4},{6,7},{7,6},{8,9},{9,8},{10,11... | collective-permute-start | bytes 2949128 | tf_op jit(solution)/shard_map/ppermute | solution.py:613
  78.3 3.9 %collective-permute-start.6 = (bf16[128,128]{1,0:T(8,128)(2,1)S(1)}, bf16[128,128]{1,0:T(8,128)(2,1)S(1)}, u32[]{:S(2)}, u32[]{:S(2)}) collective-permute-start(bf16[128,128]{1,0:T(8,128)(2,1)S(1)} %get-tuple-element.24), channel_id=1, source_target_pairs={{0,32},{32,64},{64,96},{96,128},{128,160},{160,192},{192,224},{224... | collective-permute-start | bytes 98312 | tf_op jit(solution)/shard_map/ppermute | solution.py:658
  82.3 3.1 %collective-permute-done.6.came_ref = bf16[128,128]{1,0:T(8,128)(2,1)S(1)} collective-permute-done((bf16[128,128]{1,0:T(8,128)(2,1)S(1)}, bf16[128,128]{1,0:T(8,128)(2,1)S(1)}, u32[]{:S(2)}, u32[]{:S(2)}) %collective-permute-start.6) | collective-permute-done | bytes 32800 | tf_op jit(solution)/shard_map/ppermute | solution.py:658
  85.3 0.0 collective-permute-done.5.other_ref
  85.4 5.0 %attend_far.1 = (bf16[8,256,128]{2,1,0:T(8,128)(2,1)S(1)}, bf16[9,256,128]{2,1,0:T(8,128)(2,1)S(1)}) custom-call(s32[8]{0:T(128)} %concatenate.14.refs_3_.num_ref.num_any, bf16[16,224,128]{2,1,0:T(8,128)(2,1)} %all-to-all-done.1.q_ref, bf16[8,480,128]{2,1,0:T(8,128)(2,1)} %gate.1.own_ref, bf16[8,480,128]{2,1,0:T(8,128)(2,1)S(1)} %collective-permute-done.5.other_ref, ...), custom_call_target="tpu_custom_call" | custom-call | flops 2000000000 | bytes 5000000 | tf_op jit(solution)/shard_map/attend_far/pallas_call | solution.py:529
  90.4 1.9 %collective-permute-start.7 = (bf16[9,256,128]{2,1,0:T(8,128)(2,1)S(1)}, bf16[9,256,128]{2,1,0:T(8,128)(2,1)S(1)}, u32[]{:S(2)}, u32[]{:S(2)}) collective-permute-start(bf16[9,256,128]{2,1,0:T(8,128)(2,1)S(1)} %get-tuple-element.30.own_ref.f_ref), channel_id=1, source_target_pairs={{0,1},{1,0},{2,3},{3,2},{4,5},{5,4},{6,7},{7,6},{8,9},{9,8},{10,11... | collective-permute-start | bytes 1769480 | tf_op jit(solution)/shard_map/ppermute | solution.py:613
  92.3 2.0 %collective-permute-done.7.other_ref.g_ref = bf16[9,256,128]{2,1,0:T(8,128)(2,1)S(1)} collective-permute-done((bf16[9,256,128]{2,1,0:T(8,128)(2,1)S(1)}, bf16[9,256,128]{2,1,0:T(8,128)(2,1)S(1)}, u32[]{:S(2)}, u32[]{:S(2)}) %collective-permute-start.7) | collective-permute-done | bytes 589856 | tf_op jit(solution)/shard_map/ppermute | solution.py:613
  94.3 0.0 copy-done.5
  94.3 2.6 %scan.1 = bf16[16,224,128]{2,1,0:T(8,128)(2,1)S(1)} custom-call(s32[8]{0:T(128)S(1)} %copy-done.20, f32[16,128]{1,0:T(8,128)S(1)} %get-tuple-element.19.par_ref, bf16[8,256,128]{2,1,0:T(8,128)(2,1)S(1)} %get-tuple-element.27.xe_ref, bf16[8,256,128]{2,1,0:T(8,128)(2,1)S(1)} %copy-done.6, bf16[16,4,128,128]{3,2,1,0:T(8,128)(2,1)S(1)} %copy-done.1, ...), custom_call_target="tpu_custom_call" | custom-call | tf_op jit(solution)/shard_map/scan/pallas_call | solution.py:595
  96.9 22.7 %all_to_all.15 = bf16[16,224,128]{2,1,0:T(8,128)(2,1)S(1)} all-to-all(bf16[16,224,128]{2,1,0:T(8,128)(2,1)S(1)} %scan.1), channel_id=1, replica_groups=mesh['z'=16,'y'=4,'x'=4,'core'=2] {'y','x'}, dimensions={0} | all-to-all | bytes 1835008 | tf_op jit(solution)/shard_map/all_to_all | solution.py:617
  119.6 1.3 %copy.19 = bf16[3584,128]{0,1:T(8,128)(2,1)} copy(bf16[3584,128]{1,0:T(8,128)(2,1)S(1)} %bitcast.34) | data formatting | bytes 1835008 | tf_op jit(solution)/shard_map/reshape | solution.py:664
  (32 shorter events, 0.1 us)
Async XLA Ops:
  2.9 7.2 %copy-start.22 = (bf16[1024,64]{0,1:T(8,128)(2,1)S(1)}, bf16[1024,64]{0,1:T(8,128)(2,1)}, u32[]{:S(2)}) copy-start(bf16[1024,64]{0,1:T(8,128)(2,1)} %param.18) | copy-start | bytes 393220
  2.9 7.2 %copy-start.23 = (bf16[1024,64]{0,1:T(8,128)(2,1)S(1)}, bf16[1024,64]{0,1:T(8,128)(2,1)}, u32[]{:S(2)}) copy-start(bf16[1024,64]{0,1:T(8,128)(2,1)} %param.17) | copy-start | bytes 393220
  2.9 38.3 %all-to-all-start = ((bf16[16,496,128]{2,1,0:T(8,128)(2,1)}), bf16[16,496,128]{2,1,0:T(8,128)(2,1)S(1)}, u32[]{:S(2)}, u32[]{:S(2)}) async-start(bf16[16,496,128]{2,1,0:T(8,128)(2,1)} %pack_keys_values.1), calls=%async_computation | async-start | bytes 4063232 | tf_op jit(solution)/shard_map/all_to_all | solution.py:617
  10.1 13.0 %copy-start.21 = (bf16[128,3584]{1,0:T(8,128)(2,1)S(1)}, bf16[128,3584]{1,0:T(8,128)(2,1)}, u32[]{:S(2)}) copy-start(bf16[128,3584]{1,0:T(8,128)(2,1)} %param.10) | copy-start | bytes 2752516
  10.7 30.6 %copy-start.2 = (bf16[128,4,1,128]{3,0,1,2:T(8,128)(2,1)}, bf16[128,4,1,128]{3,0,1,2:T(8,128)(2,1)S(1)}, u32[]{:S(2)}) copy-start(bf16[128,4,1,128]{3,0,1,2:T(8,128)(2,1)S(1)} %copy.22) | copy-start | bytes 393220
  10.7 27.7 %collective-permute-start.2 = (bf16[4,128,128]{2,1,0:T(8,128)(2,1)S(1)}, bf16[4,128,128]{2,1,0:T(8,128)(2,1)S(1)}, u32[]{:S(2)}, u32[]{:S(2)}) collective-permute-start(bf16[4,128,128]{2,1,0:T(8,128)(2,1)S(1)} %bitcast.22), channel_id=1, source_target_pairs={{0,24},{8,0},{16,8},{24,16},{1,25},{9,1},{17,9},{25,17},{2,26},{10... | collective-permute-start | bytes 393224 | tf_op jit(solution)/shard_map/ppermute | solution.py:641
  15.7 22.7 %collective-permute-start.1 = (bf16[4,128,128]{2,1,0:T(8,128)(2,1)S(1)}, bf16[4,128,128]{2,1,0:T(8,128)(2,1)S(1)}, u32[]{:S(2)}, u32[]{:S(2)}) collective-permute-start(bf16[4,128,128]{2,1,0:T(8,128)(2,1)S(1)} %bitcast.23), channel_id=1, source_target_pairs={{0,16},{8,24},{16,0},{24,8},{1,17},{9,25},{17,1},{25,9},{2,18},{10... | collective-permute-start | bytes 393224 | tf_op jit(solution)/shard_map/ppermute | solution.py:641
  18.5 22.7 %collective-permute-start = (bf16[4,128,128]{2,1,0:T(8,128)(2,1)S(1)}, bf16[4,128,128]{2,1,0:T(8,128)(2,1)S(1)}, u32[]{:S(2)}, u32[]{:S(2)}) collective-permute-start(bf16[4,128,128]{2,1,0:T(8,128)(2,1)S(1)} %bitcast.24), channel_id=1, source_target_pairs={{0,8},{8,16},{16,24},{24,0},{1,9},{9,17},{17,25},{25,1},{2,10},{10... | collective-permute-start | bytes 393224 | tf_op jit(solution)/shard_map/ppermute | solution.py:641
  23.1 18.2 %copy-start.13 = (s32[4,8,128]{2,1,0:T(8,128)}, s32[4,8,128]{2,1,0:T(8,128)S(1)}, u32[]{:S(2)}) copy-start(s32[4,8,128]{2,1,0:T(8,128)S(1)} %broadcast_select_fusion) | copy-start | bytes 49156
  38.4 2.9 %copy-start.7 = (bf16[4,128,128]{2,1,0:T(8,128)(2,1)}, bf16[4,128,128]{2,1,0:T(8,128)(2,1)S(1)}, u32[]{:S(2)}) copy-start(bf16[4,128,128]{2,1,0:T(8,128)(2,1)S(1)} %collective-permute-done.2.refs_7_.b3_ref) | copy-start | bytes 393220
  38.4 2.9 %copy-start.9 = (bf16[4,128,128]{2,1,0:T(8,128)(2,1)}, bf16[4,128,128]{2,1,0:T(8,128)(2,1)S(1)}, u32[]{:S(2)}) copy-start(bf16[4,128,128]{2,1,0:T(8,128)(2,1)S(1)} %collective-permute-done.1.refs_6_.b2_ref) | copy-start | bytes 393220
  41.3 0.7 copy-start.11
  41.9 7.1 %collective-permute-start.3 = (bf16[16,496,128]{2,1,0:T(8,128)(2,1)S(1)}, bf16[16,496,128]{2,1,0:T(8,128)(2,1)}, u32[]{:S(2)}, u32[]{:S(2)}) collective-permute-start(bf16[16,496,128]{2,1,0:T(8,128)(2,1)S(1)} %get-tuple-element.18.own_ref.first_ref), channel_id=1, source_target_pairs={{0,1},{1,0},{2,3},{3,2},{4,5},{5,4},{6,7},{7,6},{8,9},{9,8},{10,11... | collective-permute-start | bytes 6094856 | tf_op jit(solution)/shard_map/ppermute | solution.py:613
  43.9 21.8 %all-to-all-start.1 = ((bf16[16,224,128]{2,1,0:T(8,128)(2,1)}), bf16[16,224,128]{2,1,0:T(8,128)(2,1)}, u32[]{:S(2)}, u32[]{:S(2)}) async-start(bf16[16,224,128]{2,1,0:T(8,128)(2,1)} %get-tuple-element.20), calls=%async_computation.1 | async-start | bytes 1835008 | tf_op jit(solution)/shard_map/all_to_all | solution.py:617
  49.0 3.2 %copy-start.3 = (bf16[128,4,1,128]{3,0,1,2:T(8,128)(2,1)S(1)}, bf16[128,4,1,128]{3,0,1,2:T(8,128)(2,1)}, u32[]{:S(2)}) copy-start(bf16[128,4,1,128]{3,0,1,2:T(8,128)(2,1)} %copy-done.2) | copy-start | bytes 393220
  49.0 3.2 %copy-start.8 = (bf16[4,128,128]{2,1,0:T(8,128)(2,1)S(1)}, bf16[4,128,128]{2,1,0:T(8,128)(2,1)}, u32[]{:S(2)}) copy-start(bf16[4,128,128]{2,1,0:T(8,128)(2,1)} %copy-done.7) | copy-start | bytes 393220
  49.0 3.2 %copy-start.10 = (bf16[4,128,128]{2,1,0:T(8,128)(2,1)S(1)}, bf16[4,128,128]{2,1,0:T(8,128)(2,1)}, u32[]{:S(2)}) copy-start(bf16[4,128,128]{2,1,0:T(8,128)(2,1)} %copy-done.9) | copy-start | bytes 393220
  49.0 3.2 %copy-start.12 = (bf16[4,128,128]{2,1,0:T(8,128)(2,1)S(1)}, bf16[4,128,128]{2,1,0:T(8,128)(2,1)}, u32[]{:S(2)}) copy-start(bf16[4,128,128]{2,1,0:T(8,128)(2,1)} %copy-done.11) | copy-start | bytes 393220
  49.0 3.2 %copy-start.14 = (s32[4,8,128]{2,1,0:T(8,128)S(1)}, s32[4,8,128]{2,1,0:T(8,128)}, u32[]{:S(2)}) copy-start(s32[4,8,128]{2,1,0:T(8,128)} %copy-done.13) | copy-start | bytes 49156
  49.0 3.2 %copy-start.19 = (s32[8]{0:T(128)S(1)}, s32[8]{0:T(128)}, u32[]{:S(2)}) copy-start(s32[8]{0:T(128)} %concatenate.14.refs_3_.num_ref.num_any) | copy-start | bytes 100
  49.1 27.2 %collective-permute-start.4 = (bf16[8,480,128]{2,1,0:T(8,128)(2,1)S(1)}, bf16[8,480,128]{2,1,0:T(8,128)(2,1)}, u32[]{:S(2)}, u32[]{:S(2)}) collective-permute-start(bf16[8,480,128]{2,1,0:T(8,128)(2,1)S(1)} %cut_halo.1), channel_id=1, source_target_pairs={{0,32},{32,64},{64,96},{96,128},{128,160},{160,192},{192,224},{224... | collective-permute-start | bytes 2949128 | tf_op jit(solution)/shard_map/ppermute | solution.py:653
  57.0 1.3 %copy-start = (bf16[16,4,128,128]{3,2,1,0:T(8,128)(2,1)}, bf16[16,4,128,128]{3,2,1,0:T(8,128)(2,1)S(1)}, u32[]{:S(2)}) copy-start(bf16[16,4,128,128]{3,2,1,0:T(8,128)(2,1)S(1)} %get-tuple-element.29.inner_ref) | copy-start | bytes 6291460
  58.4 0.8 copy-start.4
  59.2 0.6 copy-start.17
  60.9 0.6 copy-start.15
  76.4 8.9 %collective-permute-start.5 = (bf16[8,480,128]{2,1,0:T(8,128)(2,1)}, bf16[8,480,128]{2,1,0:T(8,128)(2,1)S(1)}, u32[]{:S(2)}, u32[]{:S(2)}) collective-permute-start(bf16[8,480,128]{2,1,0:T(8,128)(2,1)} %gate.1.own_ref), channel_id=1, source_target_pairs={{0,1},{1,0},{2,3},{3,2},{4,5},{5,4},{6,7},{7,6},{8,9},{9,8},{10,11... | collective-permute-start | bytes 2949128 | tf_op jit(solution)/shard_map/ppermute | solution.py:613
  78.3 7.0 %collective-permute-start.6 = (bf16[128,128]{1,0:T(8,128)(2,1)S(1)}, bf16[128,128]{1,0:T(8,128)(2,1)S(1)}, u32[]{:S(2)}, u32[]{:S(2)}) collective-permute-start(bf16[128,128]{1,0:T(8,128)(2,1)S(1)} %get-tuple-element.24), channel_id=1, source_target_pairs={{0,32},{32,64},{64,96},{96,128},{128,160},{160,192},{192,224},{224... | collective-permute-start | bytes 98312 | tf_op jit(solution)/shard_map/ppermute | solution.py:658
  85.3 8.9 %copy-start.1 = (bf16[16,4,128,128]{3,2,1,0:T(8,128)(2,1)S(1)}, bf16[16,4,128,128]{3,2,1,0:T(8,128)(2,1)}, u32[]{:S(2)}) copy-start(bf16[16,4,128,128]{3,2,1,0:T(8,128)(2,1)} %copy-done) | copy-start | bytes 6291460
  85.3 8.9 %copy-start.5 = (bf16[16,128,128]{2,1,0:T(8,128)(2,1)S(1)}, bf16[16,128,128]{2,1,0:T(8,128)(2,1)}, u32[]{:S(2)}) copy-start(bf16[16,128,128]{2,1,0:T(8,128)(2,1)} %copy-done.4) | copy-start | bytes 1572868
  85.3 8.9 %copy-start.6 = (bf16[8,256,128]{2,1,0:T(8,128)(2,1)S(1)}, bf16[8,256,128]{2,1,0:T(8,128)(2,1)}, u32[]{:S(2)}) copy-start(bf16[8,256,128]{2,1,0:T(8,128)(2,1)} %get-tuple-element.28.xl_ref) | copy-start | bytes 1572868
  85.3 8.9 %copy-start.16 = (f32[16,8,128]{2,1,0:T(8,128)S(1)}, f32[16,8,128]{2,1,0:T(8,128)}, u32[]{:S(2)}) copy-start(f32[16,8,128]{2,1,0:T(8,128)} %copy-done.15) | copy-start | bytes 196612
  85.4 8.9 %copy-start.18 = (f32[16,8,128]{2,1,0:T(8,128)S(1)}, f32[16,8,128]{2,1,0:T(8,128)}, u32[]{:S(2)}) copy-start(f32[16,8,128]{2,1,0:T(8,128)} %copy-done.17) | copy-start | bytes 196612
  85.4 8.9 %copy-start.20 = (s32[8]{0:T(128)S(1)}, s32[8]{0:T(128)}, u32[]{:S(2)}) copy-start(s32[8]{0:T(128)} %concatenate.14.refs_3_.num_ref.num_any) | copy-start | bytes 100
  90.4 3.9 %collective-permute-start.7 = (bf16[9,256,128]{2,1,0:T(8,128)(2,1)S(1)}, bf16[9,256,128]{2,1,0:T(8,128)(2,1)S(1)}, u32[]{:S(2)}, u32[]{:S(2)}) collective-permute-start(bf16[9,256,128]{2,1,0:T(8,128)(2,1)S(1)} %get-tuple-element.30.own_ref.f_ref), channel_id=1, source_target_pairs={{0,1},{1,0},{2,3},{3,2},{4,5},{5,4},{6,7},{7,6},{8,9},{9,8},{10,11... | collective-permute-start | bytes 1769480 | tf_op jit(solution)/shard_map/ppermute | solution.py:613

commit v4 on v3

--- a/solution.py
+++ b/solution.py
@@ -318,11 +318,11 @@
         )
         s[:, lanes] = jnp.dot(k, self.turned[:, lanes], preferred_element_type=f32)
 
-    def absorb(self, p, s, acc_ref, stat_ref, lanes=slice(0, 512), causal=False, valid=True):
+    def absorb(self, p, s, acc_ref, stat_ref, lanes=slice(0, 512), causal=False):
         width = lanes.stop - lanes.start
         scale = LOG2E / math.sqrt(HEAD_DIM)
         line = iota((ROWS, width), 0)
-        ids = jnp.where(valid, self.ids[:, lanes], 1 << 20)
+        ids = self.ids[:, lanes]
         pieces = []
         for j in range(4):
             at = 512 * p + self.shift + 256 * (j // 2) + 128 * (self.core if j % 2 == 0 else 1 - self.core)
@@ -343,13 +343,18 @@
     def back(self, p, low, acc_ref, stat_ref):
         def two(n, carry):
             at = p - 2 * n
-            self.score(jnp.maximum(at - 1, 0), self.odd)
+            self.score(at - 1, self.odd)
             self.absorb(at, self.even, acc_ref, stat_ref)
             self.score(jnp.maximum(at - 2, 0), self.even)
-            self.absorb(jnp.maximum(at - 1, 0), self.odd, acc_ref, stat_ref, valid=at - 1 >= low)
+            self.absorb(at - 1, self.odd, acc_ref, stat_ref)
             return carry
 
-        lax.fori_loop(0, jnp.maximum(p - low + 2, 0) >> 1, two, 0)
+        count = jnp.maximum(p - low + 1, 0)
+        lax.fori_loop(0, count >> 1, two, 0)
+
+        @pl.when((count & 1) == 1)
+        def _():
+            self.absorb(low, self.even, acc_ref, stat_ref)
 
 
 def own_states(x_ref, rows_ref, keep_ref, maps_ref, send_ref, core):

time: 122 us -> 122 us (level)
  waiting for transfers between devices: 25.2 us -> 28.2 us
  starting transfers between devices: 35.6 us -> 33.7 us
    ppermute x1, waiting for transfers between devices: 3.06 us -> 5.01 us  [on_device(): came = lax.ppermute(left, 'z', following)]
    ppermute x1, starting transfers between devices: 3.95 us -> 2 us  [on_device(): came = lax.ppermute(left, 'z', following)]
  transfers between devices with their start and end apart: 10 -> 10, of which waited for: 5 -> 6; matrix products, arithmetic and copies ran while one was open for 4% -> 4% of each run, Pallas kernels for 14% -> 13%
where the time goes in v4:
time: 122 us; the launch traced here: 121 us
  starting transfers between devices  33.7 us (28%)
  waiting for transfers between devices  28.2 us (23%)
  Pallas kernels  26.4 us (22%)
  blocking collectives  22.7 us (19%)
  local copies, waits for them, and re-layouts  8.08 us (7%)
  other arithmetic  1.63 us (1%)
    all_to_all x1, blocking collectives, exchange(): lax.all_to_all(x, ('y', 'x'), split_axis=0, concat_axis=0, tiled=True)  22.7 us
    ppermute x3, waiting for transfers between devices, on_device(): lax.ppermute(both, 'y', [(i, (i + d) % 4) for i in range(4)])  16 us
    all_to_all x2, starting transfers between devices, exchange(): lax.all_to_all(x, ('y', 'x'), split_axis=0, concat_axis=0, tiled=True)  12.2 us
    ppermute x3, starting transfers between devices, on_device(): lax.ppermute(both, 'y', [(i, (i + d) % 4) for i in range(4)])  10.6 us
    pallas_call x1, Pallas kernels, attend_near(): pl.pallas_call(near_kernel, in_specs=[HBM] + [VMEM] * 4 + [HBM] * 3, out_...  9.61 us
    ppermute x3, starting transfers between devices, other_core(): return lax.ppermute(x, 'core', [(0, 1), (1, 0)])  5.84 us
    pallas_call x1, Pallas kernels, attend_far(): pl.pallas_call(far_kernel, in_specs=[HBM] + [VMEM] * 5 + [HBM] * 6, out_s...  5.31 us
    ppermute x1, waiting for transfers between devices, on_device(): came = lax.ppermute(left, 'z', following)  5.01 us
  transfers between devices with their start and end apart: 10, of which 6 were waited for; matrix products, arithmetic and copies ran while one was open for 4% of the time, Pallas kernels for 13%

profile of v4, /device:TPU:256, one launch (start us, length us, event | category | flops | bytes accessed | tf_op | source)
XLA Modules:
  0.0 121.2 jit_solution(16554493679123161406)
XLA Ops:
  0.0 2.9 %pack_keys_values.1 = bf16[16,496,128]{2,1,0:T(8,128)(2,1)} custom-call(f32[7]{0:T(128)} %bias_any.1, f32[7]{0:T(128)} %decay_any.1, f32[7]{0:T(128)} %skip_any.1, bf16[128,3584]{1,0:T(8,128)(2,1)} %k_any.1, bf16[128,3584]{1,0:T(8,128)(2,1)} %v_any.1, bf16[56,128]{1,0:T(8,128)(2,1)} %bitcast.41), custom_call_target="tpu_custom_call" | custom-call | tf_op jit(solution)/shard_map/pack_keys_values/pallas_call | solution.py:110
  2.9 0.0 copy-start.22
  2.9 0.0 copy-start.23
  2.9 7.2 %all-to-all-start = ((bf16[16,496,128]{2,1,0:T(8,128)(2,1)}), bf16[16,496,128]{2,1,0:T(8,128)(2,1)S(1)}, u32[]{:S(2)}, u32[]{:S(2)}) async-start(bf16[16,496,128]{2,1,0:T(8,128)(2,1)} %pack_keys_values.1), calls=%async_computation | async-start | bytes 4063232 | tf_op jit(solution)/shard_map/all_to_all | solution.py:622
  10.1 0.0 copy-start.21
  10.1 0.0 copy-done.22
  10.1 0.0 copy-done.23
  10.2 0.2 reshape.26
  10.4 0.3 constant_dynamic-slice_fusion
  10.7 0.0 copy-start.2
  10.7 5.0 %collective-permute-start.2 = (bf16[4,128,128]{2,1,0:T(8,128)(2,1)S(1)}, bf16[4,128,128]{2,1,0:T(8,128)(2,1)S(1)}, u32[]{:S(2)}, u32[]{:S(2)}) collective-permute-start(bf16[4,128,128]{2,1,0:T(8,128)(2,1)S(1)} %bitcast.22), channel_id=1, source_target_pairs={{0,24},{8,0},{16,8},{24,16},{1,25},{9,1},{17,9},{25,17},{2,26},{10... | collective-permute-start | bytes 393224 | tf_op jit(solution)/shard_map/ppermute | solution.py:646
  15.7 2.8 %collective-permute-start.1 = (bf16[4,128,128]{2,1,0:T(8,128)(2,1)S(1)}, bf16[4,128,128]{2,1,0:T(8,128)(2,1)S(1)}, u32[]{:S(2)}, u32[]{:S(2)}) collective-permute-start(bf16[4,128,128]{2,1,0:T(8,128)(2,1)S(1)} %bitcast.23), channel_id=1, source_target_pairs={{0,16},{8,24},{16,0},{24,8},{1,17},{9,25},{17,1},{25,9},{2,18},{10... | collective-permute-start | bytes 393224 | tf_op jit(solution)/shard_map/ppermute | solution.py:646
  18.5 2.8 %collective-permute-start = (bf16[4,128,128]{2,1,0:T(8,128)(2,1)S(1)}, bf16[4,128,128]{2,1,0:T(8,128)(2,1)S(1)}, u32[]{:S(2)}, u32[]{:S(2)}) collective-permute-start(bf16[4,128,128]{2,1,0:T(8,128)(2,1)S(1)} %bitcast.24), channel_id=1, source_target_pairs={{0,8},{8,16},{16,24},{24,0},{1,9},{9,17},{17,25},{25,1},{2,10},{10... | collective-permute-start | bytes 393224 | tf_op jit(solution)/shard_map/ppermute | solution.py:646
  21.3 0.9 add_select_fusion
  22.2 0.3 reduce_window_max.16
  22.5 0.1 slice.28
  22.6 0.1 reduce-window.4
  22.7 0.1 slice_reduce_fusion
  22.8 0.1 pad_add_fusion
  22.9 0.1 slice.31
  22.9 0.1 slice_maximum_fusion
  23.0 0.1 rev.3
  23.1 0.0 copy-start.13
  23.1 0.0 copy-done.21
  23.1 1.3 %copy.17 = bf16[3584,128]{1,0:T(8,128)(2,1)} copy(bf16[3584,128]{0,1:T(8,128)(2,1)S(1)} %bitcast.35) | data formatting | bytes 1835008 | tf_op jit(solution)/shard_map/transpose | solution.py:653
  24.4 0.2 shift-right-arithmetic_reduce_fusion
  24.6 0.7 concatenate.14.refs_3_.num_ref.num_any
  25.2 13.2 %collective-permute-done.2.refs_7_.b3_ref = bf16[4,128,128]{2,1,0:T(8,128)(2,1)S(1)} collective-permute-done((bf16[4,128,128]{2,1,0:T(8,128)(2,1)S(1)}, bf16[4,128,128]{2,1,0:T(8,128)(2,1)S(1)}, u32[]{:S(2)}, u32[]{:S(2)}) %collective-permute-start.2) | collective-permute-done | bytes 131104 | tf_op jit(solution)/shard_map/ppermute | solution.py:646
  38.4 0.0 collective-permute-done.1.refs_6_.b2_ref
  38.4 2.8 %collective-permute-done.refs_5_.b1_ref = bf16[4,128,128]{2,1,0:T(8,128)(2,1)S(1)} collective-permute-done((bf16[4,128,128]{2,1,0:T(8,128)(2,1)S(1)}, bf16[4,128,128]{2,1,0:T(8,128)(2,1)S(1)}, u32[]{:S(2)}, u32[]{:S(2)}) %collective-permute-start) | collective-permute-done | bytes 131104 | tf_op jit(solution)/shard_map/ppermute | solution.py:646
  41.3 0.0 all-to-all-done.refs_0_
  41.3 0.0 copy-done.2
  41.3 0.0 copy-done.13
  41.3 0.0 copy-done.7
  41.3 0.0 copy-done.9
  41.3 0.6 copy-done.11
  41.9 2.0 %collective-permute-start.3 = (bf16[16,496,128]{2,1,0:T(8,128)(2,1)S(1)}, bf16[16,496,128]{2,1,0:T(8,128)(2,1)}, u32[]{:S(2)}, u32[]{:S(2)}) collective-permute-start(bf16[16,496,128]{2,1,0:T(8,128)(2,1)S(1)} %get-tuple-element.18.own_ref.first_ref), channel_id=1, source_target_pairs={{0,1},{1,0},{2,3},{3,2},{4,5},{5,4},{6,7},{7,6},{8,9},{9,8},{10,11... | collective-permute-start | bytes 6094856 | tf_op jit(solution)/shard_map/ppermute | solution.py:618
  43.9 5.0 %all-to-all-start.1 = ((bf16[16,224,128]{2,1,0:T(8,128)(2,1)}), bf16[16,224,128]{2,1,0:T(8,128)(2,1)}, u32[]{:S(2)}, u32[]{:S(2)}) async-start(bf16[16,224,128]{2,1,0:T(8,128)(2,1)} %get-tuple-element.20), calls=%async_computation.1 | async-start | bytes 1835008 | tf_op jit(solution)/shard_map/all_to_all | solution.py:622
  49.0 0.0 copy-start.3
  49.0 0.0 copy-start.8
  49.0 0.0 copy-start.10
  49.0 0.0 collective-permute-done.3.other_ref.before_ref
  49.1 0.1 cut_halo.1
  49.1 3.1 %collective-permute-start.4 = (bf16[8,480,128]{2,1,0:T(8,128)(2,1)S(1)}, bf16[8,480,128]{2,1,0:T(8,128)(2,1)}, u32[]{:S(2)}, u32[]{:S(2)}) collective-permute-start(bf16[8,480,128]{2,1,0:T(8,128)(2,1)S(1)} %cut_halo.1), channel_id=1, source_target_pairs={{0,32},{32,64},{64,96},{96,128},{128,160},{160,192},{192,224},{224... | collective-permute-start | bytes 2949128 | tf_op jit(solution)/shard_map/ppermute | solution.py:658
  52.3 4.8 %scan_weights.1 = (bf16[16,4,128,128]{3,2,1,0:T(8,128)(2,1)S(1)}, f32[16,8,128]{2,1,0:T(8,128)S(1)}, f32[16,128]{1,0:T(8,128)S(1)}, bf16[16,128,128]{2,1,0:T(8,128)(2,1)S(1)}) custom-call(s32[8]{0:T(128)S(1)} %copy-done.19, bf16[16,496,128]{2,1,0:T(8,128)(2,1)S(1)} %get-tuple-element.18.own_ref.first_ref, ...), custom_call_target="tpu_custom_call" | custom-call | flops 200000000 | bytes 8000000 | tf_op jit(solution)/shard_map/scan_weights/pallas_call | solution.py:246
  57.1 1.3 %copy-done = bf16[16,4,128,128]{3,2,1,0:T(8,128)(2,1)} copy-done((bf16[16,4,128,128]{3,2,1,0:T(8,128)(2,1)}, bf16[16,4,128,128]{3,2,1,0:T(8,128)(2,1)S(1)}, u32[]{:S(2)}) %copy-start) | copy-done | bytes 2097176
  58.4 0.8 copy-done.4
  59.2 0.6 copy-done.17
  59.8 1.1 scan_keeps.1.keep_any.keep_ref
  61.0 0.6 copy-done.15
  61.6 4.2 %all-to-all-done.1.q_ref = bf16[16,224,128]{2,1,0:T(8,128)(2,1)} async-done(((bf16[16,224,128]{2,1,0:T(8,128)(2,1)}), bf16[16,224,128]{2,1,0:T(8,128)(2,1)}, u32[]{:S(2)}, u32[]{:S(2)}) %all-to-all-start.1) | async-done | bytes 917536 | tf_op jit(solution)/shard_map/all_to_all | solution.py:622
  65.7 9.6 %attend_near.1 = (bf16[8,256,128]{2,1,0:T(8,128)(2,1)}, bf16[4,256,128]{2,1,0:T(8,128)(2,1)}, bf16[128,128]{1,0:T(8,128)(2,1)S(1)}, f32[2,224,512]{2,1,0:T(8,128)}, f32[2,8,512]{2,1,0:T(8,128)}) custom-call(s32[8]{0:T(128)} %concatenate.14.refs_3_.num_ref.num_any, bf16[16,224,128]{2,1,0:T(8,128)(2,1)} %all-to-all-done.1.q_ref, ...), custom_call_target="tpu_custom_call" | custom-call | flops 5000000000 | bytes 9000000 | tf_op jit(solution)/shard_map/attend_near/pallas_call | solution.py:461
  75.4 1.0 collective-permute-done.4.refs_0_
  76.3 1.9 %collective-permute-start.5 = (bf16[8,480,128]{2,1,0:T(8,128)(2,1)}, bf16[8,480,128]{2,1,0:T(8,128)(2,1)S(1)}, u32[]{:S(2)}, u32[]{:S(2)}) collective-permute-start(bf16[8,480,128]{2,1,0:T(8,128)(2,1)} %gate.1.own_ref), channel_id=1, source_target_pairs={{0,1},{1,0},{2,3},{3,2},{4,5},{5,4},{6,7},{7,6},{8,9},{9,8},{10,11... | collective-permute-start | bytes 2949128 | tf_op jit(solution)/shard_map/ppermute | solution.py:618
  78.3 2.0 %collective-permute-start.6 = (bf16[128,128]{1,0:T(8,128)(2,1)S(1)}, bf16[128,128]{1,0:T(8,128)(2,1)S(1)}, u32[]{:S(2)}, u32[]{:S(2)}) collective-permute-start(bf16[128,128]{1,0:T(8,128)(2,1)S(1)} %get-tuple-element.24), channel_id=1, source_target_pairs={{0,32},{32,64},{64,96},{96,128},{128,160},{160,192},{192,224},{224... | collective-permute-start | bytes 98312 | tf_op jit(solution)/shard_map/ppermute | solution.py:663
  80.3 5.0 %collective-permute-done.6.came_ref = bf16[128,128]{1,0:T(8,128)(2,1)S(1)} collective-permute-done((bf16[128,128]{1,0:T(8,128)(2,1)S(1)}, bf16[128,128]{1,0:T(8,128)(2,1)S(1)}, u32[]{:S(2)}, u32[]{:S(2)}) %collective-permute-start.6) | collective-permute-done | bytes 32800 | tf_op jit(solution)/shard_map/ppermute | solution.py:663
  85.3 0.0 collective-permute-done.5.other_ref
  85.3 5.3 %attend_far.1 = (bf16[8,256,128]{2,1,0:T(8,128)(2,1)S(1)}, bf16[9,256,128]{2,1,0:T(8,128)(2,1)S(1)}) custom-call(s32[8]{0:T(128)} %concatenate.14.refs_3_.num_ref.num_any, bf16[16,224,128]{2,1,0:T(8,128)(2,1)} %all-to-all-done.1.q_ref, bf16[8,480,128]{2,1,0:T(8,128)(2,1)} %gate.1.own_ref, bf16[8,480,128]{2,1,0:T(8,128)(2,1)S(1)} %collective-permute-done.5.other_ref, ...), custom_call_target="tpu_custom_call" | custom-call | flops 2000000000 | bytes 5000000 | tf_op jit(solution)/shard_map/attend_far/pallas_call | solution.py:534
  90.6 1.9 %collective-permute-start.7 = (bf16[9,256,128]{2,1,0:T(8,128)(2,1)S(1)}, bf16[9,256,128]{2,1,0:T(8,128)(2,1)S(1)}, u32[]{:S(2)}, u32[]{:S(2)}) collective-permute-start(bf16[9,256,128]{2,1,0:T(8,128)(2,1)S(1)} %get-tuple-element.30.own_ref.f_ref), channel_id=1, source_target_pairs={{0,1},{1,0},{2,3},{3,2},{4,5},{5,4},{6,7},{7,6},{8,9},{9,8},{10,11... | collective-permute-start | bytes 1769480 | tf_op jit(solution)/shard_map/ppermute | solution.py:618
  92.6 2.0 %collective-permute-done.7.other_ref.g_ref = bf16[9,256,128]{2,1,0:T(8,128)(2,1)S(1)} collective-permute-done((bf16[9,256,128]{2,1,0:T(8,128)(2,1)S(1)}, bf16[9,256,128]{2,1,0:T(8,128)(2,1)S(1)}, u32[]{:S(2)}, u32[]{:S(2)}) %collective-permute-start.7) | collective-permute-done | bytes 589856 | tf_op jit(solution)/shard_map/ppermute | solution.py:618
  94.5 0.0 copy-done.5
  94.6 2.6 %scan.1 = bf16[16,224,128]{2,1,0:T(8,128)(2,1)S(1)} custom-call(s32[8]{0:T(128)S(1)} %copy-done.20, f32[16,128]{1,0:T(8,128)S(1)} %get-tuple-element.19.par_ref, bf16[8,256,128]{2,1,0:T(8,128)(2,1)S(1)} %get-tuple-element.27.xe_ref, bf16[8,256,128]{2,1,0:T(8,128)(2,1)S(1)} %copy-done.6, bf16[16,4,128,128]{3,2,1,0:T(8,128)(2,1)S(1)} %copy-done.1, ...), custom_call_target="tpu_custom_call" | custom-call | tf_op jit(solution)/shard_map/scan/pallas_call | solution.py:600
  97.2 22.7 %all_to_all.15 = bf16[16,224,128]{2,1,0:T(8,128)(2,1)S(1)} all-to-all(bf16[16,224,128]{2,1,0:T(8,128)(2,1)S(1)} %scan.1), channel_id=1, replica_groups=mesh['z'=16,'y'=4,'x'=4,'core'=2] {'y','x'}, dimensions={0} | all-to-all | bytes 1835008 | tf_op jit(solution)/shard_map/all_to_all | solution.py:622
  119.9 1.3 %copy.19 = bf16[3584,128]{0,1:T(8,128)(2,1)} copy(bf16[3584,128]{1,0:T(8,128)(2,1)S(1)} %bitcast.34) | data formatting | bytes 1835008 | tf_op jit(solution)/shard_map/reshape | solution.py:669
  (32 shorter events, 0.1 us)
Async XLA Ops:
  2.9 7.2 %copy-start.22 = (bf16[1024,64]{0,1:T(8,128)(2,1)S(1)}, bf16[1024,64]{0,1:T(8,128)(2,1)}, u32[]{:S(2)}) copy-start(bf16[1024,64]{0,1:T(8,128)(2,1)} %param.18) | copy-start | bytes 393220
  2.9 7.2 %copy-start.23 = (bf16[1024,64]{0,1:T(8,128)(2,1)S(1)}, bf16[1024,64]{0,1:T(8,128)(2,1)}, u32[]{:S(2)}) copy-start(bf16[1024,64]{0,1:T(8,128)(2,1)} %param.17) | copy-start | bytes 393220
  2.9 38.3 %all-to-all-start = ((bf16[16,496,128]{2,1,0:T(8,128)(2,1)}), bf16[16,496,128]{2,1,0:T(8,128)(2,1)S(1)}, u32[]{:S(2)}, u32[]{:S(2)}) async-start(bf16[16,496,128]{2,1,0:T(8,128)(2,1)} %pack_keys_values.1), calls=%async_computation | async-start | bytes 4063232 | tf_op jit(solution)/shard_map/all_to_all | solution.py:622
  10.1 13.0 %copy-start.21 = (bf16[128,3584]{1,0:T(8,128)(2,1)S(1)}, bf16[128,3584]{1,0:T(8,128)(2,1)}, u32[]{:S(2)}) copy-start(bf16[128,3584]{1,0:T(8,128)(2,1)} %param.10) | copy-start | bytes 2752516
  10.7 30.6 %copy-start.2 = (bf16[128,4,1,128]{3,0,1,2:T(8,128)(2,1)}, bf16[128,4,1,128]{3,0,1,2:T(8,128)(2,1)S(1)}, u32[]{:S(2)}) copy-start(bf16[128,4,1,128]{3,0,1,2:T(8,128)(2,1)S(1)} %copy.22) | copy-start | bytes 393220
  10.7 27.7 %collective-permute-start.2 = (bf16[4,128,128]{2,1,0:T(8,128)(2,1)S(1)}, bf16[4,128,128]{2,1,0:T(8,128)(2,1)S(1)}, u32[]{:S(2)}, u32[]{:S(2)}) collective-permute-start(bf16[4,128,128]{2,1,0:T(8,128)(2,1)S(1)} %bitcast.22), channel_id=1, source_target_pairs={{0,24},{8,0},{16,8},{24,16},{1,25},{9,1},{17,9},{25,17},{2,26},{10... | collective-permute-start | bytes 393224 | tf_op jit(solution)/shard_map/ppermute | solution.py:646
  15.7 22.7 %collective-permute-start.1 = (bf16[4,128,128]{2,1,0:T(8,128)(2,1)S(1)}, bf16[4,128,128]{2,1,0:T(8,128)(2,1)S(1)}, u32[]{:S(2)}, u32[]{:S(2)}) collective-permute-start(bf16[4,128,128]{2,1,0:T(8,128)(2,1)S(1)} %bitcast.23), channel_id=1, source_target_pairs={{0,16},{8,24},{16,0},{24,8},{1,17},{9,25},{17,1},{25,9},{2,18},{10... | collective-permute-start | bytes 393224 | tf_op jit(solution)/shard_map/ppermute | solution.py:646
  18.5 22.7 %collective-permute-start = (bf16[4,128,128]{2,1,0:T(8,128)(2,1)S(1)}, bf16[4,128,128]{2,1,0:T(8,128)(2,1)S(1)}, u32[]{:S(2)}, u32[]{:S(2)}) collective-permute-start(bf16[4,128,128]{2,1,0:T(8,128)(2,1)S(1)} %bitcast.24), channel_id=1, source_target_pairs={{0,8},{8,16},{16,24},{24,0},{1,9},{9,17},{17,25},{25,1},{2,10},{10... | collective-permute-start | bytes 393224 | tf_op jit(solution)/shard_map/ppermute | solution.py:646
  23.1 18.2 %copy-start.13 = (s32[4,8,128]{2,1,0:T(8,128)}, s32[4,8,128]{2,1,0:T(8,128)S(1)}, u32[]{:S(2)}) copy-start(s32[4,8,128]{2,1,0:T(8,128)S(1)} %broadcast_select_fusion) | copy-start | bytes 49156
  38.4 2.9 %copy-start.7 = (bf16[4,128,128]{2,1,0:T(8,128)(2,1)}, bf16[4,128,128]{2,1,0:T(8,128)(2,1)S(1)}, u32[]{:S(2)}) copy-start(bf16[4,128,128]{2,1,0:T(8,128)(2,1)S(1)} %collective-permute-done.2.refs_7_.b3_ref) | copy-start | bytes 393220
  38.4 2.9 %copy-start.9 = (bf16[4,128,128]{2,1,0:T(8,128)(2,1)}, bf16[4,128,128]{2,1,0:T(8,128)(2,1)S(1)}, u32[]{:S(2)}) copy-start(bf16[4,128,128]{2,1,0:T(8,128)(2,1)S(1)} %collective-permute-done.1.refs_6_.b2_ref) | copy-start | bytes 393220
  41.3 0.7 copy-start.11
  41.9 7.1 %collective-permute-start.3 = (bf16[16,496,128]{2,1,0:T(8,128)(2,1)S(1)}, bf16[16,496,128]{2,1,0:T(8,128)(2,1)}, u32[]{:S(2)}, u32[]{:S(2)}) collective-permute-start(bf16[16,496,128]{2,1,0:T(8,128)(2,1)S(1)} %get-tuple-element.18.own_ref.first_ref), channel_id=1, source_target_pairs={{0,1},{1,0},{2,3},{3,2},{4,5},{5,4},{6,7},{7,6},{8,9},{9,8},{10,11... | collective-permute-start | bytes 6094856 | tf_op jit(solution)/shard_map/ppermute | solution.py:618
  43.9 21.8 %all-to-all-start.1 = ((bf16[16,224,128]{2,1,0:T(8,128)(2,1)}), bf16[16,224,128]{2,1,0:T(8,128)(2,1)}, u32[]{:S(2)}, u32[]{:S(2)}) async-start(bf16[16,224,128]{2,1,0:T(8,128)(2,1)} %get-tuple-element.20), calls=%async_computation.1 | async-start | bytes 1835008 | tf_op jit(solution)/shard_map/all_to_all | solution.py:622
  49.0 3.2 %copy-start.3 = (bf16[128,4,1,128]{3,0,1,2:T(8,128)(2,1)S(1)}, bf16[128,4,1,128]{3,0,1,2:T(8,128)(2,1)}, u32[]{:S(2)}) copy-start(bf16[128,4,1,128]{3,0,1,2:T(8,128)(2,1)} %copy-done.2) | copy-start | bytes 393220
  49.0 3.2 %copy-start.8 = (bf16[4,128,128]{2,1,0:T(8,128)(2,1)S(1)}, bf16[4,128,128]{2,1,0:T(8,128)(2,1)}, u32[]{:S(2)}) copy-start(bf16[4,128,128]{2,1,0:T(8,128)(2,1)} %copy-done.7) | copy-start | bytes 393220
  49.0 3.2 %copy-start.10 = (bf16[4,128,128]{2,1,0:T(8,128)(2,1)S(1)}, bf16[4,128,128]{2,1,0:T(8,128)(2,1)}, u32[]{:S(2)}) copy-start(bf16[4,128,128]{2,1,0:T(8,128)(2,1)} %copy-done.9) | copy-start | bytes 393220
  49.0 3.2 %copy-start.12 = (bf16[4,128,128]{2,1,0:T(8,128)(2,1)S(1)}, bf16[4,128,128]{2,1,0:T(8,128)(2,1)}, u32[]{:S(2)}) copy-start(bf16[4,128,128]{2,1,0:T(8,128)(2,1)} %copy-done.11) | copy-start | bytes 393220
  49.0 3.2 %copy-start.14 = (s32[4,8,128]{2,1,0:T(8,128)S(1)}, s32[4,8,128]{2,1,0:T(8,128)}, u32[]{:S(2)}) copy-start(s32[4,8,128]{2,1,0:T(8,128)} %copy-done.13) | copy-start | bytes 49156
  49.0 3.2 %copy-start.19 = (s32[8]{0:T(128)S(1)}, s32[8]{0:T(128)}, u32[]{:S(2)}) copy-start(s32[8]{0:T(128)} %concatenate.14.refs_3_.num_ref.num_any) | copy-start | bytes 100
  49.1 27.2 %collective-permute-start.4 = (bf16[8,480,128]{2,1,0:T(8,128)(2,1)S(1)}, bf16[8,480,128]{2,1,0:T(8,128)(2,1)}, u32[]{:S(2)}, u32[]{:S(2)}) collective-permute-start(bf16[8,480,128]{2,1,0:T(8,128)(2,1)S(1)} %cut_halo.1), channel_id=1, source_target_pairs={{0,32},{32,64},{64,96},{96,128},{128,160},{160,192},{192,224},{224... | collective-permute-start | bytes 2949128 | tf_op jit(solution)/shard_map/ppermute | solution.py:658
  57.0 1.3 %copy-start = (bf16[16,4,128,128]{3,2,1,0:T(8,128)(2,1)}, bf16[16,4,128,128]{3,2,1,0:T(8,128)(2,1)S(1)}, u32[]{:S(2)}) copy-start(bf16[16,4,128,128]{3,2,1,0:T(8,128)(2,1)S(1)} %get-tuple-element.29.inner_ref) | copy-start | bytes 6291460
  58.4 0.8 copy-start.4
  59.2 0.6 copy-start.17
  60.9 0.6 copy-start.15
  76.3 8.9 %collective-permute-start.5 = (bf16[8,480,128]{2,1,0:T(8,128)(2,1)}, bf16[8,480,128]{2,1,0:T(8,128)(2,1)S(1)}, u32[]{:S(2)}, u32[]{:S(2)}) collective-permute-start(bf16[8,480,128]{2,1,0:T(8,128)(2,1)} %gate.1.own_ref), channel_id=1, source_target_pairs={{0,1},{1,0},{2,3},{3,2},{4,5},{5,4},{6,7},{7,6},{8,9},{9,8},{10,11... | collective-permute-start | bytes 2949128 | tf_op jit(solution)/shard_map/ppermute | solution.py:618
  78.3 7.0 %collective-permute-start.6 = (bf16[128,128]{1,0:T(8,128)(2,1)S(1)}, bf16[128,128]{1,0:T(8,128)(2,1)S(1)}, u32[]{:S(2)}, u32[]{:S(2)}) collective-permute-start(bf16[128,128]{1,0:T(8,128)(2,1)S(1)} %get-tuple-element.24), channel_id=1, source_target_pairs={{0,32},{32,64},{64,96},{96,128},{128,160},{160,192},{192,224},{224... | collective-permute-start | bytes 98312 | tf_op jit(solution)/shard_map/ppermute | solution.py:663
  85.3 9.3 %copy-start.1 = (bf16[16,4,128,128]{3,2,1,0:T(8,128)(2,1)S(1)}, bf16[16,4,128,128]{3,2,1,0:T(8,128)(2,1)}, u32[]{:S(2)}) copy-start(bf16[16,4,128,128]{3,2,1,0:T(8,128)(2,1)} %copy-done) | copy-start | bytes 6291460
  85.3 9.3 %copy-start.5 = (bf16[16,128,128]{2,1,0:T(8,128)(2,1)S(1)}, bf16[16,128,128]{2,1,0:T(8,128)(2,1)}, u32[]{:S(2)}) copy-start(bf16[16,128,128]{2,1,0:T(8,128)(2,1)} %copy-done.4) | copy-start | bytes 1572868
  85.3 9.3 %copy-start.6 = (bf16[8,256,128]{2,1,0:T(8,128)(2,1)S(1)}, bf16[8,256,128]{2,1,0:T(8,128)(2,1)}, u32[]{:S(2)}) copy-start(bf16[8,256,128]{2,1,0:T(8,128)(2,1)} %get-tuple-element.28.xl_ref) | copy-start | bytes 1572868
  85.3 9.3 %copy-start.16 = (f32[16,8,128]{2,1,0:T(8,128)S(1)}, f32[16,8,128]{2,1,0:T(8,128)}, u32[]{:S(2)}) copy-start(f32[16,8,128]{2,1,0:T(8,128)} %copy-done.15) | copy-start | bytes 196612
  85.3 9.3 %copy-start.18 = (f32[16,8,128]{2,1,0:T(8,128)S(1)}, f32[16,8,128]{2,1,0:T(8,128)}, u32[]{:S(2)}) copy-start(f32[16,8,128]{2,1,0:T(8,128)} %copy-done.17) | copy-start | bytes 196612
  85.3 9.3 %copy-start.20 = (s32[8]{0:T(128)S(1)}, s32[8]{0:T(128)}, u32[]{:S(2)}) copy-start(s32[8]{0:T(128)} %concatenate.14.refs_3_.num_ref.num_any) | copy-start | bytes 100
  90.6 3.9 %collective-permute-start.7 = (bf16[9,256,128]{2,1,0:T(8,128)(2,1)S(1)}, bf16[9,256,128]{2,1,0:T(8,128)(2,1)S(1)}, u32[]{:S(2)}, u32[]{:S(2)}) collective-permute-start(bf16[9,256,128]{2,1,0:T(8,128)(2,1)S(1)} %get-tuple-element.30.own_ref.f_ref), channel_id=1, source_target_pairs={{0,1},{1,0},{2,3},{3,2},{4,5},{5,4},{6,7},{7,6},{8,9},{9,8},{10,11... | collective-permute-start | bytes 1769480 | tf_op jit(solution)/shard_map/ppermute | solution.py:618

commit v5 on v4

--- a/solution.py
+++ b/solution.py
@@ -175,7 +175,8 @@
 
 
 def prep_kernel(
-    num_ref, own_ref, other_ref, ds_ref, b0_ref, b1_ref, b2_ref, b3_ref, inner_ref, rows_ref, par_ref, bc_ref, sems
+    num_ref, own_ref, other_ref, ds_ref, b0_ref, b1_ref, b2_ref, b3_ref, inner_out, rows_out, par_ref, bc_out,
+    inner_ref, rows_ref, bc_ref, sems,
 ):
     core = num_ref[CORE]
     copies = [
@@ -217,10 +218,13 @@
         at = 16 * b
         rows_ref[b, 0:4, :] = tail[at : at + 4, :]
         rows_ref[b, 4:8, :] = enter[at : at + 4, :]
+    writes = [pltpu.make_async_copy(rows_ref, rows_out, sems.at[4])]
+    writes[0].start()
     running_t, dt_t = jnp.transpose(running), jnp.transpose(dt)
     s_at, t_at = iota((ROWS, ROWS), 0), iota((ROWS, ROWS), 1)
-    for copy in copies:
-        copy.wait()
+    wait_all(copies)
+    writes.append(pltpu.make_async_copy(bc_ref, bc_out, sems.at[5]))
+    writes[1].start()
     for b in range(CHUNKS):
         at = 16 * b
         state_in = jnp.transpose(bc_ref[b, 0:64, :].astype(f32)).astype(bf16)
@@ -231,6 +235,9 @@
             gap = running[at + n : at + n + 1, :] - running_t[:, at + n : at + n + 1]
             value = jnp.exp(jnp.where(allowed, gap, 0.0)) * mix * dt_t[:, at + n : at + n + 1]
             inner_ref[b, n, :, :] = jnp.where(allowed, value, 0.0).astype(bf16)
+        writes.append(pltpu.make_async_copy(inner_ref.at[b], inner_out.at[b], sems.at[6 + b]))
+        writes[-1].start()
+    wait_all(writes)
 
 
 def spread_ids(ds_ref, which):
@@ -248,13 +255,18 @@
         grid=(1,),
         in_specs=[SMEM, STEPS, STEPS, VMEM] + [ANYWHERE] * 4,
         out_shape=(
-            jax.ShapeDtypeStruct((CHUNKS, SSM, ROWS, ROWS), bf16),
-            jax.ShapeDtypeStruct((CHUNKS, 8, ROWS), f32),
+            pltpu.HBM((CHUNKS, SSM, ROWS, ROWS), bf16),
+            pltpu.HBM((CHUNKS, 8, ROWS), f32),
             jax.ShapeDtypeStruct((16, ROWS), f32),
-            jax.ShapeDtypeStruct((CHUNKS, 128, ROWS), bf16),
+            pltpu.HBM((CHUNKS, 128, ROWS), bf16),
         ),
-        out_specs=(VMEM,) * 4,
-        scratch_shapes=[pltpu.SemaphoreType.DMA((4,))],
+        out_specs=(HBM, HBM, VMEM, HBM),
+        scratch_shapes=[
+            pltpu.VMEM((CHUNKS, SSM, ROWS, ROWS), bf16),
+            pltpu.VMEM((CHUNKS, 8, ROWS), f32),
+            pltpu.VMEM((CHUNKS, 128, ROWS), bf16),
+            pltpu.SemaphoreType.DMA((6 + CHUNKS,)),
+        ],
         compiler_params=pltpu.CompilerParams(vmem_limit_bytes=VMEM_LIMIT),
         cost_estimate=pl.CostEstimate(flops=200_000_000, bytes_accessed=8_000_000, transcendentals=2_000_000),
         name="scan_weights",

time: 122 us -> 121 us (level)
  the two profiles are of different devices: /device:TPU:256 before, /device:TPU:224 now
where the time goes in v5:
time: 121 us; the launch traced here: 119 us
  starting transfers between devices  39.5 us (33%)
  Pallas kernels  26.2 us (22%)
  waiting for transfers between devices  23.6 us (20%)
  blocking collectives  22.7 us (19%)
  local copies, waits for them, and re-layouts  5.32 us (4%)
  other arithmetic  1.63 us (1%)
    all_to_all x1, blocking collectives, exchange(): lax.all_to_all(x, ('y', 'x'), split_axis=0, concat_axis=0, tiled=True)  22.7 us
    ppermute x3, waiting for transfers between devices, on_device(): lax.ppermute(both, 'y', [(i, (i + d) % 4) for i in range(4)])  16 us
    all_to_all x2, starting transfers between devices, exchange(): lax.all_to_all(x, ('y', 'x'), split_axis=0, concat_axis=0, tiled=True)  12.2 us
    ppermute x3, starting transfers between devices, on_device(): lax.ppermute(both, 'y', [(i, (i + d) % 4) for i in range(4)])  10.6 us
    pallas_call x1, Pallas kernels, attend_near(): pl.pallas_call(near_kernel, in_specs=[HBM] + [VMEM] * 4 + [HBM] * 3, out_...  9.63 us
    pallas_call x1, Pallas kernels, prep(): pl.pallas_call(prep_kernel, grid=(1,), in_specs=[SMEM, STEPS, STEPS, VMEM...  5.89 us
    ppermute x3, starting transfers between devices, other_core(): return lax.ppermute(x, 'core', [(0, 1), (1, 0)])  5.84 us
    ppermute x1, starting transfers between devices, on_device(): came = lax.ppermute(left, 'z', following)  5.71 us
  transfers between devices with their start and end apart: 10, of which 6 were waited for; matrix products, arithmetic and copies ran while one was open for 4% of the time, Pallas kernels for 14%

profile of v5, /device:TPU:224, one launch (start us, length us, event | category | flops | bytes accessed | tf_op | source)
XLA Modules:
  0.0 119.4 jit_solution(6792323672960674582)
XLA Ops:
  0.0 2.9 %pack_keys_values.1 = bf16[16,496,128]{2,1,0:T(8,128)(2,1)} custom-call(f32[7]{0:T(128)} %bias_any.1, f32[7]{0:T(128)} %decay_any.1, f32[7]{0:T(128)} %skip_any.1, bf16[128,3584]{1,0:T(8,128)(2,1)} %k_any.1, bf16[128,3584]{1,0:T(8,128)(2,1)} %v_any.1, bf16[56,128]{1,0:T(8,128)(2,1)} %bitcast.41), custom_call_target="tpu_custom_call" | custom-call | tf_op jit(solution)/shard_map/pack_keys_values/pallas_call | solution.py:110
  2.9 0.0 copy-start.19
  2.9 0.0 copy-start.20
  2.9 7.2 %all-to-all-start = ((bf16[16,496,128]{2,1,0:T(8,128)(2,1)}), bf16[16,496,128]{2,1,0:T(8,128)(2,1)S(1)}, u32[]{:S(2)}, u32[]{:S(2)}) async-start(bf16[16,496,128]{2,1,0:T(8,128)(2,1)} %pack_keys_values.1), calls=%async_computation | async-start | bytes 4063232 | tf_op jit(solution)/shard_map/all_to_all | solution.py:634
  10.1 0.0 copy-start.18
  10.2 0.0 copy-done.19
  10.2 0.0 copy-done.20
  10.2 0.2 reshape.26
  10.4 0.3 constant_dynamic-slice_fusion
  10.7 0.0 copy-start.1
  10.7 5.0 %collective-permute-start.2 = (bf16[4,128,128]{2,1,0:T(8,128)(2,1)S(1)}, bf16[4,128,128]{2,1,0:T(8,128)(2,1)S(1)}, u32[]{:S(2)}, u32[]{:S(2)}) collective-permute-start(bf16[4,128,128]{2,1,0:T(8,128)(2,1)S(1)} %bitcast.22), channel_id=1, source_target_pairs={{0,24},{8,0},{16,8},{24,16},{1,25},{9,1},{17,9},{25,17},{2,26},{10... | collective-permute-start | bytes 393224 | tf_op jit(solution)/shard_map/ppermute | solution.py:658
  15.8 2.8 %collective-permute-start.1 = (bf16[4,128,128]{2,1,0:T(8,128)(2,1)S(1)}, bf16[4,128,128]{2,1,0:T(8,128)(2,1)S(1)}, u32[]{:S(2)}, u32[]{:S(2)}) collective-permute-start(bf16[4,128,128]{2,1,0:T(8,128)(2,1)S(1)} %bitcast.23), channel_id=1, source_target_pairs={{0,16},{8,24},{16,0},{24,8},{1,17},{9,25},{17,1},{25,9},{2,18},{10... | collective-permute-start | bytes 393224 | tf_op jit(solution)/shard_map/ppermute | solution.py:658
  18.5 2.8 %collective-permute-start = (bf16[4,128,128]{2,1,0:T(8,128)(2,1)S(1)}, bf16[4,128,128]{2,1,0:T(8,128)(2,1)S(1)}, u32[]{:S(2)}, u32[]{:S(2)}) collective-permute-start(bf16[4,128,128]{2,1,0:T(8,128)(2,1)S(1)} %bitcast.24), channel_id=1, source_target_pairs={{0,8},{8,16},{16,24},{24,0},{1,9},{9,17},{17,25},{25,1},{2,10},{10... | collective-permute-start | bytes 393224 | tf_op jit(solution)/shard_map/ppermute | solution.py:658
  21.3 0.9 add_select_fusion
  22.2 0.3 reduce_window_max.16
  22.5 0.1 slice.28
  22.6 0.1 reduce-window.4
  22.7 0.1 slice_reduce_fusion
  22.8 0.1 pad_add_fusion
  22.9 0.1 slice.31
  23.0 0.1 slice_maximum_fusion
  23.0 0.1 rev.3
  23.1 0.0 copy-start.11
  23.1 0.0 copy-done.18
  23.1 1.3 %copy.17 = bf16[3584,128]{1,0:T(8,128)(2,1)} copy(bf16[3584,128]{0,1:T(8,128)(2,1)S(1)} %bitcast.35) | data formatting | bytes 1835008 | tf_op jit(solution)/shard_map/transpose | solution.py:665
  24.4 0.2 shift-right-arithmetic_reduce_fusion
  24.6 0.7 concatenate.14.refs_3_.num_ref.num_any
  25.3 13.2 %collective-permute-done.2.refs_7_.b3_ref = bf16[4,128,128]{2,1,0:T(8,128)(2,1)S(1)} collective-permute-done((bf16[4,128,128]{2,1,0:T(8,128)(2,1)S(1)}, bf16[4,128,128]{2,1,0:T(8,128)(2,1)S(1)}, u32[]{:S(2)}, u32[]{:S(2)}) %collective-permute-start.2) | collective-permute-done | bytes 131104 | tf_op jit(solution)/shard_map/ppermute | solution.py:658
  38.4 0.0 collective-permute-done.1.refs_6_.b2_ref
  38.4 2.8 %collective-permute-done.refs_5_.b1_ref = bf16[4,128,128]{2,1,0:T(8,128)(2,1)S(1)} collective-permute-done((bf16[4,128,128]{2,1,0:T(8,128)(2,1)S(1)}, bf16[4,128,128]{2,1,0:T(8,128)(2,1)S(1)}, u32[]{:S(2)}, u32[]{:S(2)}) %collective-permute-start) | collective-permute-done | bytes 131104 | tf_op jit(solution)/shard_map/ppermute | solution.py:658
  41.3 0.0 all-to-all-done.refs_0_
  41.3 0.0 copy-done.1
  41.3 0.0 copy-done.11
  41.3 0.0 copy-done.5
  41.3 0.0 copy-done.7
  41.3 0.6 copy-done.9
  41.9 2.0 %collective-permute-start.3 = (bf16[16,496,128]{2,1,0:T(8,128)(2,1)S(1)}, bf16[16,496,128]{2,1,0:T(8,128)(2,1)}, u32[]{:S(2)}, u32[]{:S(2)}) collective-permute-start(bf16[16,496,128]{2,1,0:T(8,128)(2,1)S(1)} %get-tuple-element.18.own_ref.first_ref), channel_id=1, source_target_pairs={{0,1},{1,0},{2,3},{3,2},{4,5},{5,4},{6,7},{7,6},{8,9},{9,8},{10,11... | collective-permute-start | bytes 6094856 | tf_op jit(solution)/shard_map/ppermute | solution.py:630
  43.9 5.0 %all-to-all-start.1 = ((bf16[16,224,128]{2,1,0:T(8,128)(2,1)}), bf16[16,224,128]{2,1,0:T(8,128)(2,1)}, u32[]{:S(2)}, u32[]{:S(2)}) async-start(bf16[16,224,128]{2,1,0:T(8,128)(2,1)} %get-tuple-element.20), calls=%async_computation.1 | async-start | bytes 1835008 | tf_op jit(solution)/shard_map/all_to_all | solution.py:634
  49.0 0.0 copy-start.2
  49.0 0.0 copy-start.6
  49.0 0.0 copy-start.8
  49.0 0.0 copy-start.10
  49.0 0.0 copy-start.12
  49.0 0.0 copy-start.16
  49.0 0.0 collective-permute-done.3.other_ref.before_ref
  49.1 0.1 cut_halo.1
  49.1 5.2 %collective-permute-start.4 = (bf16[8,480,128]{2,1,0:T(8,128)(2,1)S(1)}, bf16[8,480,128]{2,1,0:T(8,128)(2,1)}, u32[]{:S(2)}, u32[]{:S(2)}) collective-permute-start(bf16[8,480,128]{2,1,0:T(8,128)(2,1)S(1)} %cut_halo.1), channel_id=1, source_target_pairs={{0,32},{32,64},{64,96},{96,128},{128,160},{160,192},{192,224},{224... | collective-permute-start | bytes 2949128 | tf_op jit(solution)/shard_map/ppermute | solution.py:670
  54.4 5.9 %scan_weights.1 = (bf16[16,4,128,128]{3,2,1,0:T(8,128)(2,1)}, f32[16,8,128]{2,1,0:T(8,128)}, f32[16,128]{1,0:T(8,128)S(1)}, bf16[16,128,128]{2,1,0:T(8,128)(2,1)}) custom-call(s32[8]{0:T(128)S(1)} %copy-done.16, bf16[16,496,128]{2,1,0:T(8,128)(2,1)S(1)} %get-tuple-element.18.own_ref.first_ref, ...), custom_call_target="tpu_custom_call" | custom-call | flops 200000000 | bytes 8000000 | tf_op jit(solution)/shard_map/scan_weights/pallas_call | solution.py:253
  60.3 1.1 scan_keeps.1.keep_any.keep_ref
  61.4 0.6 copy-done.13
  62.0 3.7 %all-to-all-done.1.q_ref = bf16[16,224,128]{2,1,0:T(8,128)(2,1)} async-done(((bf16[16,224,128]{2,1,0:T(8,128)(2,1)}), bf16[16,224,128]{2,1,0:T(8,128)(2,1)}, u32[]{:S(2)}, u32[]{:S(2)}) %all-to-all-start.1) | async-done | bytes 917536 | tf_op jit(solution)/shard_map/all_to_all | solution.py:634
  65.7 9.6 %attend_near.1 = (bf16[8,256,128]{2,1,0:T(8,128)(2,1)}, bf16[4,256,128]{2,1,0:T(8,128)(2,1)}, bf16[128,128]{1,0:T(8,128)(2,1)S(1)}, f32[2,224,512]{2,1,0:T(8,128)}, f32[2,8,512]{2,1,0:T(8,128)}) custom-call(s32[8]{0:T(128)} %concatenate.14.refs_3_.num_ref.num_any, bf16[16,224,128]{2,1,0:T(8,128)(2,1)} %all-to-all-done.1.q_ref, ...), custom_call_target="tpu_custom_call" | custom-call | flops 5000000000 | bytes 9000000 | tf_op jit(solution)/shard_map/attend_near/pallas_call | solution.py:473
  75.4 0.3 collective-permute-done.4.refs_0_
  75.7 1.9 %collective-permute-start.5 = (bf16[8,480,128]{2,1,0:T(8,128)(2,1)}, bf16[8,480,128]{2,1,0:T(8,128)(2,1)S(1)}, u32[]{:S(2)}, u32[]{:S(2)}) collective-permute-start(bf16[8,480,128]{2,1,0:T(8,128)(2,1)} %gate.1.own_ref), channel_id=1, source_target_pairs={{0,1},{1,0},{2,3},{3,2},{4,5},{5,4},{6,7},{7,6},{8,9},{9,8},{10,11... | collective-permute-start | bytes 2949128 | tf_op jit(solution)/shard_map/ppermute | solution.py:630
  77.6 5.7 %collective-permute-start.6 = (bf16[128,128]{1,0:T(8,128)(2,1)S(1)}, bf16[128,128]{1,0:T(8,128)(2,1)S(1)}, u32[]{:S(2)}, u32[]{:S(2)}) collective-permute-start(bf16[128,128]{1,0:T(8,128)(2,1)S(1)} %get-tuple-element.24), channel_id=1, source_target_pairs={{0,32},{32,64},{64,96},{96,128},{128,160},{160,192},{192,224},{224... | collective-permute-start | bytes 98312 | tf_op jit(solution)/shard_map/ppermute | solution.py:675
  83.3 1.6 %collective-permute-done.6.came_ref = bf16[128,128]{1,0:T(8,128)(2,1)S(1)} collective-permute-done((bf16[128,128]{1,0:T(8,128)(2,1)S(1)}, bf16[128,128]{1,0:T(8,128)(2,1)S(1)}, u32[]{:S(2)}, u32[]{:S(2)}) %collective-permute-start.6) | collective-permute-done | bytes 32800 | tf_op jit(solution)/shard_map/ppermute | solution.py:675
  84.9 0.0 collective-permute-done.5.other_ref
  84.9 4.0 %attend_far.1 = (bf16[8,256,128]{2,1,0:T(8,128)(2,1)S(1)}, bf16[9,256,128]{2,1,0:T(8,128)(2,1)S(1)}) custom-call(s32[8]{0:T(128)} %concatenate.14.refs_3_.num_ref.num_any, bf16[16,224,128]{2,1,0:T(8,128)(2,1)} %all-to-all-done.1.q_ref, bf16[8,480,128]{2,1,0:T(8,128)(2,1)} %gate.1.own_ref, bf16[8,480,128]{2,1,0:T(8,128)(2,1)S(1)} %collective-permute-done.5.other_ref, ...), custom_call_target="tpu_custom_call" | custom-call | flops 2000000000 | bytes 5000000 | tf_op jit(solution)/shard_map/attend_far/pallas_call | solution.py:546
  88.9 1.9 %collective-permute-start.7 = (bf16[9,256,128]{2,1,0:T(8,128)(2,1)S(1)}, bf16[9,256,128]{2,1,0:T(8,128)(2,1)S(1)}, u32[]{:S(2)}, u32[]{:S(2)}) collective-permute-start(bf16[9,256,128]{2,1,0:T(8,128)(2,1)S(1)} %get-tuple-element.30.own_ref.f_ref), channel_id=1, source_target_pairs={{0,1},{1,0},{2,3},{3,2},{4,5},{5,4},{6,7},{7,6},{8,9},{9,8},{10,11... | collective-permute-start | bytes 1769480 | tf_op jit(solution)/shard_map/ppermute | solution.py:630
  90.8 2.0 %collective-permute-done.7.other_ref.g_ref = bf16[9,256,128]{2,1,0:T(8,128)(2,1)S(1)} collective-permute-done((bf16[9,256,128]{2,1,0:T(8,128)(2,1)S(1)}, bf16[9,256,128]{2,1,0:T(8,128)(2,1)S(1)}, u32[]{:S(2)}, u32[]{:S(2)}) %collective-permute-start.7) | collective-permute-done | bytes 589856 | tf_op jit(solution)/shard_map/ppermute | solution.py:630
  92.8 0.0 copy-done.3
  92.8 2.6 %scan.1 = bf16[16,224,128]{2,1,0:T(8,128)(2,1)S(1)} custom-call(s32[8]{0:T(128)S(1)} %copy-done.17, f32[16,128]{1,0:T(8,128)S(1)} %get-tuple-element.19.par_ref, bf16[8,256,128]{2,1,0:T(8,128)(2,1)S(1)} %get-tuple-element.27.xe_ref, bf16[8,256,128]{2,1,0:T(8,128)(2,1)S(1)} %copy-done.4, bf16[16,4,128,128]{3,2,1,0:T(8,128)(2,1)S(1)} %copy-done, ...), custom_call_target="tpu_custom_call" | custom-call | tf_op jit(solution)/shard_map/scan/pallas_call | solution.py:612
  95.4 22.7 %all_to_all.15 = bf16[16,224,128]{2,1,0:T(8,128)(2,1)S(1)} all-to-all(bf16[16,224,128]{2,1,0:T(8,128)(2,1)S(1)} %scan.1), channel_id=1, replica_groups=mesh['z'=16,'y'=4,'x'=4,'core'=2] {'y','x'}, dimensions={0} | all-to-all | bytes 1835008 | tf_op jit(solution)/shard_map/all_to_all | solution.py:634
  118.1 1.3 %copy.19 = bf16[3584,128]{0,1:T(8,128)(2,1)} copy(bf16[3584,128]{1,0:T(8,128)(2,1)S(1)} %bitcast.34) | data formatting | bytes 1835008 | tf_op jit(solution)/shard_map/reshape | solution.py:681
  (26 shorter events, 0.1 us)
Async XLA Ops:
  2.9 7.2 %copy-start.19 = (bf16[1024,64]{0,1:T(8,128)(2,1)S(1)}, bf16[1024,64]{0,1:T(8,128)(2,1)}, u32[]{:S(2)}) copy-start(bf16[1024,64]{0,1:T(8,128)(2,1)} %param.18) | copy-start | bytes 393220
  2.9 7.2 %copy-start.20 = (bf16[1024,64]{0,1:T(8,128)(2,1)S(1)}, bf16[1024,64]{0,1:T(8,128)(2,1)}, u32[]{:S(2)}) copy-start(bf16[1024,64]{0,1:T(8,128)(2,1)} %param.17) | copy-start | bytes 393220
  2.9 38.3 %all-to-all-start = ((bf16[16,496,128]{2,1,0:T(8,128)(2,1)}), bf16[16,496,128]{2,1,0:T(8,128)(2,1)S(1)}, u32[]{:S(2)}, u32[]{:S(2)}) async-start(bf16[16,496,128]{2,1,0:T(8,128)(2,1)} %pack_keys_values.1), calls=%async_computation | async-start | bytes 4063232 | tf_op jit(solution)/shard_map/all_to_all | solution.py:634
  10.1 13.0 %copy-start.18 = (bf16[128,3584]{1,0:T(8,128)(2,1)S(1)}, bf16[128,3584]{1,0:T(8,128)(2,1)}, u32[]{:S(2)}) copy-start(bf16[128,3584]{1,0:T(8,128)(2,1)} %param.10) | copy-start | bytes 2752516
  10.7 30.6 %copy-start.1 = (bf16[128,4,1,128]{3,0,1,2:T(8,128)(2,1)}, bf16[128,4,1,128]{3,0,1,2:T(8,128)(2,1)S(1)}, u32[]{:S(2)}) copy-start(bf16[128,4,1,128]{3,0,1,2:T(8,128)(2,1)S(1)} %copy.22) | copy-start | bytes 393220
  10.7 27.7 %collective-permute-start.2 = (bf16[4,128,128]{2,1,0:T(8,128)(2,1)S(1)}, bf16[4,128,128]{2,1,0:T(8,128)(2,1)S(1)}, u32[]{:S(2)}, u32[]{:S(2)}) collective-permute-start(bf16[4,128,128]{2,1,0:T(8,128)(2,1)S(1)} %bitcast.22), channel_id=1, source_target_pairs={{0,24},{8,0},{16,8},{24,16},{1,25},{9,1},{17,9},{25,17},{2,26},{10... | collective-permute-start | bytes 393224 | tf_op jit(solution)/shard_map/ppermute | solution.py:658
  15.8 22.7 %collective-permute-start.1 = (bf16[4,128,128]{2,1,0:T(8,128)(2,1)S(1)}, bf16[4,128,128]{2,1,0:T(8,128)(2,1)S(1)}, u32[]{:S(2)}, u32[]{:S(2)}) collective-permute-start(bf16[4,128,128]{2,1,0:T(8,128)(2,1)S(1)} %bitcast.23), channel_id=1, source_target_pairs={{0,16},{8,24},{16,0},{24,8},{1,17},{9,25},{17,1},{25,9},{2,18},{10... | collective-permute-start | bytes 393224 | tf_op jit(solution)/shard_map/ppermute | solution.py:658
  18.5 22.7 %collective-permute-start = (bf16[4,128,128]{2,1,0:T(8,128)(2,1)S(1)}, bf16[4,128,128]{2,1,0:T(8,128)(2,1)S(1)}, u32[]{:S(2)}, u32[]{:S(2)}) collective-permute-start(bf16[4,128,128]{2,1,0:T(8,128)(2,1)S(1)} %bitcast.24), channel_id=1, source_target_pairs={{0,8},{8,16},{16,24},{24,0},{1,9},{9,17},{17,25},{25,1},{2,10},{10... | collective-permute-start | bytes 393224 | tf_op jit(solution)/shard_map/ppermute | solution.py:658
  23.1 18.2 %copy-start.11 = (s32[4,8,128]{2,1,0:T(8,128)}, s32[4,8,128]{2,1,0:T(8,128)S(1)}, u32[]{:S(2)}) copy-start(s32[4,8,128]{2,1,0:T(8,128)S(1)} %broadcast_select_fusion) | copy-start | bytes 49156
  38.4 2.9 %copy-start.5 = (bf16[4,128,128]{2,1,0:T(8,128)(2,1)}, bf16[4,128,128]{2,1,0:T(8,128)(2,1)S(1)}, u32[]{:S(2)}) copy-start(bf16[4,128,128]{2,1,0:T(8,128)(2,1)S(1)} %collective-permute-done.2.refs_7_.b3_ref) | copy-start | bytes 393220
  38.4 2.9 %copy-start.7 = (bf16[4,128,128]{2,1,0:T(8,128)(2,1)}, bf16[4,128,128]{2,1,0:T(8,128)(2,1)S(1)}, u32[]{:S(2)}) copy-start(bf16[4,128,128]{2,1,0:T(8,128)(2,1)S(1)} %collective-permute-done.1.refs_6_.b2_ref) | copy-start | bytes 393220
  41.3 0.6 copy-start.9
  41.9 7.1 %collective-permute-start.3 = (bf16[16,496,128]{2,1,0:T(8,128)(2,1)S(1)}, bf16[16,496,128]{2,1,0:T(8,128)(2,1)}, u32[]{:S(2)}, u32[]{:S(2)}) collective-permute-start(bf16[16,496,128]{2,1,0:T(8,128)(2,1)S(1)} %get-tuple-element.18.own_ref.first_ref), channel_id=1, source_target_pairs={{0,1},{1,0},{2,3},{3,2},{4,5},{5,4},{6,7},{7,6},{8,9},{9,8},{10,11... | collective-permute-start | bytes 6094856 | tf_op jit(solution)/shard_map/ppermute | solution.py:630
  43.9 21.8 %all-to-all-start.1 = ((bf16[16,224,128]{2,1,0:T(8,128)(2,1)}), bf16[16,224,128]{2,1,0:T(8,128)(2,1)}, u32[]{:S(2)}, u32[]{:S(2)}) async-start(bf16[16,224,128]{2,1,0:T(8,128)(2,1)} %get-tuple-element.20), calls=%async_computation.1 | async-start | bytes 1835008 | tf_op jit(solution)/shard_map/all_to_all | solution.py:634
  49.0 5.3 %copy-start.2 = (bf16[128,4,1,128]{3,0,1,2:T(8,128)(2,1)S(1)}, bf16[128,4,1,128]{3,0,1,2:T(8,128)(2,1)}, u32[]{:S(2)}) copy-start(bf16[128,4,1,128]{3,0,1,2:T(8,128)(2,1)} %copy-done.1) | copy-start | bytes 393220
  49.0 5.3 %copy-start.6 = (bf16[4,128,128]{2,1,0:T(8,128)(2,1)S(1)}, bf16[4,128,128]{2,1,0:T(8,128)(2,1)}, u32[]{:S(2)}) copy-start(bf16[4,128,128]{2,1,0:T(8,128)(2,1)} %copy-done.5) | copy-start | bytes 393220
  49.0 5.3 %copy-start.8 = (bf16[4,128,128]{2,1,0:T(8,128)(2,1)S(1)}, bf16[4,128,128]{2,1,0:T(8,128)(2,1)}, u32[]{:S(2)}) copy-start(bf16[4,128,128]{2,1,0:T(8,128)(2,1)} %copy-done.7) | copy-start | bytes 393220
  49.0 5.3 %copy-start.10 = (bf16[4,128,128]{2,1,0:T(8,128)(2,1)S(1)}, bf16[4,128,128]{2,1,0:T(8,128)(2,1)}, u32[]{:S(2)}) copy-start(bf16[4,128,128]{2,1,0:T(8,128)(2,1)} %copy-done.9) | copy-start | bytes 393220
  49.0 5.3 %copy-start.12 = (s32[4,8,128]{2,1,0:T(8,128)S(1)}, s32[4,8,128]{2,1,0:T(8,128)}, u32[]{:S(2)}) copy-start(s32[4,8,128]{2,1,0:T(8,128)} %copy-done.11) | copy-start | bytes 49156
  49.0 5.3 %copy-start.16 = (s32[8]{0:T(128)S(1)}, s32[8]{0:T(128)}, u32[]{:S(2)}) copy-start(s32[8]{0:T(128)} %concatenate.14.refs_3_.num_ref.num_any) | copy-start | bytes 100
  49.1 26.6 %collective-permute-start.4 = (bf16[8,480,128]{2,1,0:T(8,128)(2,1)S(1)}, bf16[8,480,128]{2,1,0:T(8,128)(2,1)}, u32[]{:S(2)}, u32[]{:S(2)}) collective-permute-start(bf16[8,480,128]{2,1,0:T(8,128)(2,1)S(1)} %cut_halo.1), channel_id=1, source_target_pairs={{0,32},{32,64},{64,96},{96,128},{128,160},{160,192},{192,224},{224... | collective-permute-start | bytes 2949128 | tf_op jit(solution)/shard_map/ppermute | solution.py:670
  61.4 0.6 copy-start.13
  75.7 9.2 %collective-permute-start.5 = (bf16[8,480,128]{2,1,0:T(8,128)(2,1)}, bf16[8,480,128]{2,1,0:T(8,128)(2,1)S(1)}, u32[]{:S(2)}, u32[]{:S(2)}) collective-permute-start(bf16[8,480,128]{2,1,0:T(8,128)(2,1)} %gate.1.own_ref), channel_id=1, source_target_pairs={{0,1},{1,0},{2,3},{3,2},{4,5},{5,4},{6,7},{7,6},{8,9},{9,8},{10,11... | collective-permute-start | bytes 2949128 | tf_op jit(solution)/shard_map/ppermute | solution.py:630
  77.6 7.3 %collective-permute-start.6 = (bf16[128,128]{1,0:T(8,128)(2,1)S(1)}, bf16[128,128]{1,0:T(8,128)(2,1)S(1)}, u32[]{:S(2)}, u32[]{:S(2)}) collective-permute-start(bf16[128,128]{1,0:T(8,128)(2,1)S(1)} %get-tuple-element.24), channel_id=1, source_target_pairs={{0,32},{32,64},{64,96},{96,128},{128,160},{160,192},{192,224},{224... | collective-permute-start | bytes 98312 | tf_op jit(solution)/shard_map/ppermute | solution.py:675
  84.9 7.9 %copy-start = (bf16[16,4,128,128]{3,2,1,0:T(8,128)(2,1)S(1)}, bf16[16,4,128,128]{3,2,1,0:T(8,128)(2,1)}, u32[]{:S(2)}) copy-start(bf16[16,4,128,128]{3,2,1,0:T(8,128)(2,1)} %get-tuple-element.29.inner_ref) | copy-start | bytes 6291460
  84.9 7.9 %copy-start.3 = (bf16[16,128,128]{2,1,0:T(8,128)(2,1)S(1)}, bf16[16,128,128]{2,1,0:T(8,128)(2,1)}, u32[]{:S(2)}) copy-start(bf16[16,128,128]{2,1,0:T(8,128)(2,1)} %get-tuple-element.22.maps_any.bc_ref) | copy-start | bytes 1572868
  84.9 7.9 %copy-start.4 = (bf16[8,256,128]{2,1,0:T(8,128)(2,1)S(1)}, bf16[8,256,128]{2,1,0:T(8,128)(2,1)}, u32[]{:S(2)}) copy-start(bf16[8,256,128]{2,1,0:T(8,128)(2,1)} %get-tuple-element.28.xl_ref) | copy-start | bytes 1572868
  84.9 7.9 %copy-start.14 = (f32[16,8,128]{2,1,0:T(8,128)S(1)}, f32[16,8,128]{2,1,0:T(8,128)}, u32[]{:S(2)}) copy-start(f32[16,8,128]{2,1,0:T(8,128)} %copy-done.13) | copy-start | bytes 196612
  84.9 7.9 %copy-start.15 = (f32[16,8,128]{2,1,0:T(8,128)S(1)}, f32[16,8,128]{2,1,0:T(8,128)}, u32[]{:S(2)}) copy-start(f32[16,8,128]{2,1,0:T(8,128)} %get-tuple-element.21.rows_any.rows_ref) | copy-start | bytes 196612
  84.9 7.9 %copy-start.17 = (s32[8]{0:T(128)S(1)}, s32[8]{0:T(128)}, u32[]{:S(2)}) copy-start(s32[8]{0:T(128)} %concatenate.14.refs_3_.num_ref.num_any) | copy-start | bytes 100
  88.9 3.9 %collective-permute-start.7 = (bf16[9,256,128]{2,1,0:T(8,128)(2,1)S(1)}, bf16[9,256,128]{2,1,0:T(8,128)(2,1)S(1)}, u32[]{:S(2)}, u32[]{:S(2)}) collective-permute-start(bf16[9,256,128]{2,1,0:T(8,128)(2,1)S(1)} %get-tuple-element.30.own_ref.f_ref), channel_id=1, source_target_pairs={{0,1},{1,0},{2,3},{3,2},{4,5},{5,4},{6,7},{7,6},{8,9},{9,8},{10,11... | collective-permute-start | bytes 1769480 | tf_op jit(solution)/shard_map/ppermute | solution.py:630
